TPU v7x, 128 devices: a whole 4x4x4 slice. The times are simulated.
128 devices in a mesh: lon: 16 (over y_hi, z, core), lat: 8 (over y_lo, x).
Axes of the slice: x: 4, y: 4 (y_hi: 2, y_lo: 2; y = y_hi * 2 + y_lo), z: 4, core: 2. Of those that a mesh axis runs over, the one named last changes fastest.
Arguments:
- tracers: float32 [32, 64, 32768], P(None, 'lat', 'lon'), may hold values from 0.1 to 10
- courant: float32 [2, 64, 512], P(None, 'lat', 'lon'), may hold values from -0.45 to 0.45
- switches: int32 [2, 64, 512], P(None, 'lat', 'lon'), may hold values 0 or 1
- day_flags: int32 [64, 512], P('lat', 'lon'), may hold values from 0 to 1, as said below
- diffusion_counts: int32 [64, 512], P('lat', 'lon'), may hold values from 1 to 8
- night_rates: float32 [32, 32], replicated, may hold values from -0.18 to 0.18
- photo_rates: float32 [32, 32], replicated, may hold values from -0.24 to 0.24
- level_light: float32 [64], replicated, may hold values from 0.1 to 1
- self_loss: float32 [32], replicated, may hold values from 0.001 to 0.05
- vertical_mixing: float32 [63], replicated, may hold values from 0.05 to 0.45
Outputs:
- tracers_out: float32 [32, 64, 32768], P(None, 'lat', 'lon')
Inputs may be any that keep to these rules, and one draw needn't show every extreme that they name: `day_flags`: in every latitude row exactly half of the 512 columns are day columns, forming one contiguous band around the longitude cycle.
All inputs are finite; a program needn't handle non-finite values. No bound on the sum of `switches` on one device may be relied on, other than what follows from the above.
Results may differ from a plain program's by a relative error of at most 0.0003.
Values sent between devices are 32-bit elements; how exact they have to be, the bound alone decides.
No kernel may reach another device: no remote copies, remote signals or barrier semaphores. Data moves between devices by JAX's collectives and lax.ppermute only.
A program may use at most 64 MiB of HBM per device.

v0:
```python
import jax
import jax.numpy as jnp
from jax import lax
from jax.experimental import pallas as pl
from jax.experimental.pallas import tpu as pltpu
from jax.sharding import PartitionSpec as P

CHEM = 6
KMAX = 8
PIECE = 128
HALF = 64
VMEM_LIMIT = 24 * 1024 * 1024
F32 = jnp.float32
BF16 = jnp.bfloat16
LON_C, LON_G, LAT_C, LAT_G, DAY, COUNT = range(6)


def ring(value, axis, steps):
    count = lax.axis_size(axis)
    return lax.ppermute(value, axis, [(i, (i + steps) % count) for i in range(count)])


def half_roll(value):
    return pltpu.roll(value, HALF, 1)


def minmod(x, y):
    return jnp.minimum(jnp.maximum(x, jnp.minimum(y, 0.0)), jnp.maximum(y, 0.0))


def gain(cour, switch):
    return 0.5 * cour * switch * jnp.where(cour >= 0.0, 1.0 - cour, -1.0 - cour)


def lon_sweep(cells, cours, gains):
    n = len(cells)
    low = lax.broadcasted_iota(jnp.int32, cells[0].shape, 1) < HALF
    turned = [half_roll(q) for q in cells]
    west = [turned[0]] + [jnp.where(low, turned[i - 1], turned[i]) for i in range(1, n)]
    step = [q - w for q, w in zip(cells, west)]
    turned = [half_roll(d) for d in step]
    ahead = [jnp.where(low, turned[i], turned[i + 1]) for i in range(n - 1)] + [turned[n - 1]]
    slope = [minmod(d, a) for d, a in zip(step, ahead)]
    turned = [half_roll(s) for s in slope]
    flux = [None]
    for i in range(1, n):
        forward = cours[i - 1] >= 0.0
        behind = jnp.where(low, turned[i - 1], turned[i])
        flux.append(
            cours[i - 1] * jnp.where(forward, west[i], cells[i])
            + gains[i - 1] * jnp.where(forward, behind, slope[i])
        )
    turned = [None] + [half_roll(f) for f in flux[1:]]
    return [
        cells[i] - (jnp.where(low, turned[i], turned[i + 1]) - flux[i]) for i in range(1, n - 1)
    ]


def lat_sweep(rows, cours, gains):
    n = len(rows) - 4
    step = [rows[i + 1] - rows[i] for i in range(n + 3)]
    slope = [minmod(step[i], step[i + 1]) for i in range(n + 2)]
    flux = []
    for i in range(n + 1):
        forward = cours[i] >= 0.0
        flux.append(
            cours[i] * jnp.where(forward, rows[i + 1], rows[i + 2])
            + gains[i] * jnp.where(forward, slope[i], slope[i + 1])
        )
    return [rows[i + 2] - (flux[i + 1] - flux[i]) for i in range(n)]


def expand(compact, first):
    rows = compact.shape[0]
    low = lax.broadcasted_iota(jnp.int32, (rows, PIECE), 1) < HALF
    left = jnp.broadcast_to(compact[:, first : first + 1], (rows, PIECE))
    right = jnp.broadcast_to(compact[:, first + 1 : first + 2], (rows, PIECE))
    return jnp.where(low, left, right)


def rate_pieces(night_ref, photo_ref):
    rates = jnp.concatenate([night_ref[...], photo_ref[...]], 0)
    high = rates.astype(BF16)
    low = (rates - high.astype(F32)).astype(BF16)
    return jnp.concatenate([high, high, low], 1)


def react(rows, suns, rates, loss):
    species = rows[0].shape[0]
    for _ in range(CHEM):
        nexts = []
        for q, sun in zip(rows, suns):
            high = q.astype(BF16)
            low = (q - high.astype(F32)).astype(BF16)
            both = jnp.dot(
                rates, jnp.concatenate([high, low, high], 0), preferred_element_type=F32
            )
            top = q + both[:species] + sun * both[species:]
            bottom = 1.0 + loss * q * q
            inverse = pl.reciprocal(bottom, approx=True)
            inverse = inverse * (2.0 - bottom * inverse)
            nexts.append(top * inverse)
        rows = nexts
    return rows


def diffuse(q, count, mixing):
    for step in range(KMAX):
        number = jnp.where(count > step, mixing, 0.0)
        flux = number * (pltpu.roll(q, PIECE - 1, 1) - q)
        q = q + flux - pltpu.roll(flux, 1, 1)
    return q


def column_block(rows, days, counts, rates, loss, level, mixing):
    suns = [day * level for day in days]
    rows = react(rows, suns, rates, loss)
    done = []
    for q, count in zip(rows, counts):
        done.append(
            jnp.concatenate(
                [
                    diffuse(q[:, h : h + PIECE], count[:, h : h + PIECE], mixing)
                    for h in (0, PIECE)
                ],
                1,
            )
        )
    return done


def call(kernel, outs, ins, *args, scratch=(), cost=1e7):
    return pl.pallas_call(
        kernel,
        out_shape=[jax.ShapeDtypeStruct(s, F32) for s in outs],
        in_specs=ins,
        out_specs=[pl.BlockSpec(memory_space=pltpu.VMEM)] * len(outs),
        scratch_shapes=list(scratch),
        compiler_params=pltpu.CompilerParams(vmem_limit_bytes=VMEM_LIMIT),
        cost_estimate=pl.CostEstimate(flops=int(cost), bytes_accessed=4000000, transcendentals=0),
    )(*args)


WHOLE = pl.BlockSpec(memory_space=pltpu.VMEM)


def first_kernel(x_ref, cour_ref, sw_ref, day_ref, cnt_ref, south_ref, north_ref, west_ref, east_ref, coef_ref):
    species, rows, width = x_ref.shape
    pieces = width // PIECE
    cour = [cour_ref[0], cour_ref[1]]
    switch = [sw_ref[0].astype(F32), sw_ref[1].astype(F32)]
    fields = [
        cour[0],
        gain(cour[0], switch[0]),
        cour[1],
        gain(cour[1], switch[1]),
        day_ref[...].astype(F32),
        cnt_ref[...].astype(F32),
    ]
    for i, field in enumerate(fields):
        for j in range(pieces):
            coef_ref[i, :, j * PIECE : (j + 1) * PIECE] = expand(field, 2 * j)
    columns = 2 * pieces
    edge = 2 * PIECE
    for ref, first, at in ((west_ref, 0, 0), (east_ref, columns - 4, width - edge)):
        for s in range(species):
            ref[s] = x_ref[s, :, at : at + edge]
        for i, field in enumerate(fields):
            for half in (0, 1):
                ref[species + i, :, half * PIECE : (half + 1) * PIECE] = expand(field, first + 2 * half)

    def tile(s, carry):
        at = pl.multiple_of(s * 8, 8)
        for r in (0, 1, rows - 2, rows - 1):
            cells = [x_ref[pl.ds(at, 8), r, j * PIECE : (j + 1) * PIECE] for j in range(pieces)]
            cours = [coef_ref[LON_C, r : r + 1, j * PIECE : (j + 1) * PIECE] for j in range(1, pieces)]
            gains = [coef_ref[LON_G, r : r + 1, j * PIECE : (j + 1) * PIECE] for j in range(1, pieces)]
            out = lon_sweep(cells, cours, gains)
            ref, row = (south_ref, r) if r < 2 else (north_ref, r - rows + 2)
            for j, value in enumerate(out):
                ref[row, pl.ds(at, 8), j * PIECE : (j + 1) * PIECE] = value
        return carry

    lax.fori_loop(0, species // 8, tile, 0)


def inner_kernel(x_ref, coef_ref, par_ref, loss_ref, night_ref, photo_ref, mid_ref, done_ref):
    species, rows, width = x_ref.shape
    pieces = width // PIECE

    def tile(s, carry):
        at = pl.multiple_of(s * 8, 8)
        for r in range(rows):
            cells = [x_ref[pl.ds(at, 8), r, j * PIECE : (j + 1) * PIECE] for j in range(pieces)]
            cours = [coef_ref[LON_C, r : r + 1, j * PIECE : (j + 1) * PIECE] for j in range(1, pieces)]
            gains = [coef_ref[LON_G, r : r + 1, j * PIECE : (j + 1) * PIECE] for j in range(1, pieces)]
            for j, value in enumerate(lon_sweep(cells, cours, gains)):
                mid_ref[r, pl.ds(at, 8), j * PIECE : (j + 1) * PIECE] = value
        return carry

    lax.fori_loop(0, species // 8, tile, 0)
    rates = rate_pieces(night_ref, photo_ref)
    level = jnp.concatenate([par_ref[0:1]] * 2, 1)
    loss = jnp.concatenate([loss_ref[...]] * 2, 1)
    mixing = par_ref[1:2]
    wide = 2 * PIECE

    def block(b, carry):
        at = pl.multiple_of(b * wide, wide)
        here = pl.ds(at, wide)
        own = pl.ds(pl.multiple_of(at + PIECE, PIECE), wide)
        cells = [mid_ref[r, :, here] for r in range(rows)]
        faces = range(2, rows - 1)
        cells = lat_sweep(
            cells,
            [coef_ref[LAT_C, f : f + 1, own] for f in faces],
            [coef_ref[LAT_G, f : f + 1, own] for f in faces],
        )
        inner = range(2, rows - 2)
        cells = column_block(
            cells,
            [coef_ref[DAY, r : r + 1, own] for r in inner],
            [coef_ref[COUNT, r : r + 1, own] for r in inner],
            rates,
            loss,
            level,
            mixing,
        )
        for i, q in enumerate(cells):
            done_ref[i, :, here] = q
        return carry

    lax.fori_loop(0, (pieces - 2) // 2, block, 0)


def side_kernel(xw_ref, xe_ref, hw_ref, he_ref, coef_ref, mid_ref, south_ref, north_ref, side_ref):
    species, rows = xw_ref.shape[0] - 6, xw_ref.shape[1]
    width = coef_ref.shape[2]
    for i in range(6):
        side_ref[i, :, 0:PIECE] = hw_ref[species + i, :, PIECE : 2 * PIECE]
        side_ref[i, :, PIECE : 2 * PIECE] = coef_ref[i, :, 0:PIECE]
        side_ref[i, :, 2 * PIECE : 3 * PIECE] = coef_ref[i, :, width - PIECE : width]
        side_ref[i, :, 3 * PIECE : 4 * PIECE] = he_ref[species + i, :, 0:PIECE]

    def tile(s, carry):
        at = pl.multiple_of(s * 8, 8)
        block = pl.ds(at, 8)
        for r in range(rows):
            row = slice(r, r + 1)
            cells = [ref[block, r, h : h + PIECE] for ref in (hw_ref, xw_ref) for h in (0, PIECE)]
            faces = [
                [side_ref[i, row, 0:PIECE], side_ref[i, row, PIECE : 2 * PIECE], coef_ref[i, row, PIECE : 2 * PIECE]]
                for i in (LON_C, LON_G)
            ]
            out = lon_sweep(cells, *faces)
            cells = [ref[block, r, h : h + PIECE] for ref in (xe_ref, he_ref) for h in (0, PIECE)]
            faces = [
                [
                    side_ref[i, row, 2 * PIECE : 3 * PIECE],
                    side_ref[i, row, 3 * PIECE : 4 * PIECE],
                    he_ref[species + i, row, PIECE : 2 * PIECE],
                ]
                for i in (LON_C, LON_G)
            ]
            out = out + lon_sweep(cells, *faces)
            for j, value in enumerate(out):
                lanes = slice(j * PIECE, (j + 1) * PIECE)
                mid_ref[r, block, lanes] = value
                if r < 2:
                    south_ref[pl.ds(r * species + at, 8), lanes] = value
                if r >= rows - 2:
                    north_ref[pl.ds((r - rows + 2) * species + at, 8), lanes] = value
        return carry

    lax.fori_loop(0, species // 8, tile, 0)
    for j in range(4):
        lanes = slice(j * PIECE, (j + 1) * PIECE)
        two = [side_ref[i, 0:1, lanes] for i in (LAT_C, LAT_G)]
        south_ref[2 * species : 2 * species + 8, lanes] = jnp.concatenate([two[0]] * 4 + [two[1]] * 4, 0)


def edge_kernel(
    mid_ref, south_ref, north_ref, done_ref, midc_ref, southc_ref, northc_ref, coef_ref, side_ref, row_ref,
    par_ref, loss_ref, night_ref, photo_ref, sent_south_ref, sent_north_ref, swept_ref, field_ref,
):
    rows, species, inner_width = mid_ref.shape
    rates = rate_pieces(night_ref, photo_ref)
    level = jnp.concatenate([par_ref[0:1]] * 2, 1)
    loss = jnp.concatenate([loss_ref[...]] * 2, 1)
    mixing = par_ref[1:2]
    wide = 2 * PIECE
    valid_south = jnp.concatenate([par_ref[2:3]] * 2, 1)
    valid_north = jnp.concatenate([par_ref[3:4]] * 2, 1)

    def block(b, carry):
        at = pl.multiple_of(b * wide, wide)
        here = pl.ds(at, wide)
        own = pl.ds(pl.multiple_of(at + PIECE, PIECE), wide)
        lower = [south_ref[i, :, here] * valid_south for i in (0, 1)] + [mid_ref[r, :, here] for r in range(4)]
        upper = [mid_ref[r, :, here] for r in range(4, 8)] + [north_ref[i, :, here] * valid_north for i in (0, 1)]
        faces = [
            [
                [coef_ref[i, 0:1, own] * valid_south, coef_ref[i, 1:2, own], coef_ref[i, 2:3, own]],
                [coef_ref[i, 6:7, own], coef_ref[i, 7:8, own], row_ref[i - LAT_C, 0:1, own] * valid_north],
            ]
            for i in (LAT_C, LAT_G)
        ]
        cells = lat_sweep(lower, faces[0][0], faces[1][0]) + lat_sweep(upper, faces[0][1], faces[1][1])
        edge = (0, 1, 6, 7)
        cells = column_block(
            cells,
            [coef_ref[DAY, r : r + 1, own] for r in edge],
            [coef_ref[COUNT, r : r + 1, own] for r in edge],
            rates,
            loss,
            level,
            mixing,
        )
        out = pl.ds(pl.multiple_of(at + wide, PIECE), wide)
        for r, q in zip(edge, cells):
            field_ref[r, :, out] = q
        for i in range(4):
            field_ref[i + 2, :, out] = done_ref[i, :, here]
        return carry

    lax.fori_loop(0, inner_width // wide, block, 0)

    def side(b, carry):
        here = pl.ds(pl.multiple_of(b * wide, wide), wide)
        cells = (
            [southc_ref[i * species : (i + 1) * species, here] * valid_south for i in (0, 1)]
            + [midc_ref[r, :, here] for r in range(rows)]
            + [northc_ref[i * species : (i + 1) * species, here] * valid_north for i in (0, 1)]
        )
        faces = [
            [side_ref[i, 0:1, here] * valid_south]
            + [side_ref[i, r : r + 1, here] for r in range(1, rows)]
            + [northc_ref[2 * species + 4 * (i - LAT_C) : 2 * species + 4 * (i - LAT_C) + 1, here] * valid_north]
            for i in (LAT_C, LAT_G)
        ]
        cells = lat_sweep(cells, *faces)
        for part in (slice(0, 4), slice(4, 8)):
            done = column_block(
                cells[part],
                [side_ref[DAY, r : r + 1, here] for r in range(rows)[part]],
                [side_ref[COUNT, r : r + 1, here] for r in range(rows)[part]],
                rates,
                loss,
                level,
                mixing,
            )
            out = pl.ds(pl.multiple_of(b * (inner_width + wide), PIECE), wide)
            for r, q in zip(range(rows)[part], done):
                field_ref[r, :, out] = q
        return carry

    lax.fori_loop(0, 2, side, 0)
    pieces = (inner_width + 4 * PIECE) // PIECE

    def tile(s, carry):
        block = pl.ds(pl.multiple_of(s * 8, 8), 8)
        for r in range(rows):
            row = slice(r, r + 1)
            cells = [field_ref[r, block, j * PIECE : (j + 1) * PIECE] for j in range(pieces)]
            faces = [
                [coef_ref[i, row, j * PIECE : (j + 1) * PIECE] for j in range(pieces - 2)]
                + [side_ref[i, row, 3 * PIECE : 4 * PIECE]]
                for i in (LON_C, LON_G)
            ]
            for j, value in enumerate(lon_sweep(cells, *faces)):
                lanes = slice(j * PIECE, (j + 1) * PIECE)
                swept_ref[r, block, lanes] = value
                if r < 2:
                    sent_south_ref[r, block, lanes] = value
                if r >= rows - 2:
                    sent_north_ref[r - rows + 2, block, lanes] = value
        return carry

    lax.fori_loop(0, species // 8, tile, 0)


def last_kernel(swept_ref, south_ref, north_ref, coef_ref, row_ref, par_ref, out_ref):
    rows, species, width = swept_ref.shape
    valid_south, valid_north = par_ref[2:3], par_ref[3:4]

    def piece(j, carry):
        here = pl.ds(pl.multiple_of(j * PIECE, PIECE), PIECE)
        cells = (
            [south_ref[i, :, here] * valid_south for i in (0, 1)]
            + [swept_ref[r, :, here] for r in range(rows)]
            + [north_ref[i, :, here] * valid_north for i in (0, 1)]
        )
        faces = [
            [coef_ref[i, 0:1, here] * valid_south]
            + [coef_ref[i, r : r + 1, here] for r in range(1, rows)]
            + [row_ref[i - LAT_C, 0:1, here] * valid_north]
            for i in (LAT_C, LAT_G)
        ]
        for r, q in enumerate(lat_sweep(cells, *faces)):
            out_ref[:, r, here] = q
        return carry

    lax.fori_loop(0, width // PIECE, piece, 0)


def shards(
    tracers,
    courant,
    switches,
    day_flags,
    diffusion_counts,
    night_rates,
    photo_rates,
    level_light,
    self_loss,
    vertical_mixing,
):
    species, rows, width = tracers.shape
    inner = width - 2 * PIECE
    lat_count = lax.axis_size("lat")
    lat = lax.axis_index("lat")
    two = 2 * PIECE

    sent_south, sent_north, sent_west, sent_east, coef = call(
        first_kernel,
        [(2, species, inner), (2, species, inner), (species + 6, rows, two), (species + 6, rows, two), (6, rows, width)],
        [WHOLE] * 5,
        tracers,
        courant,
        switches,
        day_flags,
        diffusion_counts,
    )
    south = ring(sent_north, "lat", 1)
    north = ring(sent_south, "lat", -1)
    halo_west = ring(sent_east, "lon", 1)
    halo_east = ring(sent_west, "lon", -1)
    row = ring(coef[LAT_C : LAT_G + 1, 0:1], "lat", -1)

    edge = jnp.zeros((1,), F32)
    mixing = jnp.concatenate([vertical_mixing, edge])
    ones = jnp.ones((PIECE,), F32)
    par = jnp.stack(
        [
            jnp.tile(level_light, 2),
            jnp.tile(mixing, 2),
            ones * (lat > 0).astype(F32),
            ones * (lat < lat_count - 1).astype(F32),
        ]
    )
    loss = jnp.broadcast_to(self_loss[:, None], (species, PIECE))
    rates = (night_rates, photo_rates)

    mid, done = call(
        inner_kernel,
        [(rows, species, inner), (rows - 4, species, inner)],
        [WHOLE] * 6,
        tracers,
        coef,
        par,
        loss,
        *rates,
    )
    mid_side, side_south, side_north, side = call(
        side_kernel,
        [(rows, species, 2 * two), (2 * species + 8, 2 * two), (2 * species, 2 * two), (6, rows, 2 * two)],
        [WHOLE] * 5,
        sent_west,
        sent_east,
        halo_west,
        halo_east,
        coef,
    )
    side_from_south = ring(side_north, "lat", 1)
    side_from_north = ring(side_south, "lat", -1)
    sent_south, sent_north, swept = call(
        edge_kernel,
        [(2, species, width), (2, species, width), (rows, species, width)],
        [WHOLE] * 14,
        mid,
        south,
        north,
        done,
        mid_side,
        side_from_south,
        side_from_north,
        coef,
        side,
        row,
        par,
        loss,
        *rates,
        scratch=[pltpu.VMEM((rows, species, width + two), F32)],
    )
    south = ring(sent_north, "lat", 1)
    north = ring(sent_south, "lat", -1)
    (out,) = call(
        last_kernel, [(species, rows, width)], [WHOLE] * 6, swept, south, north, coef, row, par
    )
    return out


def solution(mesh):
    in_specs = (
        P(None, "lat", "lon"),
        P(None, "lat", "lon"),
        P(None, "lat", "lon"),
        P("lat", "lon"),
        P("lat", "lon"),
        P(),
        P(),
        P(),
        P(),
        P(),
    )
    out_specs = P(None, "lat", "lon")
    return jax.shard_map(shards, mesh=mesh, in_specs=in_specs, out_specs=out_specs, check_vma=False)
```

profile of v0, /device:TPU:6, one launch (start us, length us, event | category | flops | bytes accessed | tf_op | source)
XLA Modules:
  0.0 106.0 jit_solution(16472984203492364414)
XLA Ops:
  0.0 1.6 %copy-done = f32[32,8,2048]{2,1,0:T(8,128)S(1)} copy-done((f32[32,8,2048]{2,1,0:T(8,128)S(1)}, f32[32,8,2048]{2,1,0:T(8,128)}, u32[]{:S(2)}) %copy-start) | copy-done | bytes 2097176
  1.6 0.7 copy-done.4
  2.3 0.7 copy-done.5
  3.0 0.7 copy-done.6
  3.7 0.7 copy-done.7
  4.4 3.3 %shard_map.100 = (f32[2,32,1792]{2,1,0:T(8,128)}, f32[2,32,1792]{2,1,0:T(8,128)}, f32[38,8,256]{2,1,0:T(8,128)}, f32[38,8,256]{2,1,0:T(8,128)}, f32[6,8,2048]{2,1,0:T(8,128)S(1)}) custom-call(f32[32,8,2048]{2,1,0:T(8,128)S(1)} %copy-done, f32[2,8,32]{2,1,0:T(8,128)S(1)} %copy-done.4, s32[2,8,32]{2,1,0:T(8,128)S(1)} %copy-done.5, s32[8,32]{1,0:T(8,128)S(1)} %copy-done.6, ...), custom_call_target="tpu_custom_call" | custom-call | flops 10000000 | bytes 4000000 | tf_op jit(solution)/shard_map/pallas_call | solution.py:133
  7.7 6.1 %collective-permute-start.3 = (f32[38,8,256]{2,1,0:T(8,128)}, f32[38,8,256]{2,1,0:T(8,128)}, u32[]{:S(2)}, u32[]{:S(2)}) collective-permute-start(f32[38,8,256]{2,1,0:T(8,128)} %get-tuple-element.24.xw_ref), channel_id=1, source_target_pairs={{0,120},{8,0},{16,8},{24,16},{32,24},{40,32},{48,40},{56,48},{64,5... | collective-permute-start | bytes 933896 | tf_op jit(solution)/shard_map/ppermute | solution.py:20
  13.8 0.6 collective-permute-start
  14.4 1.4 %collective-permute-start.1 = (f32[2,32,1792]{2,1,0:T(8,128)}, f32[2,32,1792]{2,1,0:T(8,128)S(1)}, u32[]{:S(2)}, u32[]{:S(2)}) collective-permute-start(f32[2,32,1792]{2,1,0:T(8,128)} %get-tuple-element.22), channel_id=1, source_target_pairs={{0,7},{1,0},{2,1},{3,2},{4,3},{5,4},{6,5},{7,6},{8,15},{9,8},{10,9... | collective-permute-start | bytes 1376264 | tf_op jit(solution)/shard_map/ppermute | solution.py:20
  15.9 0.9 collective-permute-start.6
  16.8 0.1 pad.3.clone
  16.9 0.1 pad_maximum_fusion
  17.0 0.1 stack_tile.7
  17.1 0.1 stack_tile.6
  17.2 11.9 %collective-permute-done.3.he_ref = f32[38,8,256]{2,1,0:T(8,128)} collective-permute-done((f32[38,8,256]{2,1,0:T(8,128)}, f32[38,8,256]{2,1,0:T(8,128)}, u32[]{:S(2)}, u32[]{:S(2)}) %collective-permute-start.3) | collective-permute-done | bytes 311328 | tf_op jit(solution)/shard_map/ppermute | solution.py:20
  29.1 6.8 %collective-permute-done.2.hw_ref = f32[38,8,256]{2,1,0:T(8,128)} collective-permute-done((f32[38,8,256]{2,1,0:T(8,128)}, f32[38,8,256]{2,1,0:T(8,128)}, u32[]{:S(2)}, u32[]{:S(2)}) %collective-permute-start.2) | collective-permute-done | bytes 311328 | tf_op jit(solution)/shard_map/ppermute | solution.py:20
  35.8 3.2 %shard_map.102 = (f32[8,32,512]{2,1,0:T(8,128)S(1)}, f32[72,512]{1,0:T(8,128)S(1)}, f32[64,512]{1,0:T(8,128)S(1)}, f32[6,8,512]{2,1,0:T(8,128)S(1)}) custom-call(f32[38,8,256]{2,1,0:T(8,128)} %get-tuple-element.24.xw_ref, f32[38,8,256]{2,1,0:T(8,128)} %get-tuple-element.25.xe_ref, f32[38,8,256]{2,1,0:T(8,128)} %collective-permute-done.2.hw_ref, ...), custom_call_target="tpu_custom_call" | custom-call | flops 10000000 | bytes 4000000 | tf_op jit(solution)/shard_map/pallas_call | solution.py:133
  39.1 2.0 %collective-permute-start.5 = (f32[72,512]{1,0:T(8,128)S(1)}, f32[72,512]{1,0:T(8,128)S(1)}, u32[]{:S(2)}, u32[]{:S(2)}) collective-permute-start(f32[72,512]{1,0:T(8,128)S(1)} %get-tuple-element.28), channel_id=1, source_target_pairs={{0,7},{1,0},{2,1},{3,2},{4,3},{5,4},{6,5},{7,6},{8,15},{9,8},{10,9... | collective-permute-start | bytes 442376 | tf_op jit(solution)/shard_map/ppermute | solution.py:20
  41.3 20.2 %shard_map.101 = (f32[8,32,1792]{2,1,0:T(8,128)S(1)}, f32[4,32,1792]{2,1,0:T(8,128)S(1)}) custom-call(f32[32,8,2048]{2,1,0:T(8,128)S(1)} %copy-done.1, f32[6,8,2048]{2,1,0:T(8,128)S(1)} %get-tuple-element.19.coef_ref, f32[4,128]{1,0:T(4,128)S(1)} %maximum_maximum_fusion.par_ref, f32[32,128]{1,0:T(8,128)S(1)} %broadcast_in_dim.2.loss_ref, ...), custom_call_target="tpu_custom_call" | custom-call | flops 10000000 | bytes 4000000 | tf_op jit(solution)/shard_map/pallas_call | solution.py:133
  61.6 27.0 %shard_map.103 = (f32[2,32,2048]{2,1,0:T(8,128)S(1)}, f32[2,32,2048]{2,1,0:T(8,128)S(1)}, f32[8,32,2048]{2,1,0:T(8,128)S(1)}) custom-call(f32[8,32,1792]{2,1,0:T(8,128)S(1)} %get-tuple-element.20.mid_ref, f32[2,32,1792]{2,1,0:T(8,128)S(1)} %collective-permute-done.south_ref, f32[2,32,1792]{2,1,0:T(8,128)S(1)} %collective-permute-done.1.north_ref, ...), custom_call_target="tpu_custom_call" | custom-call | flops 10000000 | bytes 4000000 | tf_op jit(solution)/shard_map/pallas_call | solution.py:133
  88.6 2.3 %collective-permute-start.7 = (f32[2,32,2048]{2,1,0:T(8,128)S(1)}, f32[2,32,2048]{2,1,0:T(8,128)S(1)}, u32[]{:S(2)}, u32[]{:S(2)}) collective-permute-start(f32[2,32,2048]{2,1,0:T(8,128)S(1)} %get-tuple-element.31), channel_id=1, source_target_pairs={{0,1},{1,2},{2,3},{3,4},{4,5},{5,6},{6,7},{7,0},{8,9},{9,10},{10,1... | collective-permute-start | bytes 1572872 | tf_op jit(solution)/shard_map/ppermute | solution.py:20
  90.8 7.0 %collective-permute-done.7.south_ref = f32[2,32,2048]{2,1,0:T(8,128)S(1)} collective-permute-done((f32[2,32,2048]{2,1,0:T(8,128)S(1)}, f32[2,32,2048]{2,1,0:T(8,128)S(1)}, u32[]{:S(2)}, u32[]{:S(2)}) %collective-permute-start.7) | collective-permute-done | bytes 524320 | tf_op jit(solution)/shard_map/ppermute | solution.py:20
  97.8 4.3 %collective-permute-done.8.north_ref = f32[2,32,2048]{2,1,0:T(8,128)S(1)} collective-permute-done((f32[2,32,2048]{2,1,0:T(8,128)S(1)}, f32[2,32,2048]{2,1,0:T(8,128)S(1)}, u32[]{:S(2)}, u32[]{:S(2)}) %collective-permute-start.8) | collective-permute-done | bytes 524320 | tf_op jit(solution)/shard_map/ppermute | solution.py:20
  102.1 3.9 %shard_map.104 = f32[32,8,2048]{2,1,0:T(8,128)} custom-call(f32[8,32,2048]{2,1,0:T(8,128)S(1)} %get-tuple-element.30.swept_ref, f32[2,32,2048]{2,1,0:T(8,128)S(1)} %collective-permute-done.7.south_ref, f32[2,32,2048]{2,1,0:T(8,128)S(1)} %collective-permute-done.8.north_ref, f32[6,8,2048]{2,1,0:T(8,128)S(1)} %get-tuple-element.19.coef_ref, ...), custom_call_target="tpu_custom_call" | custom-call | flops 10000000 | bytes 4000000 | tf_op jit(solution)/shard_map/pallas_call | solution.py:133
  (31 shorter events, 0.3 us)
Async XLA Ops:
  0.0 1.6 %copy-start = (f32[32,8,2048]{2,1,0:T(8,128)S(1)}, f32[32,8,2048]{2,1,0:T(8,128)}, u32[]{:S(2)}) copy-start(f32[32,8,2048]{2,1,0:T(8,128)} %x_ref.3) | copy-start | bytes 6291460
  1.6 0.7 copy-start.4
  2.3 0.7 copy-start.5
  3.0 0.7 copy-start.6
  3.7 0.7 copy-start.7
  4.4 12.6 %copy-start.9 = (f32[63]{0:T(128)S(1)}, f32[63]{0:T(128)}, u32[]{:S(2)}) copy-start(f32[63]{0:T(128)} %param.19) | copy-start | bytes 760
  4.4 12.7 %copy-start.10 = (f32[64]{0:T(128)S(1)}, f32[64]{0:T(128)}, u32[]{:S(2)}) copy-start(f32[64]{0:T(128)} %param.17) | copy-start | bytes 772
  4.4 36.8 %copy-start.8 = (f32[32]{0:T(128)S(1)}, f32[32]{0:T(128)}, u32[]{:S(2)}) copy-start(f32[32]{0:T(128)} %param.18) | copy-start | bytes 388
  4.4 36.9 %copy-start.1 = (f32[32,8,2048]{2,1,0:T(8,128)S(1)}, f32[32,8,2048]{2,1,0:T(8,128)}, u32[]{:S(2)}) copy-start(f32[32,8,2048]{2,1,0:T(8,128)} %x_ref.3) | copy-start | bytes 6291460
  4.4 36.9 %copy-start.2 = (f32[32,32]{1,0:T(8,128)S(1)}, f32[32,32]{1,0:T(8,128)}, u32[]{:S(2)}) copy-start(f32[32,32]{1,0:T(8,128)} %night_ref.3) | copy-start | bytes 12292
  4.4 36.9 %copy-start.3 = (f32[32,32]{1,0:T(8,128)S(1)}, f32[32,32]{1,0:T(8,128)}, u32[]{:S(2)}) copy-start(f32[32,32]{1,0:T(8,128)} %photo_ref.3) | copy-start | bytes 12292
  7.7 21.3 %collective-permute-start.3 = (f32[38,8,256]{2,1,0:T(8,128)}, f32[38,8,256]{2,1,0:T(8,128)}, u32[]{:S(2)}, u32[]{:S(2)}) collective-permute-start(f32[38,8,256]{2,1,0:T(8,128)} %get-tuple-element.24.xw_ref), channel_id=1, source_target_pairs={{0,120},{8,0},{16,8},{24,16},{32,24},{40,32},{48,40},{56,48},{64,5... | collective-permute-start | bytes 933896 | tf_op jit(solution)/shard_map/ppermute | solution.py:20
  13.8 22.0 %collective-permute-start.2 = (f32[38,8,256]{2,1,0:T(8,128)}, f32[38,8,256]{2,1,0:T(8,128)}, u32[]{:S(2)}, u32[]{:S(2)}) collective-permute-start(f32[38,8,256]{2,1,0:T(8,128)} %get-tuple-element.25.xe_ref), channel_id=1, source_target_pairs={{0,8},{8,16},{16,24},{24,32},{32,40},{40,48},{48,56},{56,64},{64,7... | collective-permute-start | bytes 933896 | tf_op jit(solution)/shard_map/ppermute | solution.py:20
  13.8 47.7 %collective-permute-start = (f32[2,32,1792]{2,1,0:T(8,128)}, f32[2,32,1792]{2,1,0:T(8,128)S(1)}, u32[]{:S(2)}, u32[]{:S(2)}) collective-permute-start(f32[2,32,1792]{2,1,0:T(8,128)} %get-tuple-element.21), channel_id=1, source_target_pairs={{0,1},{1,2},{2,3},{3,4},{4,5},{5,6},{6,7},{7,0},{8,9},{9,10},{10,1... | collective-permute-start | bytes 1376264 | tf_op jit(solution)/shard_map/ppermute | solution.py:20
  14.4 47.2 %collective-permute-start.1 = (f32[2,32,1792]{2,1,0:T(8,128)}, f32[2,32,1792]{2,1,0:T(8,128)S(1)}, u32[]{:S(2)}, u32[]{:S(2)}) collective-permute-start(f32[2,32,1792]{2,1,0:T(8,128)} %get-tuple-element.22), channel_id=1, source_target_pairs={{0,7},{1,0},{2,1},{3,2},{4,3},{5,4},{6,5},{7,6},{8,15},{9,8},{10,9... | collective-permute-start | bytes 1376264 | tf_op jit(solution)/shard_map/ppermute | solution.py:20
  15.9 45.7 %collective-permute-start.6 = (f32[2,1,2048]{2,1,0:T(1,128)S(1)}, f32[2,1,2048]{2,1,0:T(1,128)S(1)}, u32[]{:S(2)}, u32[]{:S(2)}) collective-permute-start(f32[2,1,2048]{2,1,0:T(1,128)S(1)} %slice.3), channel_id=1, source_target_pairs={{0,7},{1,0},{2,1},{3,2},{4,3},{5,4},{6,5},{7,6},{8,15},{9,8},{10,9... | collective-permute-start | bytes 49160 | tf_op jit(solution)/shard_map/ppermute | solution.py:20
  39.0 22.5 %collective-permute-start.4 = (f32[64,512]{1,0:T(8,128)S(1)}, f32[64,512]{1,0:T(8,128)S(1)}, u32[]{:S(2)}, u32[]{:S(2)}) collective-permute-start(f32[64,512]{1,0:T(8,128)S(1)} %get-tuple-element.27), channel_id=1, source_target_pairs={{0,1},{1,2},{2,3},{3,4},{4,5},{5,6},{6,7},{7,0},{8,9},{9,10},{10,1... | collective-permute-start | bytes 393224 | tf_op jit(solution)/shard_map/ppermute | solution.py:20
  39.1 22.4 %collective-permute-start.5 = (f32[72,512]{1,0:T(8,128)S(1)}, f32[72,512]{1,0:T(8,128)S(1)}, u32[]{:S(2)}, u32[]{:S(2)}) collective-permute-start(f32[72,512]{1,0:T(8,128)S(1)} %get-tuple-element.28), channel_id=1, source_target_pairs={{0,7},{1,0},{2,1},{3,2},{4,3},{5,4},{6,5},{7,6},{8,15},{9,8},{10,9... | collective-permute-start | bytes 442376 | tf_op jit(solution)/shard_map/ppermute | solution.py:20
  88.6 9.2 %collective-permute-start.7 = (f32[2,32,2048]{2,1,0:T(8,128)S(1)}, f32[2,32,2048]{2,1,0:T(8,128)S(1)}, u32[]{:S(2)}, u32[]{:S(2)}) collective-permute-start(f32[2,32,2048]{2,1,0:T(8,128)S(1)} %get-tuple-element.31), channel_id=1, source_target_pairs={{0,1},{1,2},{2,3},{3,4},{4,5},{5,6},{6,7},{7,0},{8,9},{9,10},{10,1... | collective-permute-start | bytes 1572872 | tf_op jit(solution)/shard_map/ppermute | solution.py:20
  90.8 11.3 %collective-permute-start.8 = (f32[2,32,2048]{2,1,0:T(8,128)S(1)}, f32[2,32,2048]{2,1,0:T(8,128)S(1)}, u32[]{:S(2)}, u32[]{:S(2)}) collective-permute-start(f32[2,32,2048]{2,1,0:T(8,128)S(1)} %get-tuple-element.32), channel_id=1, source_target_pairs={{0,7},{1,0},{2,1},{3,2},{4,3},{5,4},{6,5},{7,6},{8,15},{9,8},{10,9... | collective-permute-start | bytes 1572872 | tf_op jit(solution)/shard_map/ppermute | solution.py:20
where the time goes:
time: 106 us
  Pallas kernels  57.7 us (54%)
  waiting for transfers between devices  30 us (28%)
  starting transfers between devices  13.4 us (13%)
  local copies, waits for them, and re-layouts  4.78 us (5%)
    pallas_call x5, Pallas kernels, call(): pl.pallas_call(kernel, out_shape=[jax.ShapeDtypeStruct(s, F32) for s in o...  57.7 us
    ppermute x9, waiting for transfers between devices, ring(): lax.ppermute(value, axis, [(i, (i + steps) % count) for i in range(count)])  30 us
    ppermute x9, starting transfers between devices, ring(): lax.ppermute(value, axis, [(i, (i + steps) % count) for i in range(count)])  13.4 us
    unnamed x22, local copies, waits for them, and re-layouts  4.38 us
  transfers between devices with their start and end apart: 9, of which 4 were waited for; matrix products, arithmetic and copies ran while one was open for 1% of the time, Pallas kernels for 22%

commit v1 on v0

v1 whole, which is shorter than its diff:
```python
import jax
import jax.numpy as jnp
from jax import lax
from jax.experimental import pallas as pl
from jax.experimental.pallas import tpu as pltpu
from jax.sharding import PartitionSpec as P

CHEM = 6
KMAX = 8
PIECE = 128
HALF = 64
LEVELS = 64
VMEM_LIMIT = 24 * 1024 * 1024
F32 = jnp.float32
BF16 = jnp.bfloat16
LON_C, LON_G, LAT_C, LAT_G, DAY, COUNT = range(6)


def ring(value, axis, steps):
    count = lax.axis_size(axis)
    return lax.ppermute(value, axis, [(i, (i + steps) % count) for i in range(count)])


def half_roll(value):
    return pltpu.roll(value, HALF, 1)


def minmod(x, y):
    return jnp.minimum(jnp.maximum(x, jnp.minimum(y, 0.0)), jnp.maximum(y, 0.0))


def gain(cour, switch):
    return 0.5 * cour * switch * jnp.where(cour >= 0.0, 1.0 - cour, -1.0 - cour)


def lon_sweep(cells, cours, gains):
    n = len(cells)
    low = lax.broadcasted_iota(jnp.int32, cells[0].shape, 1) < HALF
    turned = [half_roll(q) for q in cells]
    flux = [None]
    for i in range(1, n):
        west = jnp.where(low, turned[i - 1], turned[i])
        east = jnp.where(low, turned[i], turned[i + 1]) if i < n - 1 else turned[i]
        step = cells[i] - west
        slope = minmod(step, east - cells[i])
        behind = minmod(west - cells[i - 1], step)
        forward = cours[i - 1] >= 0.0
        flux.append(
            cours[i - 1] * jnp.where(forward, west, cells[i])
            + gains[i - 1] * jnp.where(forward, behind, slope)
        )
    turned = [None] + [half_roll(f) for f in flux[1:]]
    return [
        cells[i] - (jnp.where(low, turned[i], turned[i + 1]) - flux[i]) for i in range(1, n - 1)
    ]


def lat_sweep(rows, cours, gains):
    n = len(rows) - 4
    step = [rows[i + 1] - rows[i] for i in range(n + 3)]
    slope = [minmod(step[i], step[i + 1]) for i in range(n + 2)]
    flux = []
    for i in range(n + 1):
        forward = cours[i] >= 0.0
        flux.append(
            cours[i] * jnp.where(forward, rows[i + 1], rows[i + 2])
            + gains[i] * jnp.where(forward, slope[i], slope[i + 1])
        )
    return [rows[i + 2] - (flux[i + 1] - flux[i]) for i in range(n)]


def expand(compact, first):
    rows = compact.shape[0]
    low = lax.broadcasted_iota(jnp.int32, (rows, PIECE), 1) < HALF
    left = jnp.broadcast_to(compact[:, first : first + 1], (rows, PIECE))
    right = jnp.broadcast_to(compact[:, first + 1 : first + 2], (rows, PIECE))
    return jnp.where(low, left, right)


def rate_pieces(night_ref, photo_ref):
    rates = jnp.concatenate([night_ref[...], photo_ref[...]], 0)
    high = rates.astype(BF16)
    low = (rates - high.astype(F32)).astype(BF16)
    return jnp.concatenate([high, high, low], 1)


def react(rows, suns, rates, loss):
    species = rows[0].shape[0]
    for _ in range(CHEM):
        nexts = []
        for q, sun in zip(rows, suns):
            high = q.astype(BF16)
            low = (q - high.astype(F32)).astype(BF16)
            both = jnp.dot(
                rates, jnp.concatenate([high, low, high], 0), preferred_element_type=F32
            )
            top = q + both[:species] + sun * both[species:]
            bottom = 1.0 + loss * q * q
            inverse = pl.reciprocal(bottom, approx=True)
            inverse = inverse * (2.0 - bottom * inverse)
            nexts.append(top * inverse)
        rows = nexts
    return rows


def fill_table(mixing, table_ref):
    shape = (HALF, PIECE)
    lane = lax.broadcasted_iota(jnp.int32, shape, 1)
    low = lane < HALF
    q = jnp.where((lane & (HALF - 1)) == lax.broadcasted_iota(jnp.int32, shape, 0), 1.0, 0.0)
    for n in range(KMAX):
        flux = mixing * (pltpu.roll(q, PIECE - 1, 1) - q)
        q = q + flux - pltpu.roll(flux, 1, 1)
        high = q.astype(BF16).astype(F32)
        for i, term in enumerate((high, q - high)):
            table_ref[0, n, i] = jnp.where(low, term, 0.0).astype(BF16)
            table_ref[1, n, i] = jnp.where(low, 0.0, term).astype(BF16)


def diffuse(q, first, second, table_ref):
    species = q.shape[0]
    high = q.astype(BF16)
    low = (q - high.astype(F32)).astype(BF16)
    state = jnp.concatenate(
        [jnp.concatenate([high, high], 1), jnp.concatenate([low, low], 1)], 0
    )
    powers = jnp.concatenate(
        [table_ref[0, first - 1, i] if side == 0 else table_ref[1, second - 1, i] for i in (0, 1) for side in (0, 1)], 0
    )
    both = jnp.dot(state, powers, preferred_element_type=F32)
    return both[:species] + both[species:]


def column_block(rows, days, counts, rates, loss, level, table_ref):
    pieces = rows[0].shape[1] // PIECE
    level = jnp.concatenate([level] * pieces, 1)
    loss = jnp.concatenate([loss] * pieces, 1)
    rows = react(rows, [day * level for day in days], rates, loss)
    return [
        [
            diffuse(q[:, j * PIECE : (j + 1) * PIECE], counts(i, 2 * j), counts(i, 2 * j + 1), table_ref)
            for j in range(pieces)
        ]
        for i, q in enumerate(rows)
    ]


WHOLE = pl.BlockSpec(memory_space=pltpu.VMEM)
SCALARS = pl.BlockSpec(memory_space=pltpu.SMEM)
FAR = pl.BlockSpec(memory_space=pl.ANY)
BLOCK = 4 * PIECE


def call(kernel, outs, ins, *args, scratch=(), out_specs=None, cost=10.0):
    return pl.pallas_call(
        kernel,
        out_shape=[s if isinstance(s, jax.ShapeDtypeStruct) else jax.ShapeDtypeStruct(s, F32) for s in outs],
        in_specs=ins,
        out_specs=out_specs or [WHOLE] * len(outs),
        scratch_shapes=list(scratch),
        compiler_params=pltpu.CompilerParams(vmem_limit_bytes=VMEM_LIMIT),
        cost_estimate=pl.CostEstimate(flops=0, bytes_accessed=int(cost * 3.0e6), transcendentals=0),
    )(*args)


def lanes_of(j, count=1):
    return slice(j * PIECE, (j + count) * PIECE)


def blocks(width, body):
    full = width // BLOCK

    def step(b, carry):
        body(pl.multiple_of(b * BLOCK, BLOCK), BLOCK)
        return carry

    if full:
        lax.fori_loop(0, full, step, 0)
    if width % BLOCK:
        body(full * BLOCK, width % BLOCK)


def tiles(species, body):
    def step(s, carry):
        body(pl.ds(pl.multiple_of(s * 8, 8), 8))
        return carry

    lax.fori_loop(0, species // 8, step, 0)


def wide(row, lanes):
    return jnp.concatenate([row] * (lanes // PIECE), 1)


def first_kernel(
    x_ref, cour_in, sw_in, day_in, cnt_in,
    xt_ref, south_ref, north_ref, west_ref, east_ref, coef_ref, row_ref,
    cour_ref, sw_ref, day_ref, cnt_ref, row_sems, sems,
):
    rows, species, width = xt_ref.shape
    pieces = width // PIECE
    edge = (0, 1, rows - 2, rows - 1)
    small = [
        pltpu.make_async_copy(a, b, sems.at[i])
        for i, (a, b) in enumerate(((cour_in, cour_ref), (sw_in, sw_ref), (day_in, day_ref), (cnt_in, cnt_ref)))
    ]
    big = [pltpu.make_async_copy(x_ref.at[:, r, :], xt_ref.at[r], row_sems.at[r]) for r in range(rows)]
    for copy in small:
        copy.start()
    for r in edge + tuple(range(2, rows - 2)):
        big[r].start()
    for copy in small:
        copy.wait()
    cour = [cour_ref[0], cour_ref[1]]
    switch = [sw_ref[0].astype(F32), sw_ref[1].astype(F32)]
    fields = [
        cour[0],
        gain(cour[0], switch[0]),
        cour[1],
        gain(cour[1], switch[1]),
        day_ref[...].astype(F32),
        cnt_ref[...].astype(F32),
    ]
    for i, field in enumerate(fields):
        for j in range(pieces):
            coef_ref[i, :, lanes_of(j)] = expand(field, 2 * j)
    row_ref[0:8] = coef_ref[LAT_C]
    row_ref[8:16] = coef_ref[LAT_G]
    for r in edge:
        big[r].wait()

    def tile(block):
        for r in edge:
            cells = [xt_ref[r, block, lanes_of(j)] for j in range(pieces)]
            faces = [
                [coef_ref[i, r : r + 1, lanes_of(j)] for j in range(1, pieces)] for i in (LON_C, LON_G)
            ]
            ref, row = (south_ref, r) if r < 2 else (north_ref, r - rows + 2)
            for j, value in enumerate(lon_sweep(cells, *faces)):
                ref[row, block, lanes_of(j)] = value

    tiles(species, tile)
    for r in range(2, rows - 2):
        big[r].wait()
    for ref, j in ((west_ref, 0), (east_ref, pieces - 2)):
        for r in range(rows):
            ref[r * species : (r + 1) * species] = xt_ref[r, :, lanes_of(j, 2)]
        for i in range(6):
            at = rows * species + i * rows
            ref[at : at + rows] = coef_ref[i, :, lanes_of(j, 2)]


def inner_kernel(
    xt_ref, south_ref, north_ref, coef_ref, par_ref, loss_ref, night_ref, photo_ref, cnt_ref,
    mid_ref, done_ref, table_ref,
):
    rows, species, width = xt_ref.shape
    pieces = width // PIECE
    inner = range(2, rows - 2)

    def tile(block):
        for r in inner:
            cells = [xt_ref[r, block, lanes_of(j)] for j in range(pieces)]
            faces = [
                [coef_ref[i, r : r + 1, lanes_of(j)] for j in range(1, pieces)] for i in (LON_C, LON_G)
            ]
            for j, value in enumerate(lon_sweep(cells, *faces)):
                mid_ref[r - 2, block, lanes_of(j)] = value

    tiles(species, tile)
    fill_table(par_ref[1:2], table_ref)
    rates = rate_pieces(night_ref, photo_ref)

    def block(at, lanes):
        here = pl.ds(at, lanes)
        own = pl.ds(at + PIECE if isinstance(at, int) else pl.multiple_of(at + PIECE, PIECE), lanes)
        column = 2 + at // LEVELS
        cells = (
            [south_ref[i, :, here] for i in (0, 1)]
            + [mid_ref[i, :, here] for i in range(rows - 4)]
            + [north_ref[i, :, here] for i in (0, 1)]
        )
        faces = [[coef_ref[i, f : f + 1, own] for f in range(2, rows - 1)] for i in (LAT_C, LAT_G)]
        done = column_block(
            lat_sweep(cells, *faces),
            [coef_ref[DAY, r : r + 1, own] for r in inner],
            lambda i, j: cnt_ref[2 + i, column + j],
            rates,
            loss_ref[...],
            par_ref[0:1],
            table_ref,
        )
        for i, row in enumerate(done):
            done_ref[i, :, here] = jnp.concatenate(row, 1)

    blocks(width - 2 * PIECE, block)


def side_kernel(
    done_ref, xw_ref, xe_ref, hw_ref, he_ref, coef_ref, mid_ref, south_ref, north_ref, side_ref
):
    rows, species = mid_ref.shape[:2]
    width = coef_ref.shape[2]
    base = rows * species
    for i in range(6):
        here = slice(base + i * rows, base + (i + 1) * rows)
        side_ref[i, :, lanes_of(0)] = hw_ref[here, lanes_of(1)]
        side_ref[i, :, lanes_of(1)] = coef_ref[i, :, 0:PIECE]
        side_ref[i, :, lanes_of(2)] = coef_ref[i, :, width - PIECE : width]
        side_ref[i, :, lanes_of(3)] = he_ref[here, lanes_of(0)]

    def tile(s, carry):
        for r in range(rows):
            row = slice(r, r + 1)
            from_row = pl.ds(pl.multiple_of(r * species + s * 8, 8), 8)
            block = pl.ds(pl.multiple_of(s * 8, 8), 8)
            faces = [
                [side_ref[i, row, lanes_of(0)], side_ref[i, row, lanes_of(1)], coef_ref[i, row, lanes_of(1)]]
                for i in (LON_C, LON_G)
            ]
            out = lon_sweep([ref[from_row, lanes_of(h)] for ref in (hw_ref, xw_ref) for h in (0, 1)], *faces)
            faces = [
                [
                    side_ref[i, row, lanes_of(2)],
                    side_ref[i, row, lanes_of(3)],
                    he_ref[base + i * rows + r : base + i * rows + r + 1, lanes_of(1)],
                ]
                for i in (LON_C, LON_G)
            ]
            out = out + lon_sweep([ref[from_row, lanes_of(h)] for ref in (xe_ref, he_ref) for h in (0, 1)], *faces)
            for j, value in enumerate(out):
                mid_ref[r, block, lanes_of(j)] = value
                if r < 2:
                    south_ref[pl.ds(pl.multiple_of(r * species + s * 8, 8), 8), lanes_of(j)] = value
                if r >= rows - 2:
                    north_ref[pl.ds(pl.multiple_of((r - rows + 2) * species + s * 8, 8), 8), lanes_of(j)] = value
        return carry

    lax.fori_loop(0, species // 8, tile, 0)
    for j in range(4):
        two = [side_ref[i, 0:1, lanes_of(j)] for i in (LAT_C, LAT_G)]
        south_ref[2 * species : 2 * species + 8, lanes_of(j)] = jnp.concatenate([two[0]] * 4 + [two[1]] * 4, 0)


def edge_kernel(
    mid_ref, own_south_ref, own_north_ref, south_ref, north_ref, coef_ref, row_ref,
    par_ref, loss_ref, night_ref, photo_ref, table_ref, cnt_ref,
    done_ref, sent_south_ref, sent_north_ref,
):
    species, inner_width = mid_ref.shape[1:]
    rows = coef_ref.shape[1]
    rates = rate_pieces(night_ref, photo_ref)
    edge = (0, 1, rows - 2, rows - 1)

    def block(at, lanes):
        here = pl.ds(at, lanes)
        own = pl.ds(at + PIECE if isinstance(at, int) else pl.multiple_of(at + PIECE, PIECE), lanes)
        column = 2 + at // LEVELS
        valid_south, valid_north = wide(par_ref[2:3], lanes), wide(par_ref[3:4], lanes)
        lower = (
            [south_ref[i, :, here] * valid_south for i in (0, 1)]
            + [own_south_ref[i, :, here] for i in (0, 1)]
            + [mid_ref[i, :, here] for i in (0, 1)]
        )
        upper = (
            [mid_ref[i, :, here] for i in (2, 3)]
            + [own_north_ref[i, :, here] for i in (0, 1)]
            + [north_ref[i, :, here] * valid_north for i in (0, 1)]
        )
        lower_faces = [
            [coef_ref[i, 0:1, own] * valid_south, coef_ref[i, 1:2, own], coef_ref[i, 2:3, own]]
            for i in (LAT_C, LAT_G)
        ]
        upper_faces = [
            [
                coef_ref[i, rows - 2 : rows - 1, own],
                coef_ref[i, rows - 1 : rows, own],
                row_ref[8 * (i - LAT_C) : 8 * (i - LAT_C) + 1, own] * valid_north,
            ]
            for i in (LAT_C, LAT_G)
        ]
        done = column_block(
            lat_sweep(lower, *lower_faces) + lat_sweep(upper, *upper_faces),
            [coef_ref[DAY, r : r + 1, own] for r in edge],
            lambda i, j: cnt_ref[edge[i], column + j],
            rates,
            loss_ref[...],
            par_ref[0:1],
            table_ref,
        )
        for i, row in enumerate(done):
            done_ref[i, :, here] = jnp.concatenate(row, 1)

    blocks(inner_width, block)
    pieces = inner_width // PIECE

    def tile(block):
        for k, r in enumerate(edge):
            cells = [done_ref[k, block, lanes_of(j)] for j in range(pieces)]
            faces = [
                [coef_ref[i, r : r + 1, lanes_of(j + 1)] for j in range(1, pieces)] for i in (LON_C, LON_G)
            ]
            ref = sent_south_ref if k < 2 else sent_north_ref
            for j, value in enumerate(lon_sweep(cells, *faces)):
                ref[k % 2, block, lanes_of(j)] = value

    tiles(species, tile)


def corner_kernel(
    mid_ref, south_ref, north_ref, edge_ref, coef_ref, side_ref,
    par_ref, loss_ref, night_ref, photo_ref, table_ref, cnt_ref,
    done_ref, sent_south_ref, sent_north_ref,
):
    rows, species, width = mid_ref.shape
    rates = rate_pieces(night_ref, photo_ref)
    valid_south, valid_north = wide(par_ref[2:3], width), wide(par_ref[3:4], width)
    cells = (
        [south_ref[i * species : (i + 1) * species] * valid_south for i in (0, 1)]
        + [mid_ref[r] for r in range(rows)]
        + [north_ref[i * species : (i + 1) * species] * valid_north for i in (0, 1)]
    )
    faces = [
        [side_ref[i, 0:1] * valid_south]
        + [side_ref[i, r : r + 1] for r in range(1, rows)]
        + [north_ref[2 * species + 4 * (i - LAT_C) : 2 * species + 4 * (i - LAT_C) + 1] * valid_north]
        for i in (LAT_C, LAT_G)
    ]
    for r, q in enumerate(lat_sweep(cells, *faces)):
        done_ref[r] = q
    for part in (0, rows // 2):
        done = column_block(
            [done_ref[part + i] for i in range(rows // 2)],
            [side_ref[DAY, part + i : part + i + 1] for i in range(rows // 2)],
            lambda i, j: cnt_ref[part + i, j],
            rates,
            loss_ref[...],
            par_ref[0:1],
            table_ref,
        )
        for i, row in enumerate(done):
            done_ref[part + i] = jnp.concatenate(row, 1)
    last = edge_ref.shape[2] // PIECE
    total = coef_ref.shape[2] // PIECE

    def tile(block):
        for k, r in enumerate((0, 1, rows - 2, rows - 1)):
            row = slice(r, r + 1)
            ref = sent_south_ref if k < 2 else sent_north_ref
            cells = [done_ref[r, block, lanes_of(j)] for j in (0, 1)] + [
                edge_ref[k, block, lanes_of(j)] for j in (0, 1)
            ]
            faces = [[coef_ref[i, row, lanes_of(j)] for j in range(3)] for i in (LON_C, LON_G)]
            out = lon_sweep(cells, *faces)
            cells = [edge_ref[k, block, lanes_of(j)] for j in (last - 2, last - 1)] + [
                done_ref[r, block, lanes_of(j)] for j in (2, 3)
            ]
            faces = [
                [coef_ref[i, row, lanes_of(j)] for j in (total - 2, total - 1)] + [side_ref[i, row, lanes_of(3)]]
                for i in (LON_C, LON_G)
            ]
            for j, value in enumerate(out + lon_sweep(cells, *faces)):
                ref[k % 2, block, lanes_of(j)] = value

    tiles(species, tile)


def rest_kernel(
    done_ref, corner_ref, south_a_ref, north_a_ref, south_c_ref, north_c_ref, coef_ref, side_ref, swept_ref, out_ref
):
    count, species = done_ref.shape[:2]
    width = coef_ref.shape[2]
    pieces = width // PIECE

    def tile(block):
        for k in range(count):
            row = slice(k + 2, k + 3)
            cells = (
                [corner_ref[k + 2, block, lanes_of(j)] for j in (0, 1)]
                + [done_ref[k, block, lanes_of(j)] for j in range(pieces - 2)]
                + [corner_ref[k + 2, block, lanes_of(j)] for j in (2, 3)]
            )
            faces = [
                [coef_ref[i, row, lanes_of(j)] for j in range(pieces)] + [side_ref[i, row, lanes_of(3)]]
                for i in (LON_C, LON_G)
            ]
            for j, value in enumerate(lon_sweep(cells, *faces)):
                swept_ref[k, block, lanes_of(j)] = value

    tiles(species, tile)

    for j in range(pieces):
        own = lanes_of(j)
        (a, c), at = join(j, pieces)
        south, north = ((south_c_ref, north_c_ref) if c else (south_a_ref, north_a_ref))
        cells = (
            [south[i, :, at] for i in (0, 1)]
            + [swept_ref[i, :, own] for i in range(count)]
            + [north[i, :, at] for i in (0, 1)]
        )
        faces = [[coef_ref[i, f : f + 1, own] for f in range(2, count + 3)] for i in (LAT_C, LAT_G)]
        for i, q in enumerate(lat_sweep(cells, *faces)):
            out_ref[i, :, own] = q


def join(j, pieces):
    if 2 <= j < pieces - 2:
        return (True, False), lanes_of(j - 2)
    return (False, True), lanes_of(j if j < 2 else j - pieces + 4)


def last_kernel(
    inner_ref, swept_ref, own_south_a, own_north_a, own_south_c, own_north_c,
    south_a, north_a, south_c, north_c, coef_ref, row_ref, par_ref,
    out_ref, edge_ref, sems,
):
    count, species, width = inner_ref.shape
    rows = count + 4
    pieces = width // PIECE
    edge = (0, 1, rows - 2, rows - 1)
    copies = [
        pltpu.make_async_copy(inner_ref.at[i], out_ref.at[:, i + 2, :], sems.at[i]) for i in range(count)
    ]
    for copy in copies:
        copy.start()
    valid_south, valid_north = par_ref[2:3], par_ref[3:4]
    for j in range(pieces):
        own = lanes_of(j)
        (_, c), at = join(j, pieces)
        south, own_south, own_north, north = (
            (south_c, own_south_c, own_north_c, north_c) if c else (south_a, own_south_a, own_north_a, north_a)
        )
        lower = (
            [south[i, :, at] * valid_south for i in (0, 1)]
            + [own_south[i, :, at] for i in (0, 1)]
            + [swept_ref[i, :, own] for i in (0, 1)]
        )
        upper = (
            [swept_ref[i, :, own] for i in (2, 3)]
            + [own_north[i, :, at] for i in (0, 1)]
            + [north[i, :, at] * valid_north for i in (0, 1)]
        )
        lower_faces = [
            [coef_ref[i, 0:1, own] * valid_south, coef_ref[i, 1:2, own], coef_ref[i, 2:3, own]]
            for i in (LAT_C, LAT_G)
        ]
        upper_faces = [
            [
                coef_ref[i, rows - 2 : rows - 1, own],
                coef_ref[i, rows - 1 : rows, own],
                row_ref[8 * (i - LAT_C) : 8 * (i - LAT_C) + 1, own] * valid_north,
            ]
            for i in (LAT_C, LAT_G)
        ]
        for k, q in enumerate(lat_sweep(lower, *lower_faces) + lat_sweep(upper, *upper_faces)):
            edge_ref[k, :, own] = q
    more = [
        pltpu.make_async_copy(edge_ref.at[k], out_ref.at[:, r, :], sems.at[count + k]) for k, r in enumerate(edge)
    ]
    for copy in more:
        copy.start()
    for copy in copies + more:
        copy.wait()


def shards(
    tracers,
    courant,
    switches,
    day_flags,
    diffusion_counts,
    night_rates,
    photo_rates,
    level_light,
    self_loss,
    vertical_mixing,
):
    species, rows, width = tracers.shape
    inner = width - 2 * PIECE
    lat_count = lax.axis_size("lat")
    lat = lax.axis_index("lat")
    two = 2 * PIECE
    four = 4 * PIECE
    message = (rows * species + 6 * rows, two)

    xt, own_south, own_north, west, east, coef, own_row = call(
        first_kernel,
        [(rows, species, width), (2, species, inner), (2, species, inner), message, message, (6, rows, width), (16, width)],
        [FAR] * 5,
        tracers,
        courant,
        switches,
        day_flags,
        diffusion_counts,
        scratch=[
            pltpu.VMEM(courant.shape, F32),
            pltpu.VMEM(switches.shape, jnp.int32),
            pltpu.VMEM(day_flags.shape, jnp.int32),
            pltpu.VMEM(diffusion_counts.shape, jnp.int32),
            pltpu.SemaphoreType.DMA((rows,)),
            pltpu.SemaphoreType.DMA((4,)),
        ],
        cost=3,
    )
    south = ring(own_north, "lat", 1)
    north = ring(own_south, "lat", -1)
    halo_west = ring(east, "lon", 1)
    halo_east = ring(west, "lon", -1)
    row = ring(own_row, "lat", -1)

    edge = jnp.zeros((1,), F32)
    mixing = jnp.concatenate([vertical_mixing, edge])
    ones = jnp.ones((PIECE,), F32)
    par = jnp.stack(
        [
            jnp.tile(level_light, 2),
            jnp.tile(mixing, 2),
            ones * (lat > 0).astype(F32),
            ones * (lat < lat_count - 1).astype(F32),
        ]
    )
    loss = jnp.broadcast_to(self_loss[:, None], (species, PIECE))
    chem = (par, loss, night_rates, photo_rates)

    mid, done, table = call(
        inner_kernel,
        [
            (rows - 4, species, inner),
            (rows - 4, species, inner),
            jax.ShapeDtypeStruct((2, KMAX, 2, HALF, PIECE), BF16),
        ],
        [WHOLE] * 8 + [SCALARS],
        xt,
        own_south,
        own_north,
        coef,
        *chem,
        diffusion_counts,
        cost=9,
    )
    mid_side, side_south, side_north, side = call(
        side_kernel,
        [(rows, species, four), (2 * species + 8, four), (2 * species, four), (6, rows, four)],
        [pl.BlockSpec(memory_space=pl.ANY)] + [WHOLE] * 5,
        done,
        west,
        east,
        halo_west,
        halo_east,
        coef,
        cost=3,
    )
    counts = side[COUNT][:, ::LEVELS].astype(jnp.int32)
    side_from_south = ring(side_north, "lat", 1)
    side_from_north = ring(side_south, "lat", -1)
    edge_done, main_south, main_north = call(
        edge_kernel,
        [(4, species, inner), (2, species, inner - two), (2, species, inner - two)],
        [WHOLE] * 12 + [SCALARS],
        mid,
        own_south,
        own_north,
        south,
        north,
        coef,
        row,
        *chem,
        table,
        diffusion_counts,
        cost=9,
    )
    main_from_south = ring(main_north, "lat", 1)
    main_from_north = ring(main_south, "lat", -1)
    corner, corner_south, corner_north = call(
        corner_kernel,
        [(rows, species, four), (2, species, four), (2, species, four)],
        [WHOLE] * 11 + [SCALARS],
        mid_side,
        side_from_south,
        side_from_north,
        edge_done,
        coef,
        side,
        *chem,
        table,
        counts,
        cost=5,
    )
    corner_from_south = ring(corner_north, "lat", 1)
    corner_from_north = ring(corner_south, "lat", -1)
    swept, inner_out = call(
        rest_kernel,
        [(rows - 4, species, width), (rows - 4, species, width)],
        [WHOLE] * 8,
        done,
        corner,
        main_south,
        main_north,
        corner_south,
        corner_north,
        coef,
        side,
        cost=4,
    )
    (out,) = call(
        last_kernel,
        [(species, rows, width)],
        [WHOLE] * 13,
        inner_out,
        swept,
        main_south,
        main_north,
        corner_south,
        corner_north,
        main_from_south,
        main_from_north,
        corner_from_south,
        corner_from_north,
        coef,
        row,
        par,
        scratch=[pltpu.VMEM((4, species, width), F32), pltpu.SemaphoreType.DMA((rows,))],
        out_specs=[FAR],
        cost=3,
    )
    return out


def solution(mesh):
    in_specs = (
        P(None, "lat", "lon"),
        P(None, "lat", "lon"),
        P(None, "lat", "lon"),
        P("lat", "lon"),
        P("lat", "lon"),
        P(),
        P(),
        P(),
        P(),
        P(),
    )
    out_specs = P(None, "lat", "lon")
    return jax.shard_map(shards, mesh=mesh, in_specs=in_specs, out_specs=out_specs, check_vma=False)
```

time: 106 us -> 76.3 us (0.72)
  the two profiles are of different devices: /device:TPU:6 before, /device:TPU:0 now
where the time goes in v1:
time: 76.3 us; the launch traced here: 75.5 us
  Pallas kernels  34.3 us (45%)
  starting transfers between devices  19.6 us (26%)
  local copies, waits for them, and re-layouts  11.3 us (15%)
  waiting for transfers between devices  9.78 us (13%)
    pallas_call x7, Pallas kernels, call(): pl.pallas_call(kernel, out_shape=[s if isinstance(s, jax.ShapeDtypeStruct...  34.3 us
    ppermute x11, starting transfers between devices, ring(): lax.ppermute(value, axis, [(i, (i + steps) % count) for i in range(count)])  19.6 us
    unnamed x42, local copies, waits for them, and re-layouts  10.9 us
    ppermute x11, waiting for transfers between devices, ring(): lax.ppermute(value, axis, [(i, (i + steps) % count) for i in range(count)])  9.78 us
  transfers between devices with their start and end apart: 11, of which 3 were waited for; matrix products, arithmetic and copies ran while one was open for 1% of the time, Pallas kernels for 36%

profile of v1, /device:TPU:0, one launch (start us, length us, event | category | flops | bytes accessed | tf_op | source)
XLA Modules:
  0.0 75.5 jit_solution(10400194413805250538)
XLA Ops:
  0.0 1.6 %copy-done = f32[32,8,2048]{2,1,0:T(8,128)S(1)} copy-done((f32[32,8,2048]{2,1,0:T(8,128)S(1)}, f32[32,8,2048]{2,1,0:T(8,128)}, u32[]{:S(2)}) %copy-start) | copy-done | bytes 2097176
  4.4 4.3 %shard_map.100 = (f32[8,32,2048]{2,1,0:T(8,128)S(1)}, f32[2,32,1792]{2,1,0:T(8,128)}, f32[2,32,1792]{2,1,0:T(8,128)}, f32[304,256]{1,0:T(8,128)}, f32[304,256]{1...) custom-call(f32[32,8,2048]{2,1,0:T(8,128)S(1)} %copy-done, f32[2,8,32]{2,1,0:T(8,128)S(1)} %copy-done.15, ...), custom_call_target="tpu_custom_call" | custom-call | bytes 9000000 | tf_op jit(solution)/shard_map/pallas_call | solution.py:155
  8.7 1.6 %collective-permute-start.4 = (f32[2,32,1792]{2,1,0:T(8,128)}, f32[2,32,1792]{2,1,0:T(8,128)}, u32[]{:S(2)}, u32[]{:S(2)}) collective-permute-start(f32[2,32,1792]{2,1,0:T(8,128)} %get-tuple-element.29.north_ref.own_north_ref), channel_id=1, source_target_pairs={{0,1},{1,2},{2,3},{3,4},{4,5},{5,6},{6,7},{7,0},{8,9},{9,10},{10,1... | collective-permute-start | bytes 1376264 | tf_op jit(solution)/shard_map/ppermute | solution.py:21
  10.3 2.6 %collective-permute-start.5 = (f32[2,32,1792]{2,1,0:T(8,128)}, f32[2,32,1792]{2,1,0:T(8,128)}, u32[]{:S(2)}, u32[]{:S(2)}) collective-permute-start(f32[2,32,1792]{2,1,0:T(8,128)} %get-tuple-element.28.south_ref.own_south_ref), channel_id=1, source_target_pairs={{0,7},{1,0},{2,1},{3,2},{4,3},{5,4},{6,5},{7,6},{8,15},{9,8},{10,9... | collective-permute-start | bytes 1376264 | tf_op jit(solution)/shard_map/ppermute | solution.py:21
  12.9 1.7 %collective-permute-start.6 = (f32[16,2048]{1,0:T(8,128)}, f32[16,2048]{1,0:T(8,128)S(1)}, u32[]{:S(2)}, u32[]{:S(2)}) collective-permute-start(f32[16,2048]{1,0:T(8,128)} %get-tuple-element.38), channel_id=1, source_target_pairs={{0,7},{1,0},{2,1},{3,2},{4,3},{5,4},{6,5},{7,6},{8,15},{9,8},{10,9... | collective-permute-start | bytes 393224 | tf_op jit(solution)/shard_map/ppermute | solution.py:21
  14.6 5.4 %collective-permute-start.1 = (f32[304,256]{1,0:T(8,128)}, f32[304,256]{1,0:T(8,128)}, u32[]{:S(2)}, u32[]{:S(2)}) collective-permute-start(f32[304,256]{1,0:T(8,128)} %get-tuple-element.32.xw_ref), channel_id=1, source_target_pairs={{0,120},{8,0},{16,8},{24,16},{32,24},{40,32},{48,40},{56,48},{64,5... | collective-permute-start | bytes 933896 | tf_op jit(solution)/shard_map/ppermute | solution.py:21
  20.6 0.7 copy-done.5
  21.3 0.7 copy-done.8
  22.7 9.1 %shard_map.101 = (f32[4,32,1792]{2,1,0:T(8,128)S(1)}, f32[4,32,1792]{2,1,0:T(8,128)S(1)}, bf16[2,8,2,64,128]{4,3,2,1,0:T(8,128)(2,1)S(1)}) custom-call(f32[8,32,2048]{2,1,0:T(8,128)S(1)} %get-tuple-element.27.xt_ref, f32[2,32,1792]{2,1,0:T(8,128)} %get-tuple-element.28.south_ref.own_south_ref, f32[2,32,1792]{2,1,0:T(8,128)} %get-tuple-element.29.north_ref.own_north_ref, ...), custom_call_target="tpu_custom_call" | custom-call | bytes 27000000 | tf_op jit(solution)/shard_map/pallas_call | solution.py:155
  31.9 0.8 copy-done.6
  33.3 8.4 %shard_map.103 = (f32[4,32,1792]{2,1,0:T(8,128)S(1)}, f32[2,32,1536]{2,1,0:T(8,128)S(1)}, f32[2,32,1536]{2,1,0:T(8,128)S(1)}) custom-call(f32[4,32,1792]{2,1,0:T(8,128)S(1)} %get-tuple-element.37.mid_ref, f32[2,32,1792]{2,1,0:T(8,128)} %get-tuple-element.28.south_ref.own_south_ref, f32[2,32,1792]{2,1,0:T(8,128)} %get-tuple-element.29.north_ref.own_north_ref, ...), custom_call_target="tpu_custom_call" | custom-call | bytes 27000000 | tf_op jit(solution)/shard_map/pallas_call | solution.py:155
  42.1 3.9 %collective-permute-start.8 = (f32[2,32,1536]{2,1,0:T(8,128)S(1)}, f32[2,32,1536]{2,1,0:T(8,128)}, u32[]{:S(2)}, u32[]{:S(2)}) collective-permute-start(f32[2,32,1536]{2,1,0:T(8,128)S(1)} %get-tuple-element.43.south_a_ref.own_south_a), channel_id=1, source_target_pairs={{0,7},{1,0},{2,1},{3,2},{4,3},{5,4},{6,5},{7,6},{8,15},{9,8},{10,9... | collective-permute-start | bytes 1179656 | tf_op jit(solution)/shard_map/ppermute | solution.py:21
  46.0 3.0 %shard_map.102 = (f32[8,32,512]{2,1,0:T(8,128)S(1)}, f32[72,512]{1,0:T(8,128)}, f32[64,512]{1,0:T(8,128)}, f32[6,8,512]{2,1,0:T(8,128)S(1)}) custom-call(f32[4,32,1792]{2,1,0:T(8,128)S(1)} %get-tuple-element.31.done_ref, f32[304,256]{1,0:T(8,128)} %get-tuple-element.32.xw_ref, f32[304,256]{1,0:T(8,128)} %get-tuple-element.33.xe_ref, ...), custom_call_target="tpu_custom_call" | custom-call | bytes 9000000 | tf_op jit(solution)/shard_map/pallas_call | solution.py:155
  49.0 0.8 %copy-done.3 = f32[8,32,512]{2,1,0:T(8,128)} copy-done((f32[8,32,512]{2,1,0:T(8,128)}, f32[8,32,512]{2,1,0:T(8,128)S(1)}, u32[]{:S(2)}) %copy-start.3) | copy-done | bytes 524312
  49.9 2.0 %collective-permute-start.2 = (f32[64,512]{1,0:T(8,128)}, f32[64,512]{1,0:T(8,128)}, u32[]{:S(2)}, u32[]{:S(2)}) collective-permute-start(f32[64,512]{1,0:T(8,128)} %get-tuple-element.35), channel_id=1, source_target_pairs={{0,1},{1,2},{2,3},{3,4},{4,5},{5,6},{6,7},{7,0},{8,9},{9,10},{10,1... | collective-permute-start | bytes 393224 | tf_op jit(solution)/shard_map/ppermute | solution.py:21
  52.0 5.3 %collective-permute-done.2.south_ref = f32[64,512]{1,0:T(8,128)} collective-permute-done((f32[64,512]{1,0:T(8,128)}, f32[64,512]{1,0:T(8,128)}, u32[]{:S(2)}, u32[]{:S(2)}) %collective-permute-start.2) | collective-permute-done | bytes 131104 | tf_op jit(solution)/shard_map/ppermute | solution.py:21
  57.3 1.0 %copy-done.2 = bf16[2,8,2,64,128]{4,3,2,1,0:T(8,128)(2,1)S(1)} copy-done((bf16[2,8,2,64,128]{4,3,2,1,0:T(8,128)(2,1)S(1)}, bf16[2,8,2,64,128]{4,3,2,1,0:T(8,128)(2,1)}, u32[]{:S(2)}) %copy-start.2) | copy-done | bytes 524312
  58.3 1.0 %copy-done.4 = f32[8,32,512]{2,1,0:T(8,128)S(1)} copy-done((f32[8,32,512]{2,1,0:T(8,128)S(1)}, f32[8,32,512]{2,1,0:T(8,128)}, u32[]{:S(2)}) %copy-start.4) | copy-done | bytes 524312
  59.4 4.6 %shard_map.104 = (f32[8,32,512]{2,1,0:T(8,128)S(1)}, f32[2,32,512]{2,1,0:T(8,128)S(1)}, f32[2,32,512]{2,1,0:T(8,128)S(1)}) custom-call(f32[8,32,512]{2,1,0:T(8,128)S(1)} %copy-done.4, f32[64,512]{1,0:T(8,128)} %collective-permute-done.2.south_ref, f32[72,512]{1,0:T(8,128)S(1)} %collective-permute-done.3.north_ref, ...), custom_call_target="tpu_custom_call" | custom-call | bytes 15000000 | tf_op jit(solution)/shard_map/pallas_call | solution.py:155
  63.9 1.5 %collective-permute-start.10 = (f32[2,32,512]{2,1,0:T(8,128)S(1)}, f32[2,32,512]{2,1,0:T(8,128)S(1)}, u32[]{:S(2)}, u32[]{:S(2)}) collective-permute-start(f32[2,32,512]{2,1,0:T(8,128)S(1)} %get-tuple-element.45.south_c_ref.own_south_c), channel_id=1, source_target_pairs={{0,7},{1,0},{2,1},{3,2},{4,3},{5,4},{6,5},{7,6},{8,15},{9,8},{10,9... | collective-permute-start | bytes 393224 | tf_op jit(solution)/shard_map/ppermute | solution.py:21
  66.0 2.0 %shard_map.105 = (f32[4,32,2048]{2,1,0:T(8,128)S(1)}, f32[4,32,2048]{2,1,0:T(8,128)S(1)}) custom-call(f32[4,32,1792]{2,1,0:T(8,128)S(1)} %get-tuple-element.31.done_ref, f32[8,32,512]{2,1,0:T(8,128)S(1)} %get-tuple-element.42.corner_ref, f32[2,32,1536]{2,1,0:T(8,128)S(1)} %get-tuple-element.43.south_a_ref.own_south_a, ...), custom_call_target="tpu_custom_call" | custom-call | bytes 12000000 | tf_op jit(solution)/shard_map/pallas_call | solution.py:155
  68.0 1.0 %collective-permute-done.10.north_c = f32[2,32,512]{2,1,0:T(8,128)S(1)} collective-permute-done((f32[2,32,512]{2,1,0:T(8,128)S(1)}, f32[2,32,512]{2,1,0:T(8,128)S(1)}, u32[]{:S(2)}, u32[]{:S(2)}) %collective-permute-start.10) | collective-permute-done | bytes 131104 | tf_op jit(solution)/shard_map/ppermute | solution.py:21
  69.0 3.5 %collective-permute-done.9.south_c = f32[2,32,512]{2,1,0:T(8,128)S(1)} collective-permute-done((f32[2,32,512]{2,1,0:T(8,128)S(1)}, f32[2,32,512]{2,1,0:T(8,128)S(1)}, u32[]{:S(2)}, u32[]{:S(2)}) %collective-permute-start.9) | collective-permute-done | bytes 131104 | tf_op jit(solution)/shard_map/ppermute | solution.py:21
  72.5 2.9 %shard_map.106 = f32[32,8,2048]{2,1,0:T(8,128)} custom-call(f32[4,32,2048]{2,1,0:T(8,128)S(1)} %get-tuple-element.47.inner_ref, f32[4,32,2048]{2,1,0:T(8,128)S(1)} %get-tuple-element.48.swept_ref, f32[2,32,1536]{2,1,0:T(8,128)S(1)} %get-tuple-element.43.south_a_ref.own_south_a, f32[2,32,1536]{2,1,0:T(8,128)S(1)} %get-tuple-element.44.north_a_ref.own_north_a, ...), custom_call_target="tpu_custom_call" | custom-call | bytes 9000000 | tf_op jit(solution)/shard_map/pallas_call | solution.py:155
  (59 shorter events, 5.8 us)
Async XLA Ops:
  0.0 1.6 %copy-start = (f32[32,8,2048]{2,1,0:T(8,128)S(1)}, f32[32,8,2048]{2,1,0:T(8,128)}, u32[]{:S(2)}) copy-start(f32[32,8,2048]{2,1,0:T(8,128)} %x_ref.1) | copy-start | bytes 6291460
  4.4 15.6 %copy-start.19 = (f32[63]{0:T(128)S(1)}, f32[63]{0:T(128)}, u32[]{:S(2)}) copy-start(f32[63]{0:T(128)} %param.19) | copy-start | bytes 760
  4.4 16.0 %copy-start.20 = (f32[64]{0:T(128)S(1)}, f32[64]{0:T(128)}, u32[]{:S(2)}) copy-start(f32[64]{0:T(128)} %param.17) | copy-start | bytes 772
  4.4 16.1 %copy-start.18 = (f32[32]{0:T(128)S(1)}, f32[32]{0:T(128)}, u32[]{:S(2)}) copy-start(f32[32]{0:T(128)} %param.18) | copy-start | bytes 388
  8.7 23.1 %collective-permute-start.4 = (f32[2,32,1792]{2,1,0:T(8,128)}, f32[2,32,1792]{2,1,0:T(8,128)}, u32[]{:S(2)}, u32[]{:S(2)}) collective-permute-start(f32[2,32,1792]{2,1,0:T(8,128)} %get-tuple-element.29.north_ref.own_north_ref), channel_id=1, source_target_pairs={{0,1},{1,2},{2,3},{3,4},{4,5},{5,6},{6,7},{7,0},{8,9},{9,10},{10,1... | collective-permute-start | bytes 1376264 | tf_op jit(solution)/shard_map/ppermute | solution.py:21
  10.3 21.5 %collective-permute-start.5 = (f32[2,32,1792]{2,1,0:T(8,128)}, f32[2,32,1792]{2,1,0:T(8,128)}, u32[]{:S(2)}, u32[]{:S(2)}) collective-permute-start(f32[2,32,1792]{2,1,0:T(8,128)} %get-tuple-element.28.south_ref.own_south_ref), channel_id=1, source_target_pairs={{0,7},{1,0},{2,1},{3,2},{4,3},{5,4},{6,5},{7,6},{8,15},{9,8},{10,9... | collective-permute-start | bytes 1376264 | tf_op jit(solution)/shard_map/ppermute | solution.py:21
  12.9 18.9 %collective-permute-start.6 = (f32[16,2048]{1,0:T(8,128)}, f32[16,2048]{1,0:T(8,128)S(1)}, u32[]{:S(2)}, u32[]{:S(2)}) collective-permute-start(f32[16,2048]{1,0:T(8,128)} %get-tuple-element.38), channel_id=1, source_target_pairs={{0,7},{1,0},{2,1},{3,2},{4,3},{5,4},{6,5},{7,6},{8,15},{9,8},{10,9... | collective-permute-start | bytes 393224 | tf_op jit(solution)/shard_map/ppermute | solution.py:21
  14.6 31.4 %collective-permute-start = (f32[304,256]{1,0:T(8,128)}, f32[304,256]{1,0:T(8,128)}, u32[]{:S(2)}, u32[]{:S(2)}) collective-permute-start(f32[304,256]{1,0:T(8,128)} %get-tuple-element.33.xe_ref), channel_id=1, source_target_pairs={{0,8},{8,16},{16,24},{24,32},{32,40},{40,48},{48,56},{56,64},{64,7... | collective-permute-start | bytes 933896 | tf_op jit(solution)/shard_map/ppermute | solution.py:21
  14.6 31.4 %collective-permute-start.1 = (f32[304,256]{1,0:T(8,128)}, f32[304,256]{1,0:T(8,128)}, u32[]{:S(2)}, u32[]{:S(2)}) collective-permute-start(f32[304,256]{1,0:T(8,128)} %get-tuple-element.32.xw_ref), channel_id=1, source_target_pairs={{0,120},{8,0},{16,8},{24,16},{32,24},{40,32},{48,40},{56,48},{64,5... | collective-permute-start | bytes 933896 | tf_op jit(solution)/shard_map/ppermute | solution.py:21
  20.5 21.3 %copy-start.11 = (f32[4,128]{1,0:T(4,128)}, f32[4,128]{1,0:T(4,128)S(1)}, u32[]{:S(2)}) copy-start(f32[4,128]{1,0:T(4,128)S(1)} %maximum_maximum_fusion.par_ref) | copy-start | bytes 6148
  31.8 17.2 %copy-start.1 = (bf16[2,8,2,64,128]{4,3,2,1,0:T(8,128)(2,1)}, bf16[2,8,2,64,128]{4,3,2,1,0:T(8,128)(2,1)S(1)}, u32[]{:S(2)}) copy-start(bf16[2,8,2,64,128]{4,3,2,1,0:T(8,128)(2,1)S(1)} %get-tuple-element.39.table_ref) | copy-start | bytes 1572868
  31.8 0.8 %copy-start.6 = (f32[32,32]{1,0:T(8,128)S(1)}, f32[32,32]{1,0:T(8,128)}, u32[]{:S(2)}) copy-start(f32[32,32]{1,0:T(8,128)} %night_ref.5) | copy-start | bytes 12292
  41.8 15.5 %copy-start.7 = (f32[32,32]{1,0:T(8,128)S(1)}, f32[32,32]{1,0:T(8,128)}, u32[]{:S(2)}) copy-start(f32[32,32]{1,0:T(8,128)} %night_ref.5) | copy-start | bytes 12292
  41.8 15.5 %copy-start.10 = (f32[32,32]{1,0:T(8,128)S(1)}, f32[32,32]{1,0:T(8,128)}, u32[]{:S(2)}) copy-start(f32[32,32]{1,0:T(8,128)} %photo_ref.5) | copy-start | bytes 12292
  41.8 15.5 %copy-start.12 = (f32[4,128]{1,0:T(4,128)S(1)}, f32[4,128]{1,0:T(4,128)}, u32[]{:S(2)}) copy-start(f32[4,128]{1,0:T(4,128)} %copy-done.11) | copy-start | bytes 6148
  41.8 30.7 %collective-permute-start.7 = (f32[2,32,1536]{2,1,0:T(8,128)S(1)}, f32[2,32,1536]{2,1,0:T(8,128)}, u32[]{:S(2)}, u32[]{:S(2)}) collective-permute-start(f32[2,32,1536]{2,1,0:T(8,128)S(1)} %get-tuple-element.44.north_a_ref.own_north_a), channel_id=1, source_target_pairs={{0,1},{1,2},{2,3},{3,4},{4,5},{5,6},{6,7},{7,0},{8,9},{9,10},{10,1... | collective-permute-start | bytes 1179656 | tf_op jit(solution)/shard_map/ppermute | solution.py:21
  42.1 30.3 %collective-permute-start.8 = (f32[2,32,1536]{2,1,0:T(8,128)S(1)}, f32[2,32,1536]{2,1,0:T(8,128)}, u32[]{:S(2)}, u32[]{:S(2)}) collective-permute-start(f32[2,32,1536]{2,1,0:T(8,128)S(1)} %get-tuple-element.43.south_a_ref.own_south_a), channel_id=1, source_target_pairs={{0,7},{1,0},{2,1},{3,2},{4,3},{5,4},{6,5},{7,6},{8,15},{9,8},{10,9... | collective-permute-start | bytes 1179656 | tf_op jit(solution)/shard_map/ppermute | solution.py:21
  49.0 0.8 %copy-start.3 = (f32[8,32,512]{2,1,0:T(8,128)}, f32[8,32,512]{2,1,0:T(8,128)S(1)}, u32[]{:S(2)}) copy-start(f32[8,32,512]{2,1,0:T(8,128)S(1)} %get-tuple-element.34.mid_ref) | copy-start | bytes 1572868
  49.8 7.4 %collective-permute-start.3 = (f32[72,512]{1,0:T(8,128)}, f32[72,512]{1,0:T(8,128)S(1)}, u32[]{:S(2)}, u32[]{:S(2)}) collective-permute-start(f32[72,512]{1,0:T(8,128)} %get-tuple-element.36), channel_id=1, source_target_pairs={{0,7},{1,0},{2,1},{3,2},{4,3},{5,4},{6,5},{7,6},{8,15},{9,8},{10,9... | collective-permute-start | bytes 442376 | tf_op jit(solution)/shard_map/ppermute | solution.py:21
  49.9 7.4 %collective-permute-start.2 = (f32[64,512]{1,0:T(8,128)}, f32[64,512]{1,0:T(8,128)}, u32[]{:S(2)}, u32[]{:S(2)}) collective-permute-start(f32[64,512]{1,0:T(8,128)} %get-tuple-element.35), channel_id=1, source_target_pairs={{0,1},{1,2},{2,3},{3,4},{4,5},{5,6},{6,7},{7,0},{8,9},{9,10},{10,1... | collective-permute-start | bytes 393224 | tf_op jit(solution)/shard_map/ppermute | solution.py:21
  57.3 1.0 %copy-start.2 = (bf16[2,8,2,64,128]{4,3,2,1,0:T(8,128)(2,1)S(1)}, bf16[2,8,2,64,128]{4,3,2,1,0:T(8,128)(2,1)}, u32[]{:S(2)}) copy-start(bf16[2,8,2,64,128]{4,3,2,1,0:T(8,128)(2,1)} %copy-done.1) | copy-start | bytes 1572868
  58.3 1.0 %copy-start.4 = (f32[8,32,512]{2,1,0:T(8,128)S(1)}, f32[8,32,512]{2,1,0:T(8,128)}, u32[]{:S(2)}) copy-start(f32[8,32,512]{2,1,0:T(8,128)} %copy-done.3) | copy-start | bytes 1572868
  63.9 5.0 %collective-permute-start.10 = (f32[2,32,512]{2,1,0:T(8,128)S(1)}, f32[2,32,512]{2,1,0:T(8,128)S(1)}, u32[]{:S(2)}, u32[]{:S(2)}) collective-permute-start(f32[2,32,512]{2,1,0:T(8,128)S(1)} %get-tuple-element.45.south_c_ref.own_south_c), channel_id=1, source_target_pairs={{0,7},{1,0},{2,1},{3,2},{4,3},{5,4},{6,5},{7,6},{8,15},{9,8},{10,9... | collective-permute-start | bytes 393224 | tf_op jit(solution)/shard_map/ppermute | solution.py:21
  65.4 7.1 %collective-permute-start.9 = (f32[2,32,512]{2,1,0:T(8,128)S(1)}, f32[2,32,512]{2,1,0:T(8,128)S(1)}, u32[]{:S(2)}, u32[]{:S(2)}) collective-permute-start(f32[2,32,512]{2,1,0:T(8,128)S(1)} %get-tuple-element.46.north_c_ref.own_north_c), channel_id=1, source_target_pairs={{0,1},{1,2},{2,3},{3,4},{4,5},{5,6},{6,7},{7,0},{8,9},{9,10},{10,1... | collective-permute-start | bytes 393224 | tf_op jit(solution)/shard_map/ppermute | solution.py:21
  (8 other events, 5.6 us)

commit v2 on v1

--- a/solution.py
+++ b/solution.py
@@ -11,6 +11,7 @@
 HALF = 64
 LEVELS = 64
 VMEM_LIMIT = 24 * 1024 * 1024
+VMEM_ALL = 60 * 1024 * 1024
 F32 = jnp.float32
 BF16 = jnp.bfloat16
 LON_C, LON_G, LAT_C, LAT_G, DAY, COUNT = range(6)
@@ -77,8 +78,8 @@
     return jnp.where(low, left, right)
 
 
-def rate_pieces(night_ref, photo_ref):
-    rates = jnp.concatenate([night_ref[...], photo_ref[...]], 0)
+def rate_pieces(chem_ref, species):
+    rates = chem_ref[0 : 2 * species, 0:species]
     high = rates.astype(BF16)
     low = (rates - high.astype(F32)).astype(BF16)
     return jnp.concatenate([high, high, low], 1)
@@ -151,15 +152,15 @@
 BLOCK = 4 * PIECE
 
 
-def call(kernel, outs, ins, *args, scratch=(), out_specs=None, cost=10.0):
+def call(kernel, outs, ins, *args, scratch=(), out_specs=None, cost=10.0, limit=VMEM_LIMIT):
     return pl.pallas_call(
         kernel,
         out_shape=[s if isinstance(s, jax.ShapeDtypeStruct) else jax.ShapeDtypeStruct(s, F32) for s in outs],
         in_specs=ins,
         out_specs=out_specs or [WHOLE] * len(outs),
         scratch_shapes=list(scratch),
-        compiler_params=pltpu.CompilerParams(vmem_limit_bytes=VMEM_LIMIT),
-        cost_estimate=pl.CostEstimate(flops=0, bytes_accessed=int(cost * 3.0e6), transcendentals=0),
+        compiler_params=pltpu.CompilerParams(vmem_limit_bytes=limit),
+        cost_estimate=pl.CostEstimate(flops=int(cost * 1.0e9), bytes_accessed=int(cost * 3.0e6), transcendentals=0),
     )(*args)
 
 
@@ -192,23 +193,61 @@
     return jnp.concatenate([row] * (lanes // PIECE), 1)
 
 
+def fill_chem(night_ref, photo_ref, level_ref, loss_ref, mixing_ref, chem_ref):
+    species = night_ref.shape[0]
+    chem_ref[0:species, 0:species] = night_ref[...]
+    chem_ref[species : 2 * species, 0:species] = photo_ref[...]
+    square = (species, species)
+    own = lax.broadcasted_iota(jnp.int32, square, 0) == lax.broadcasted_iota(jnp.int32, square, 1)
+    loss = jnp.sum(jnp.where(own, loss_ref[...], 0.0), axis=1, keepdims=True)
+    chem_ref[2 * species : 3 * species] = jnp.broadcast_to(loss, (species, PIECE))
+    at = 3 * species
+    chem_ref[at : at + 8] = jnp.zeros((8, PIECE), F32)
+    for i, ref in enumerate((level_ref, mixing_ref)):
+        row = slice(at + i, at + i + 1)
+        chem_ref[row, 0 : ref.shape[1]] = ref[...]
+        low = lax.broadcasted_iota(jnp.int32, (1, PIECE), 1) < HALF
+        value = chem_ref[row]
+        chem_ref[row] = jnp.where(low, value, half_roll(value))
+    lat = lax.axis_index("lat")
+    for i, there in ((2, lat > 0), (3, lat < lax.axis_size("lat") - 1)):
+        chem_ref[at + i : at + i + 1] = jnp.where(there, 1.0, 0.0) * jnp.ones((1, PIECE), F32)
+
+
 def first_kernel(
-    x_ref, cour_in, sw_in, day_in, cnt_in,
-    xt_ref, south_ref, north_ref, west_ref, east_ref, coef_ref, row_ref,
-    cour_ref, sw_ref, day_ref, cnt_ref, row_sems, sems,
+    x_ref, cour_in, sw_in, day_in, cnt_in, night_in, photo_in, level_in, loss_in, mixing_in,
+    south_ref, north_ref, west_ref, east_ref, coef_ref, row_ref, chem_ref,
+    xt_ref, sides_ref, cour_ref, sw_ref, day_ref, cnt_ref, night_ref, photo_ref, level_ref, loss_ref, mixing_ref,
+    row_sems, sems,
 ):
     rows, species, width = xt_ref.shape
     pieces = width // PIECE
     edge = (0, 1, rows - 2, rows - 1)
     small = [
         pltpu.make_async_copy(a, b, sems.at[i])
-        for i, (a, b) in enumerate(((cour_in, cour_ref), (sw_in, sw_ref), (day_in, day_ref), (cnt_in, cnt_ref)))
+        for i, (a, b) in enumerate(
+            (
+                (cour_in, cour_ref),
+                (sw_in, sw_ref),
+                (day_in, day_ref),
+                (cnt_in, cnt_ref),
+                (night_in, night_ref),
+                (photo_in, photo_ref),
+                (level_in, level_ref),
+                (loss_in, loss_ref),
+                (mixing_in, mixing_ref),
+            )
+        )
     ]
-    big = [pltpu.make_async_copy(x_ref.at[:, r, :], xt_ref.at[r], row_sems.at[r]) for r in range(rows)]
+    big = {r: pltpu.make_async_copy(x_ref.at[:, r, :], xt_ref.at[r], row_sems.at[r]) for r in edge}
+    for j in (0, pieces - 2):
+        big[rows + j] = pltpu.make_async_copy(
+            x_ref.at[:, :, lanes_of(j, 2)], sides_ref.at[:, :, lanes_of(2 if j else 0, 2)], row_sems.at[4 + (1 if j else 0)]
+        )
     for copy in small:
         copy.start()
-    for r in edge + tuple(range(2, rows - 2)):
-        big[r].start()
+    for copy in big.values():
+        copy.start()
     for copy in small:
         copy.wait()
     cour = [cour_ref[0], cour_ref[1]]
@@ -224,6 +263,7 @@
     for i, field in enumerate(fields):
         for j in range(pieces):
             coef_ref[i, :, lanes_of(j)] = expand(field, 2 * j)
+    fill_chem(night_ref, photo_ref, level_ref, loss_ref, mixing_ref, chem_ref)
     row_ref[0:8] = coef_ref[LAT_C]
     row_ref[8:16] = coef_ref[LAT_G]
     for r in edge:
@@ -240,27 +280,33 @@
                 ref[row, block, lanes_of(j)] = value
 
     tiles(species, tile)
-    for r in range(2, rows - 2):
-        big[r].wait()
+    big[rows].wait()
+    big[rows + pieces - 2].wait()
     for ref, j in ((west_ref, 0), (east_ref, pieces - 2)):
         for r in range(rows):
-            ref[r * species : (r + 1) * species] = xt_ref[r, :, lanes_of(j, 2)]
+            ref[r * species : (r + 1) * species] = sides_ref[:, r, lanes_of(2 if j else 0, 2)]
         for i in range(6):
             at = rows * species + i * rows
             ref[at : at + rows] = coef_ref[i, :, lanes_of(j, 2)]
 
 
 def inner_kernel(
-    xt_ref, south_ref, north_ref, coef_ref, par_ref, loss_ref, night_ref, photo_ref, cnt_ref,
-    mid_ref, done_ref, table_ref,
+    x_ref, south_ref, north_ref, coef_ref, chem_ref, cnt_ref,
+    mid_ref, done_ref, table_ref, xt_ref, sems,
 ):
-    rows, species, width = xt_ref.shape
+    species, rows, width = x_ref.shape
     pieces = width // PIECE
     inner = range(2, rows - 2)
+    copies = [pltpu.make_async_copy(x_ref.at[:, r, :], xt_ref.at[r - 2], sems.at[r - 2]) for r in inner]
+    for copy in copies:
+        copy.start()
+    fill_table(chem_ref[3 * species + 1 : 3 * species + 2], table_ref)
+    for copy in copies:
+        copy.wait()
 
     def tile(block):
         for r in inner:
-            cells = [xt_ref[r, block, lanes_of(j)] for j in range(pieces)]
+            cells = [xt_ref[r - 2, block, lanes_of(j)] for j in range(pieces)]
             faces = [
                 [coef_ref[i, r : r + 1, lanes_of(j)] for j in range(1, pieces)] for i in (LON_C, LON_G)
             ]
@@ -268,8 +314,7 @@
                 mid_ref[r - 2, block, lanes_of(j)] = value
 
     tiles(species, tile)
-    fill_table(par_ref[1:2], table_ref)
-    rates = rate_pieces(night_ref, photo_ref)
+    rates = rate_pieces(chem_ref, species)
 
     def block(at, lanes):
         here = pl.ds(at, lanes)
@@ -286,8 +331,8 @@
             [coef_ref[DAY, r : r + 1, own] for r in inner],
             lambda i, j: cnt_ref[2 + i, column + j],
             rates,
-            loss_ref[...],
-            par_ref[0:1],
+            chem_ref[2 * species : 3 * species],
+            chem_ref[3 * species + 0 : 3 * species + 1],
             table_ref,
         )
         for i, row in enumerate(done):
@@ -297,7 +342,7 @@
 
 
 def side_kernel(
-    done_ref, xw_ref, xe_ref, hw_ref, he_ref, coef_ref, mid_ref, south_ref, north_ref, side_ref
+    edge_ref, xw_ref, xe_ref, hw_ref, he_ref, coef_ref, mid_ref, south_ref, north_ref, side_ref, cnt_ref
 ):
     rows, species = mid_ref.shape[:2]
     width = coef_ref.shape[2]
@@ -308,6 +353,8 @@
         side_ref[i, :, lanes_of(1)] = coef_ref[i, :, 0:PIECE]
         side_ref[i, :, lanes_of(2)] = coef_ref[i, :, width - PIECE : width]
         side_ref[i, :, lanes_of(3)] = he_ref[here, lanes_of(0)]
+
+    cnt_ref[...] = side_ref[COUNT].astype(jnp.int32)
 
     def tile(s, carry):
         for r in range(rows):
@@ -344,19 +391,19 @@
 
 def edge_kernel(
     mid_ref, own_south_ref, own_north_ref, south_ref, north_ref, coef_ref, row_ref,
-    par_ref, loss_ref, night_ref, photo_ref, table_ref, cnt_ref,
+    chem_ref, table_ref, cnt_ref,
     done_ref, sent_south_ref, sent_north_ref,
 ):
     species, inner_width = mid_ref.shape[1:]
     rows = coef_ref.shape[1]
-    rates = rate_pieces(night_ref, photo_ref)
+    rates = rate_pieces(chem_ref, species)
     edge = (0, 1, rows - 2, rows - 1)
 
     def block(at, lanes):
         here = pl.ds(at, lanes)
         own = pl.ds(at + PIECE if isinstance(at, int) else pl.multiple_of(at + PIECE, PIECE), lanes)
         column = 2 + at // LEVELS
-        valid_south, valid_north = wide(par_ref[2:3], lanes), wide(par_ref[3:4], lanes)
+        valid_south, valid_north = wide(chem_ref[3 * species + 2 : 3 * species + 3], lanes), wide(chem_ref[3 * species + 3 : 3 * species + 4], lanes)
         lower = (
             [south_ref[i, :, here] * valid_south for i in (0, 1)]
             + [own_south_ref[i, :, here] for i in (0, 1)]
@@ -384,8 +431,8 @@
             [coef_ref[DAY, r : r + 1, own] for r in edge],
             lambda i, j: cnt_ref[edge[i], column + j],
             rates,
-            loss_ref[...],
-            par_ref[0:1],
+            chem_ref[2 * species : 3 * species],
+            chem_ref[3 * species + 0 : 3 * species + 1],
             table_ref,
         )
         for i, row in enumerate(done):
@@ -409,12 +456,12 @@
 
 def corner_kernel(
     mid_ref, south_ref, north_ref, edge_ref, coef_ref, side_ref,
-    par_ref, loss_ref, night_ref, photo_ref, table_ref, cnt_ref,
+    chem_ref, table_ref, cnt_ref,
     done_ref, sent_south_ref, sent_north_ref,
 ):
     rows, species, width = mid_ref.shape
-    rates = rate_pieces(night_ref, photo_ref)
-    valid_south, valid_north = wide(par_ref[2:3], width), wide(par_ref[3:4], width)
+    rates = rate_pieces(chem_ref, species)
+    valid_south, valid_north = wide(chem_ref[3 * species + 2 : 3 * species + 3], width), wide(chem_ref[3 * species + 3 : 3 * species + 4], width)
     cells = (
         [south_ref[i * species : (i + 1) * species] * valid_south for i in (0, 1)]
         + [mid_ref[r] for r in range(rows)]
@@ -432,111 +479,145 @@
         done = column_block(
             [done_ref[part + i] for i in range(rows // 2)],
             [side_ref[DAY, part + i : part + i + 1] for i in range(rows // 2)],
-            lambda i, j: cnt_ref[part + i, j],
+            lambda i, j: cnt_ref[part + i, LEVELS * j],
             rates,
-            loss_ref[...],
-            par_ref[0:1],
+            chem_ref[2 * species : 3 * species],
+            chem_ref[3 * species + 0 : 3 * species + 1],
             table_ref,
         )
         for i, row in enumerate(done):
             done_ref[part + i] = jnp.concatenate(row, 1)
     last = edge_ref.shape[2] // PIECE
-    total = coef_ref.shape[2] // PIECE
 
     def tile(block):
         for k, r in enumerate((0, 1, rows - 2, rows - 1)):
             row = slice(r, r + 1)
             ref = sent_south_ref if k < 2 else sent_north_ref
-            cells = [done_ref[r, block, lanes_of(j)] for j in (0, 1)] + [
-                edge_ref[k, block, lanes_of(j)] for j in (0, 1)
-            ]
-            faces = [[coef_ref[i, row, lanes_of(j)] for j in range(3)] for i in (LON_C, LON_G)]
-            out = lon_sweep(cells, *faces)
-            cells = [edge_ref[k, block, lanes_of(j)] for j in (last - 2, last - 1)] + [
-                done_ref[r, block, lanes_of(j)] for j in (2, 3)
-            ]
-            faces = [
-                [coef_ref[i, row, lanes_of(j)] for j in (total - 2, total - 1)] + [side_ref[i, row, lanes_of(3)]]
-                for i in (LON_C, LON_G)
-            ]
-            for j, value in enumerate(out + lon_sweep(cells, *faces)):
+            out = corner_sweep(
+                [done_ref[r, block, lanes_of(j)] for j in range(4)],
+                [edge_ref[k, block, lanes_of(j)] for j in (0, 1, last - 2, last - 1)],
+                row,
+                coef_ref,
+                side_ref,
+            )
+            for j, value in enumerate(out):
                 ref[k % 2, block, lanes_of(j)] = value
 
     tiles(species, tile)
 
 
-def rest_kernel(
-    done_ref, corner_ref, south_a_ref, north_a_ref, south_c_ref, north_c_ref, coef_ref, side_ref, swept_ref, out_ref
-):
-    count, species = done_ref.shape[:2]
-    width = coef_ref.shape[2]
+def rest_kernel(done_ref, south_ref, north_ref, coef_ref, swept_ref, out_ref):
+    count, species, width = done_ref.shape
     pieces = width // PIECE
 
     def tile(block):
         for k in range(count):
             row = slice(k + 2, k + 3)
-            cells = (
-                [corner_ref[k + 2, block, lanes_of(j)] for j in (0, 1)]
-                + [done_ref[k, block, lanes_of(j)] for j in range(pieces - 2)]
-                + [corner_ref[k + 2, block, lanes_of(j)] for j in (2, 3)]
-            )
-            faces = [
-                [coef_ref[i, row, lanes_of(j)] for j in range(pieces)] + [side_ref[i, row, lanes_of(3)]]
-                for i in (LON_C, LON_G)
-            ]
+            cells = [done_ref[k, block, lanes_of(j)] for j in range(pieces)]
+            faces = [[coef_ref[i, row, lanes_of(j + 1)] for j in range(1, pieces)] for i in (LON_C, LON_G)]
             for j, value in enumerate(lon_sweep(cells, *faces)):
                 swept_ref[k, block, lanes_of(j)] = value
 
     tiles(species, tile)
-
+    for j in range(pieces - 2):
+        inner_lat(swept_ref, south_ref, north_ref, coef_ref, out_ref, j, j + 2)
+
+
+def inner_lat(swept_ref, south_ref, north_ref, coef_ref, out_ref, j, own):
+    count = swept_ref.shape[0]
+    at = lanes_of(j)
+    cells = (
+        [south_ref[i, :, at] for i in (0, 1)]
+        + [swept_ref[i, :, at] for i in range(count)]
+        + [north_ref[i, :, at] for i in (0, 1)]
+    )
+    faces = [[coef_ref[i, f : f + 1, lanes_of(own)] for f in range(2, count + 3)] for i in (LAT_C, LAT_G)]
+    for i, q in enumerate(lat_sweep(cells, *faces)):
+        out_ref[i, :, at] = q
+
+
+def rest_corner_kernel(done_ref, corner_ref, south_ref, north_ref, coef_ref, side_ref, swept_ref, out_ref):
+    count, species, width = done_ref.shape
+    last = width // PIECE
+    total = coef_ref.shape[2] // PIECE
+
+    def tile(block):
+        for k in range(count):
+            row = slice(k + 2, k + 3)
+            out = corner_sweep(
+                [corner_ref[k + 2, block, lanes_of(j)] for j in range(4)],
+                [done_ref[k, block, lanes_of(j)] for j in (0, 1, last - 2, last - 1)],
+                row,
+                coef_ref,
+                side_ref,
+            )
+            for j, value in enumerate(out):
+                swept_ref[k, block, lanes_of(j)] = value
+
+    tiles(species, tile)
+    for j, own in enumerate((0, 1, total - 2, total - 1)):
+        inner_lat(swept_ref, south_ref, north_ref, coef_ref, out_ref, j, own)
+
+
+def corner_sweep(corner, inner, row, coef_ref, side_ref):
+    total = coef_ref.shape[2] // PIECE
+    faces = [[coef_ref[i, row, lanes_of(j)] for j in range(3)] for i in (LON_C, LON_G)]
+    out = lon_sweep(corner[:2] + inner[:2], *faces)
+    faces = [
+        [coef_ref[i, row, lanes_of(j)] for j in (total - 2, total - 1)] + [side_ref[i, row, lanes_of(3)]]
+        for i in (LON_C, LON_G)
+    ]
+    return out + lon_sweep(inner[2:] + corner[2:], *faces)
+
+
+def join(j, pieces):
+    if 2 <= j < pieces - 2:
+        return False, lanes_of(j - 2)
+    return True, lanes_of(j if j < 2 else j - pieces + 4)
+
+
+def last_kernel(
+    inner_a, inner_c, swept_a, swept_c, own_south_a, own_north_a, own_south_c, own_north_c,
+    south_a, north_a, south_c, north_c, coef_ref, row_ref, chem_ref,
+    out_ref, edge_ref, sems,
+):
+    count, species, main = inner_a.shape
+    rows = count + 4
+    width = coef_ref.shape[2]
+    pieces = width // PIECE
+    edge = (0, 1, rows - 2, rows - 1)
+    two = 2 * PIECE
+    copies = []
+    for i in range(count):
+        for k, (source, at) in enumerate(
+            (
+                (inner_a.at[i], two),
+                (inner_c.at[i, :, 0:two], 0),
+                (inner_c.at[i, :, two : 2 * two], width - two),
+            )
+        ):
+            lanes = main if k == 0 else two
+            copies.append(
+                pltpu.make_async_copy(source, out_ref.at[:, i + 2, at : at + lanes], sems.at[3 * i + k])
+            )
+    for copy in copies:
+        copy.start()
+    valid_south, valid_north = chem_ref[3 * species + 2 : 3 * species + 3], chem_ref[3 * species + 3 : 3 * species + 4]
     for j in range(pieces):
         own = lanes_of(j)
-        (a, c), at = join(j, pieces)
-        south, north = ((south_c_ref, north_c_ref) if c else (south_a_ref, north_a_ref))
-        cells = (
-            [south[i, :, at] for i in (0, 1)]
-            + [swept_ref[i, :, own] for i in range(count)]
-            + [north[i, :, at] for i in (0, 1)]
-        )
-        faces = [[coef_ref[i, f : f + 1, own] for f in range(2, count + 3)] for i in (LAT_C, LAT_G)]
-        for i, q in enumerate(lat_sweep(cells, *faces)):
-            out_ref[i, :, own] = q
-
-
-def join(j, pieces):
-    if 2 <= j < pieces - 2:
-        return (True, False), lanes_of(j - 2)
-    return (False, True), lanes_of(j if j < 2 else j - pieces + 4)
-
-
-def last_kernel(
-    inner_ref, swept_ref, own_south_a, own_north_a, own_south_c, own_north_c,
-    south_a, north_a, south_c, north_c, coef_ref, row_ref, par_ref,
-    out_ref, edge_ref, sems,
-):
-    count, species, width = inner_ref.shape
-    rows = count + 4
-    pieces = width // PIECE
-    edge = (0, 1, rows - 2, rows - 1)
-    copies = [
-        pltpu.make_async_copy(inner_ref.at[i], out_ref.at[:, i + 2, :], sems.at[i]) for i in range(count)
-    ]
-    for copy in copies:
-        copy.start()
-    valid_south, valid_north = par_ref[2:3], par_ref[3:4]
-    for j in range(pieces):
-        own = lanes_of(j)
-        (_, c), at = join(j, pieces)
-        south, own_south, own_north, north = (
-            (south_c, own_south_c, own_north_c, north_c) if c else (south_a, own_south_a, own_north_a, north_a)
+        side, at = join(j, pieces)
+        south, own_south, own_north, north, swept_ref = (
+            (south_c, own_south_c, own_north_c, north_c, swept_c)
+            if side
+            else (south_a, own_south_a, own_north_a, north_a, swept_a)
         )
         lower = (
             [south[i, :, at] * valid_south for i in (0, 1)]
             + [own_south[i, :, at] for i in (0, 1)]
-            + [swept_ref[i, :, own] for i in (0, 1)]
+            + [swept_ref[i, :, at] for i in (0, 1)]
         )
         upper = (
-            [swept_ref[i, :, own] for i in (2, 3)]
+            [swept_ref[i, :, at] for i in (2, 3)]
             + [own_north[i, :, at] for i in (0, 1)]
             + [north[i, :, at] * valid_north for i in (0, 1)]
         )
@@ -555,7 +636,7 @@
         for k, q in enumerate(lat_sweep(lower, *lower_faces) + lat_sweep(upper, *upper_faces)):
             edge_ref[k, :, own] = q
     more = [
-        pltpu.make_async_copy(edge_ref.at[k], out_ref.at[:, r, :], sems.at[count + k]) for k, r in enumerate(edge)
+        pltpu.make_async_copy(edge_ref.at[k], out_ref.at[:, r, :], sems.at[3 * count + k]) for k, r in enumerate(edge)
     ]
     for copy in more:
         copy.start()
@@ -577,50 +658,47 @@
 ):
     species, rows, width = tracers.shape
     inner = width - 2 * PIECE
-    lat_count = lax.axis_size("lat")
-    lat = lax.axis_index("lat")
     two = 2 * PIECE
     four = 4 * PIECE
     message = (rows * species + 6 * rows, two)
 
-    xt, own_south, own_north, west, east, coef, own_row = call(
+    own_south, own_north, west, east, coef, own_row, chem = call(
         first_kernel,
-        [(rows, species, width), (2, species, inner), (2, species, inner), message, message, (6, rows, width), (16, width)],
-        [FAR] * 5,
+        [(2, species, inner), (2, species, inner), message, message, (6, rows, width), (16, width), (3 * species + 8, PIECE)],
+        [FAR] * 10,
         tracers,
         courant,
         switches,
         day_flags,
         diffusion_counts,
+        night_rates,
+        photo_rates,
+        level_light[None],
+        self_loss[None],
+        vertical_mixing[None],
         scratch=[
+            pltpu.VMEM((rows, species, width), F32),
+            pltpu.VMEM((species, rows, four), F32),
             pltpu.VMEM(courant.shape, F32),
             pltpu.VMEM(switches.shape, jnp.int32),
             pltpu.VMEM(day_flags.shape, jnp.int32),
             pltpu.VMEM(diffusion_counts.shape, jnp.int32),
+            pltpu.VMEM(night_rates.shape, F32),
+            pltpu.VMEM(photo_rates.shape, F32),
+            pltpu.VMEM((1,) + level_light.shape, F32),
+            pltpu.VMEM((1,) + self_loss.shape, F32),
+            pltpu.VMEM((1,) + vertical_mixing.shape, F32),
             pltpu.SemaphoreType.DMA((rows,)),
-            pltpu.SemaphoreType.DMA((4,)),
+            pltpu.SemaphoreType.DMA((9,)),
         ],
         cost=3,
+        limit=VMEM_ALL,
     )
     south = ring(own_north, "lat", 1)
     north = ring(own_south, "lat", -1)
     halo_west = ring(east, "lon", 1)
     halo_east = ring(west, "lon", -1)
     row = ring(own_row, "lat", -1)
-
-    edge = jnp.zeros((1,), F32)
-    mixing = jnp.concatenate([vertical_mixing, edge])
-    ones = jnp.ones((PIECE,), F32)
-    par = jnp.stack(
-        [
-            jnp.tile(level_light, 2),
-            jnp.tile(mixing, 2),
-            ones * (lat > 0).astype(F32),
-            ones * (lat < lat_count - 1).astype(F32),
-        ]
-    )
-    loss = jnp.broadcast_to(self_loss[:, None], (species, PIECE))
-    chem = (par, loss, night_rates, photo_rates)
 
     mid, done, table = call(
         inner_kernel,
@@ -629,34 +707,21 @@
             (rows - 4, species, inner),
             jax.ShapeDtypeStruct((2, KMAX, 2, HALF, PIECE), BF16),
         ],
-        [WHOLE] * 8 + [SCALARS],
-        xt,
+        [FAR] + [WHOLE] * 4 + [SCALARS],
+        tracers,
         own_south,
         own_north,
         coef,
-        *chem,
+        chem,
         diffusion_counts,
+        scratch=[pltpu.VMEM((rows - 4, species, width), F32), pltpu.SemaphoreType.DMA((rows - 4,))],
         cost=9,
-    )
-    mid_side, side_south, side_north, side = call(
-        side_kernel,
-        [(rows, species, four), (2 * species + 8, four), (2 * species, four), (6, rows, four)],
-        [pl.BlockSpec(memory_space=pl.ANY)] + [WHOLE] * 5,
-        done,
-        west,
-        east,
-        halo_west,
-        halo_east,
-        coef,
-        cost=3,
-    )
-    counts = side[COUNT][:, ::LEVELS].astype(jnp.int32)
-    side_from_south = ring(side_north, "lat", 1)
-    side_from_north = ring(side_south, "lat", -1)
+        limit=VMEM_ALL,
+    )
     edge_done, main_south, main_north = call(
         edge_kernel,
         [(4, species, inner), (2, species, inner - two), (2, species, inner - two)],
-        [WHOLE] * 12 + [SCALARS],
+        [WHOLE] * 9 + [SCALARS],
         mid,
         own_south,
         own_north,
@@ -664,50 +729,74 @@
         north,
         coef,
         row,
-        *chem,
+        chem,
         table,
         diffusion_counts,
         cost=9,
     )
     main_from_south = ring(main_north, "lat", 1)
     main_from_north = ring(main_south, "lat", -1)
+    mid_side, side_south, side_north, side, counts = call(
+        side_kernel,
+        [(rows, species, four), (2 * species + 8, four), (2 * species, four), (6, rows, four), jax.ShapeDtypeStruct((rows, four), jnp.int32)],
+        [FAR] + [WHOLE] * 5,
+        edge_done,
+        west,
+        east,
+        halo_west,
+        halo_east,
+        coef,
+        cost=3,
+    )
+    side_from_south = ring(side_north, "lat", 1)
+    side_from_north = ring(side_south, "lat", -1)
+    swept_main, main_out = call(
+        rest_kernel,
+        [(rows - 4, species, inner - two)] * 2,
+        [WHOLE] * 4,
+        done,
+        main_south,
+        main_north,
+        coef,
+        cost=3,
+    )
     corner, corner_south, corner_north = call(
         corner_kernel,
         [(rows, species, four), (2, species, four), (2, species, four)],
-        [WHOLE] * 11 + [SCALARS],
+        [WHOLE] * 8 + [SCALARS],
         mid_side,
         side_from_south,
         side_from_north,
         edge_done,
         coef,
         side,
-        *chem,
+        chem,
         table,
         counts,
         cost=5,
     )
     corner_from_south = ring(corner_north, "lat", 1)
     corner_from_north = ring(corner_south, "lat", -1)
-    swept, inner_out = call(
-        rest_kernel,
-        [(rows - 4, species, width), (rows - 4, species, width)],
-        [WHOLE] * 8,
+    swept_corner, corner_out = call(
+        rest_corner_kernel,
+        [(rows - 4, species, four)] * 2,
+        [WHOLE] * 6,
         done,
         corner,
-        main_south,
-        main_north,
         corner_south,
         corner_north,
         coef,
         side,
-        cost=4,
+        cost=2,
     )
     (out,) = call(
         last_kernel,
         [(species, rows, width)],
-        [WHOLE] * 13,
-        inner_out,
-        swept,
+        [WHOLE] * 15,
+        main_out,
+        corner_out,
+        swept_main,
+        swept_corner,
         main_south,
         main_north,
         corner_south,
@@ -718,8 +807,8 @@
         corner_from_north,
         coef,
         row,
-        par,
-        scratch=[pltpu.VMEM((4, species, width), F32), pltpu.SemaphoreType.DMA((rows,))],
+        chem,
+        scratch=[pltpu.VMEM((4, species, width), F32), pltpu.SemaphoreType.DMA((3 * rows,))],
         out_specs=[FAR],
         cost=3,
     )

time: 76.3 us -> 60.9 us (0.80)
  local copies, waits for them, and re-layouts: 11.3 us -> 2.24 us
  waiting for transfers between devices: 9.78 us -> 5.89 us
  Pallas kernels: 34.3 us -> 32.5 us
    unnamed x42 -> x20, local copies, waits for them, and re-layouts: 10.9 us -> 2.24 us
    ppermute x11, waiting for transfers between devices: 9.78 us -> 5.89 us  [ring(): lax.ppermute(value, axis, [(i, (i + steps) % count) for i in range(count)])]
    pallas_call x7 -> x8, Pallas kernels: 34.3 us -> 32.5 us  [call(): pl.pallas_call(kernel, out_shape=[s if isinstance(s, jax.ShapeDtypeStruct...]
  transfers between devices with their start and end apart: 11 -> 11, of which waited for: 3 -> 3; matrix products, arithmetic and copies ran while one was open for 1% -> 0% of each run, Pallas kernels for 36% -> 42%
where the time goes in v2:
time: 60.9 us; the launch traced here: 60.6 us
  Pallas kernels  32.5 us (53%)
  starting transfers between devices  19.6 us (32%)
  waiting for transfers between devices  5.89 us (10%)
  local copies, waits for them, and re-layouts  2.24 us (4%)
    pallas_call x8, Pallas kernels, call(): pl.pallas_call(kernel, out_shape=[s if isinstance(s, jax.ShapeDtypeStruct...  32.5 us
    ppermute x11, starting transfers between devices, ring(): lax.ppermute(value, axis, [(i, (i + steps) % count) for i in range(count)])  19.6 us
    ppermute x11, waiting for transfers between devices, ring(): lax.ppermute(value, axis, [(i, (i + steps) % count) for i in range(count)])  5.89 us
    unnamed x20, local copies, waits for them, and re-layouts  2.24 us
  transfers between devices with their start and end apart: 11, of which 3 were waited for; matrix products, arithmetic and copies ran while one was open for 0% of the time, Pallas kernels for 42%

profile of v2, /device:TPU:0, one launch (start us, length us, event | category | flops | bytes accessed | tf_op | source)
XLA Modules:
  0.0 60.6 jit_solution(10749005028386140830)
XLA Ops:
  0.0 4.1 %shard_map.100 = (f32[2,32,1792]{2,1,0:T(8,128)}, f32[2,32,1792]{2,1,0:T(8,128)}, f32[304,256]{1,0:T(8,128)}, f32[304,256]{1,0:T(8,128)}, f32[6,8,2048]{2,1,0:T(...) custom-call(f32[32,8,2048]{2,1,0:T(8,128)} %x_ref.3, f32[2,8,32]{2,1,0:T(8,128)} %cour_in.1, s32[2,8,32]{2,1,0:T(8,128)} %sw_in.1, ...), custom_call_target="tpu_custom_call" | custom-call | flops 3000000000 | bytes 9000000 | tf_op jit(solution)/shard_map/pallas_call | solution.py:156
  4.1 1.6 %collective-permute-start = (f32[2,32,1792]{2,1,0:T(8,128)}, f32[2,32,1792]{2,1,0:T(8,128)S(1)}, u32[]{:S(2)}, u32[]{:S(2)}) collective-permute-start(f32[2,32,1792]{2,1,0:T(8,128)} %get-tuple-element.31.north_ref.own_north_ref), channel_id=1, source_target_pairs={{0,1},{1,2},{2,3},{3,4},{4,5},{5,6},{6,7},{7,0},{8,9},{9,10},{10,1... | collective-permute-start | bytes 1376264 | tf_op jit(solution)/shard_map/ppermute | solution.py:22
  5.7 2.6 %collective-permute-start.1 = (f32[2,32,1792]{2,1,0:T(8,128)}, f32[2,32,1792]{2,1,0:T(8,128)S(1)}, u32[]{:S(2)}, u32[]{:S(2)}) collective-permute-start(f32[2,32,1792]{2,1,0:T(8,128)} %get-tuple-element.30.south_ref.own_south_ref), channel_id=1, source_target_pairs={{0,7},{1,0},{2,1},{3,2},{4,3},{5,4},{6,5},{7,6},{8,15},{9,8},{10,9... | collective-permute-start | bytes 1376264 | tf_op jit(solution)/shard_map/ppermute | solution.py:22
  8.3 1.7 %collective-permute-start.2 = (f32[16,2048]{1,0:T(8,128)}, f32[16,2048]{1,0:T(8,128)S(1)}, u32[]{:S(2)}, u32[]{:S(2)}) collective-permute-start(f32[16,2048]{1,0:T(8,128)} %get-tuple-element.36), channel_id=1, source_target_pairs={{0,7},{1,0},{2,1},{3,2},{4,3},{5,4},{6,5},{7,6},{8,15},{9,8},{10,9... | collective-permute-start | bytes 393224 | tf_op jit(solution)/shard_map/ppermute | solution.py:22
  10.0 0.0 collective-permute-start.3
  10.0 5.4 %collective-permute-start.4 = (f32[304,256]{1,0:T(8,128)}, f32[304,256]{1,0:T(8,128)S(1)}, u32[]{:S(2)}, u32[]{:S(2)}) collective-permute-start(f32[304,256]{1,0:T(8,128)} %get-tuple-element.42.xw_ref), channel_id=1, source_target_pairs={{0,120},{8,0},{16,8},{24,16},{32,24},{40,32},{48,40},{56,48},{64,5... | collective-permute-start | bytes 933896 | tf_op jit(solution)/shard_map/ppermute | solution.py:22
  15.4 10.8 %shard_map.101 = (f32[4,32,1792]{2,1,0:T(8,128)}, f32[4,32,1792]{2,1,0:T(8,128)}, bf16[2,8,2,64,128]{4,3,2,1,0:T(8,128)(2,1)}) custom-call(f32[32,8,2048]{2,1,0:T(8,128)} %x_ref.3, f32[2,32,1792]{2,1,0:T(8,128)} %get-tuple-element.30.south_ref.own_south_ref, f32[2,32,1792]{2,1,0:T(8,128)} %get-tuple-element.31.north_ref.own_north_ref, ...), custom_call_target="tpu_custom_call" | custom-call | flops 8999999488 | bytes 27000000 | tf_op jit(solution)/shard_map/pallas_call | solution.py:156
  26.3 1.0 %copy-done.8 = bf16[2,8,2,64,128]{4,3,2,1,0:T(8,128)(2,1)S(1)} copy-done((bf16[2,8,2,64,128]{4,3,2,1,0:T(8,128)(2,1)S(1)}, bf16[2,8,2,64,128]{4,3,2,1,0:T(8,128)(2,1)}, u32[]{:S(2)}) %copy-start.8) | copy-done | bytes 524312
  27.3 1.2 %copy-done.9 = f32[4,32,1792]{2,1,0:T(8,128)S(1)} copy-done((f32[4,32,1792]{2,1,0:T(8,128)S(1)}, f32[4,32,1792]{2,1,0:T(8,128)}, u32[]{:S(2)}) %copy-start.9) | copy-done | bytes 917528
  28.5 7.6 %shard_map.102 = (f32[4,32,1792]{2,1,0:T(8,128)S(1)}, f32[2,32,1536]{2,1,0:T(8,128)S(1)}, f32[2,32,1536]{2,1,0:T(8,128)S(1)}) custom-call(f32[4,32,1792]{2,1,0:T(8,128)S(1)} %copy-done.9, f32[2,32,1792]{2,1,0:T(8,128)S(1)} %copy-done, f32[2,32,1792]{2,1,0:T(8,128)S(1)} %copy-done.1, f32[2,32,1792]{2,1,0:T(8,128)S(1)} %collective-permute-done.south_ref, ...), custom_call_target="tpu_custom_call" | custom-call | flops 8999999488 | bytes 27000000 | tf_op jit(solution)/shard_map/pallas_call | solution.py:156
  36.2 1.1 %shard_map.104 = (f32[8,32,512]{2,1,0:T(8,128)S(1)}, f32[72,512]{1,0:T(8,128)S(1)}, f32[64,512]{1,0:T(8,128)S(1)}, f32[6,8,512]{2,1,0:T(8,128)S(1)}, s32[8,512]{1,0:T(8,128)S(1)}) custom-call(f32[4,32,1792]{2,1,0:T(8,128)S(1)} %get-tuple-element.41.edge_ref, f32[304,256]{1,0:T(8,128)S(1)} %copy-done.2, f32[304,256]{1,0:T(8,128)S(1)} %copy-done.3, ...), custom_call_target="tpu_custom_call" | custom-call | flops 3000000000 | bytes 9000000 | tf_op jit(solution)/shard_map/pallas_call | solution.py:156
  37.3 0.9 %collective-permute-start.6 = (f32[72,512]{1,0:T(8,128)S(1)}, f32[72,512]{1,0:T(8,128)S(1)}, u32[]{:S(2)}, u32[]{:S(2)}) collective-permute-start(f32[72,512]{1,0:T(8,128)S(1)} %get-tuple-element.46), channel_id=1, source_target_pairs={{0,7},{1,0},{2,1},{3,2},{4,3},{5,4},{6,5},{7,6},{8,15},{9,8},{10,9... | collective-permute-start | bytes 442376 | tf_op jit(solution)/shard_map/ppermute | solution.py:22
  38.2 1.2 %collective-permute-start.5 = (f32[64,512]{1,0:T(8,128)S(1)}, f32[64,512]{1,0:T(8,128)S(1)}, u32[]{:S(2)}, u32[]{:S(2)}) collective-permute-start(f32[64,512]{1,0:T(8,128)S(1)} %get-tuple-element.45), channel_id=1, source_target_pairs={{0,1},{1,2},{2,3},{3,4},{4,5},{5,6},{6,7},{7,0},{8,9},{9,10},{10,1... | collective-permute-start | bytes 393224 | tf_op jit(solution)/shard_map/ppermute | solution.py:22
  39.4 0.3 collective-permute-start.7
  39.6 3.9 %collective-permute-start.8 = (f32[2,32,1536]{2,1,0:T(8,128)S(1)}, f32[2,32,1536]{2,1,0:T(8,128)S(1)}, u32[]{:S(2)}, u32[]{:S(2)}) collective-permute-start(f32[2,32,1536]{2,1,0:T(8,128)S(1)} %get-tuple-element.38.south_ref.own_south_a), channel_id=1, source_target_pairs={{0,7},{1,0},{2,1},{3,2},{4,3},{5,4},{6,5},{7,6},{8,15},{9,8},{10,9... | collective-permute-start | bytes 1179656 | tf_op jit(solution)/shard_map/ppermute | solution.py:22
  43.5 1.5 %shard_map.103 = (f32[4,32,1536]{2,1,0:T(8,128)S(1)}, f32[4,32,1536]{2,1,0:T(8,128)S(1)}) custom-call(f32[4,32,1792]{2,1,0:T(8,128)S(1)} %copy-done.5, f32[2,32,1536]{2,1,0:T(8,128)S(1)} %get-tuple-element.38.south_ref.own_south_a, f32[2,32,1536]{2,1,0:T(8,128)S(1)} %get-tuple-element.39.north_ref.own_north_a, f32[6,8,2048]{2,1,0:T(8,128)S(1)} %copy-done.6), custom_call_target="tpu_custom_call" | custom-call | flops 3000000000 | bytes 9000000 | tf_op jit(solution)/shard_map/pallas_call | solution.py:156
  45.0 1.7 %collective-permute-done.5.south_ref = f32[64,512]{1,0:T(8,128)S(1)} collective-permute-done((f32[64,512]{1,0:T(8,128)S(1)}, f32[64,512]{1,0:T(8,128)S(1)}, u32[]{:S(2)}, u32[]{:S(2)}) %collective-permute-start.5) | collective-permute-done | bytes 131104 | tf_op jit(solution)/shard_map/ppermute | solution.py:22
  46.7 4.5 %shard_map.105 = (f32[8,32,512]{2,1,0:T(8,128)S(1)}, f32[2,32,512]{2,1,0:T(8,128)S(1)}, f32[2,32,512]{2,1,0:T(8,128)S(1)}) custom-call(f32[8,32,512]{2,1,0:T(8,128)S(1)} %get-tuple-element.44.mid_ref, f32[64,512]{1,0:T(8,128)S(1)} %collective-permute-done.5.south_ref, f32[72,512]{1,0:T(8,128)S(1)} %collective-permute-done.6.north_ref, ...), custom_call_target="tpu_custom_call" | custom-call | flops 5000000000 | bytes 15000000 | tf_op jit(solution)/shard_map/pallas_call | solution.py:156
  51.2 0.1 collective-permute-start.10
  51.4 1.9 %collective-permute-start.9 = (f32[2,32,512]{2,1,0:T(8,128)S(1)}, f32[2,32,512]{2,1,0:T(8,128)S(1)}, u32[]{:S(2)}, u32[]{:S(2)}) collective-permute-start(f32[2,32,512]{2,1,0:T(8,128)S(1)} %get-tuple-element.51.north_ref.own_north_c), channel_id=1, source_target_pairs={{0,1},{1,2},{2,3},{3,4},{4,5},{5,6},{6,7},{7,0},{8,9},{9,10},{10,1... | collective-permute-start | bytes 393224 | tf_op jit(solution)/shard_map/ppermute | solution.py:22
  53.3 1.0 %shard_map.106 = (f32[4,32,512]{2,1,0:T(8,128)S(1)}, f32[4,32,512]{2,1,0:T(8,128)S(1)}) custom-call(f32[4,32,1792]{2,1,0:T(8,128)S(1)} %copy-done.5, f32[8,32,512]{2,1,0:T(8,128)S(1)} %get-tuple-element.49.corner_ref, f32[2,32,512]{2,1,0:T(8,128)S(1)} %get-tuple-element.50.south_ref.own_south_c, f32[2,32,512]{2,1,0:T(8,128)S(1)} %get-tuple-element.51.north_ref.own_north_c, ...), custom_call_target="tpu_custom_call" | custom-call | flops 2000000000 | bytes 6000000 | tf_op jit(solution)/shard_map/pallas_call | solution.py:156
  54.3 2.0 %collective-permute-done.10.north_c = f32[2,32,512]{2,1,0:T(8,128)S(1)} collective-permute-done((f32[2,32,512]{2,1,0:T(8,128)S(1)}, f32[2,32,512]{2,1,0:T(8,128)S(1)}, u32[]{:S(2)}, u32[]{:S(2)}) %collective-permute-start.10) | collective-permute-done | bytes 131104 | tf_op jit(solution)/shard_map/ppermute | solution.py:22
  56.2 2.2 %collective-permute-done.9.south_c = f32[2,32,512]{2,1,0:T(8,128)S(1)} collective-permute-done((f32[2,32,512]{2,1,0:T(8,128)S(1)}, f32[2,32,512]{2,1,0:T(8,128)S(1)}, u32[]{:S(2)}, u32[]{:S(2)}) %collective-permute-start.9) | collective-permute-done | bytes 131104 | tf_op jit(solution)/shard_map/ppermute | solution.py:22
  58.4 2.0 %shard_map.107 = f32[32,8,2048]{2,1,0:T(8,128)} custom-call(f32[4,32,1536]{2,1,0:T(8,128)S(1)} %get-tuple-element.40.inner_a, f32[4,32,512]{2,1,0:T(8,128)S(1)} %get-tuple-element.52.inner_c, f32[4,32,1536]{2,1,0:T(8,128)S(1)} %get-tuple-element.53.swept_a, f32[4,32,512]{2,1,0:T(8,128)S(1)} %get-tuple-element.54.swept_c, ...), custom_call_target="tpu_custom_call" | custom-call | flops 3000000000 | bytes 9000000 | tf_op jit(solution)/shard_map/pallas_call | solution.py:156
  (26 shorter events, 0.1 us)
Async XLA Ops:
  4.1 22.1 %collective-permute-start = (f32[2,32,1792]{2,1,0:T(8,128)}, f32[2,32,1792]{2,1,0:T(8,128)S(1)}, u32[]{:S(2)}, u32[]{:S(2)}) collective-permute-start(f32[2,32,1792]{2,1,0:T(8,128)} %get-tuple-element.31.north_ref.own_north_ref), channel_id=1, source_target_pairs={{0,1},{1,2},{2,3},{3,4},{4,5},{5,6},{6,7},{7,0},{8,9},{9,10},{10,1... | collective-permute-start | bytes 1376264 | tf_op jit(solution)/shard_map/ppermute | solution.py:22
  5.7 20.5 %collective-permute-start.1 = (f32[2,32,1792]{2,1,0:T(8,128)}, f32[2,32,1792]{2,1,0:T(8,128)S(1)}, u32[]{:S(2)}, u32[]{:S(2)}) collective-permute-start(f32[2,32,1792]{2,1,0:T(8,128)} %get-tuple-element.30.south_ref.own_south_ref), channel_id=1, source_target_pairs={{0,7},{1,0},{2,1},{3,2},{4,3},{5,4},{6,5},{7,6},{8,15},{9,8},{10,9... | collective-permute-start | bytes 1376264 | tf_op jit(solution)/shard_map/ppermute | solution.py:22
  8.3 17.9 %collective-permute-start.2 = (f32[16,2048]{1,0:T(8,128)}, f32[16,2048]{1,0:T(8,128)S(1)}, u32[]{:S(2)}, u32[]{:S(2)}) collective-permute-start(f32[16,2048]{1,0:T(8,128)} %get-tuple-element.36), channel_id=1, source_target_pairs={{0,7},{1,0},{2,1},{3,2},{4,3},{5,4},{6,5},{7,6},{8,15},{9,8},{10,9... | collective-permute-start | bytes 393224 | tf_op jit(solution)/shard_map/ppermute | solution.py:22
  10.0 26.1 %collective-permute-start.3 = (f32[304,256]{1,0:T(8,128)}, f32[304,256]{1,0:T(8,128)S(1)}, u32[]{:S(2)}, u32[]{:S(2)}) collective-permute-start(f32[304,256]{1,0:T(8,128)} %get-tuple-element.43.xe_ref), channel_id=1, source_target_pairs={{0,8},{8,16},{16,24},{24,32},{32,40},{40,48},{48,56},{56,64},{64,7... | collective-permute-start | bytes 933896 | tf_op jit(solution)/shard_map/ppermute | solution.py:22
  10.0 26.1 %collective-permute-start.4 = (f32[304,256]{1,0:T(8,128)}, f32[304,256]{1,0:T(8,128)S(1)}, u32[]{:S(2)}, u32[]{:S(2)}) collective-permute-start(f32[304,256]{1,0:T(8,128)} %get-tuple-element.42.xw_ref), channel_id=1, source_target_pairs={{0,120},{8,0},{16,8},{24,16},{32,24},{40,32},{48,40},{56,48},{64,5... | collective-permute-start | bytes 933896 | tf_op jit(solution)/shard_map/ppermute | solution.py:22
  15.4 10.9 %copy-start = (f32[2,32,1792]{2,1,0:T(8,128)S(1)}, f32[2,32,1792]{2,1,0:T(8,128)}, u32[]{:S(2)}) copy-start(f32[2,32,1792]{2,1,0:T(8,128)} %get-tuple-element.30.south_ref.own_south_ref) | copy-start | bytes 1376260
  15.4 10.9 %copy-start.1 = (f32[2,32,1792]{2,1,0:T(8,128)S(1)}, f32[2,32,1792]{2,1,0:T(8,128)}, u32[]{:S(2)}) copy-start(f32[2,32,1792]{2,1,0:T(8,128)} %get-tuple-element.31.north_ref.own_north_ref) | copy-start | bytes 1376260
  15.4 10.9 %copy-start.4 = (s32[8,32]{1,0:T(8,128)S(1)}, s32[8,32]{1,0:T(8,128)}, u32[]{:S(2)}) copy-start(s32[8,32]{1,0:T(8,128)} %cnt_ref.3) | copy-start | bytes 3076
  15.4 10.9 %copy-start.6 = (f32[6,8,2048]{2,1,0:T(8,128)S(1)}, f32[6,8,2048]{2,1,0:T(8,128)}, u32[]{:S(2)}) copy-start(f32[6,8,2048]{2,1,0:T(8,128)} %get-tuple-element.32.coef_ref) | copy-start | bytes 1179652
  15.4 10.9 %copy-start.7 = (f32[104,128]{1,0:T(8,128)S(1)}, f32[104,128]{1,0:T(8,128)}, u32[]{:S(2)}) copy-start(f32[104,128]{1,0:T(8,128)} %get-tuple-element.33.chem_ref) | copy-start | bytes 159748
  26.3 1.0 %copy-start.8 = (bf16[2,8,2,64,128]{4,3,2,1,0:T(8,128)(2,1)S(1)}, bf16[2,8,2,64,128]{4,3,2,1,0:T(8,128)(2,1)}, u32[]{:S(2)}) copy-start(bf16[2,8,2,64,128]{4,3,2,1,0:T(8,128)(2,1)} %get-tuple-element.37.table_ref) | copy-start | bytes 1572868
  27.3 1.2 %copy-start.9 = (f32[4,32,1792]{2,1,0:T(8,128)S(1)}, f32[4,32,1792]{2,1,0:T(8,128)}, u32[]{:S(2)}) copy-start(f32[4,32,1792]{2,1,0:T(8,128)} %get-tuple-element.35.mid_ref) | copy-start | bytes 2752516
  28.5 7.6 %copy-start.2 = (f32[304,256]{1,0:T(8,128)S(1)}, f32[304,256]{1,0:T(8,128)}, u32[]{:S(2)}) copy-start(f32[304,256]{1,0:T(8,128)} %get-tuple-element.42.xw_ref) | copy-start | bytes 933892
  28.5 7.7 %copy-start.3 = (f32[304,256]{1,0:T(8,128)S(1)}, f32[304,256]{1,0:T(8,128)}, u32[]{:S(2)}) copy-start(f32[304,256]{1,0:T(8,128)} %get-tuple-element.43.xe_ref) | copy-start | bytes 933892
  36.2 7.3 %copy-start.5 = (f32[4,32,1792]{2,1,0:T(8,128)S(1)}, f32[4,32,1792]{2,1,0:T(8,128)}, u32[]{:S(2)}) copy-start(f32[4,32,1792]{2,1,0:T(8,128)} %get-tuple-element.34.done_ref) | copy-start | bytes 2752516
  37.3 9.4 %collective-permute-start.6 = (f32[72,512]{1,0:T(8,128)S(1)}, f32[72,512]{1,0:T(8,128)S(1)}, u32[]{:S(2)}, u32[]{:S(2)}) collective-permute-start(f32[72,512]{1,0:T(8,128)S(1)} %get-tuple-element.46), channel_id=1, source_target_pairs={{0,7},{1,0},{2,1},{3,2},{4,3},{5,4},{6,5},{7,6},{8,15},{9,8},{10,9... | collective-permute-start | bytes 442376 | tf_op jit(solution)/shard_map/ppermute | solution.py:22
  38.2 8.5 %collective-permute-start.5 = (f32[64,512]{1,0:T(8,128)S(1)}, f32[64,512]{1,0:T(8,128)S(1)}, u32[]{:S(2)}, u32[]{:S(2)}) collective-permute-start(f32[64,512]{1,0:T(8,128)S(1)} %get-tuple-element.45), channel_id=1, source_target_pairs={{0,1},{1,2},{2,3},{3,4},{4,5},{5,6},{6,7},{7,0},{8,9},{9,10},{10,1... | collective-permute-start | bytes 393224 | tf_op jit(solution)/shard_map/ppermute | solution.py:22
  39.4 19.1 %collective-permute-start.7 = (f32[2,32,1536]{2,1,0:T(8,128)S(1)}, f32[2,32,1536]{2,1,0:T(8,128)S(1)}, u32[]{:S(2)}, u32[]{:S(2)}) collective-permute-start(f32[2,32,1536]{2,1,0:T(8,128)S(1)} %get-tuple-element.39.north_ref.own_north_a), channel_id=1, source_target_pairs={{0,1},{1,2},{2,3},{3,4},{4,5},{5,6},{6,7},{7,0},{8,9},{9,10},{10,1... | collective-permute-start | bytes 1179656 | tf_op jit(solution)/shard_map/ppermute | solution.py:22
  39.6 18.8 %collective-permute-start.8 = (f32[2,32,1536]{2,1,0:T(8,128)S(1)}, f32[2,32,1536]{2,1,0:T(8,128)S(1)}, u32[]{:S(2)}, u32[]{:S(2)}) collective-permute-start(f32[2,32,1536]{2,1,0:T(8,128)S(1)} %get-tuple-element.38.south_ref.own_south_a), channel_id=1, source_target_pairs={{0,7},{1,0},{2,1},{3,2},{4,3},{5,4},{6,5},{7,6},{8,15},{9,8},{10,9... | collective-permute-start | bytes 1179656 | tf_op jit(solution)/shard_map/ppermute | solution.py:22
  51.2 5.0 %collective-permute-start.10 = (f32[2,32,512]{2,1,0:T(8,128)S(1)}, f32[2,32,512]{2,1,0:T(8,128)S(1)}, u32[]{:S(2)}, u32[]{:S(2)}) collective-permute-start(f32[2,32,512]{2,1,0:T(8,128)S(1)} %get-tuple-element.50.south_ref.own_south_c), channel_id=1, source_target_pairs={{0,7},{1,0},{2,1},{3,2},{4,3},{5,4},{6,5},{7,6},{8,15},{9,8},{10,9... | collective-permute-start | bytes 393224 | tf_op jit(solution)/shard_map/ppermute | solution.py:22
  51.4 7.1 %collective-permute-start.9 = (f32[2,32,512]{2,1,0:T(8,128)S(1)}, f32[2,32,512]{2,1,0:T(8,128)S(1)}, u32[]{:S(2)}, u32[]{:S(2)}) collective-permute-start(f32[2,32,512]{2,1,0:T(8,128)S(1)} %get-tuple-element.51.north_ref.own_north_c), channel_id=1, source_target_pairs={{0,1},{1,2},{2,3},{3,4},{4,5},{5,6},{6,7},{7,0},{8,9},{9,10},{10,1... | collective-permute-start | bytes 393224 | tf_op jit(solution)/shard_map/ppermute | solution.py:22

commit v3 on v2

--- a/solution.py
+++ b/solution.py
@@ -79,7 +79,9 @@
 
 
 def rate_pieces(chem_ref, species):
-    rates = chem_ref[0 : 2 * species, 0:species]
+    square = (2 * species, species)
+    own = lax.broadcasted_iota(jnp.int32, square, 0) == lax.broadcasted_iota(jnp.int32, square, 1)
+    rates = chem_ref[0 : 2 * species, 0:species] + jnp.where(own, 1.0, 0.0)
     high = rates.astype(BF16)
     low = (rates - high.astype(F32)).astype(BF16)
     return jnp.concatenate([high, high, low], 1)
@@ -95,11 +97,8 @@
             both = jnp.dot(
                 rates, jnp.concatenate([high, low, high], 0), preferred_element_type=F32
             )
-            top = q + both[:species] + sun * both[species:]
-            bottom = 1.0 + loss * q * q
-            inverse = pl.reciprocal(bottom, approx=True)
-            inverse = inverse * (2.0 - bottom * inverse)
-            nexts.append(top * inverse)
+            top = both[:species] + sun * both[species:]
+            nexts.append(top * pl.reciprocal(1.0 + loss * q * q, approx=True))
         rows = nexts
     return rows
 
@@ -214,10 +213,59 @@
         chem_ref[at + i : at + i + 1] = jnp.where(there, 1.0, 0.0) * jnp.ones((1, PIECE), F32)
 
 
+def face_fields(cour_ref, sw_ref, day_ref, cnt_ref):
+    cour = [cour_ref[0], cour_ref[1]]
+    switch = [sw_ref[0].astype(F32), sw_ref[1].astype(F32)]
+    return [
+        cour[0],
+        gain(cour[0], switch[0]),
+        cour[1],
+        gain(cour[1], switch[1]),
+        day_ref[...].astype(F32),
+        cnt_ref[...].astype(F32),
+    ]
+
+
+def start_kernel(
+    x_ref, cour_in, sw_in, day_in, cnt_in, west_ref, east_ref, sides_ref, cour_ref, sw_ref, day_ref, cnt_ref, sems
+):
+    species, rows, width = x_ref.shape
+    two = 2 * PIECE
+    copies = [
+        pltpu.make_async_copy(a, b, sems.at[i])
+        for i, (a, b) in enumerate(
+            (
+                (cour_in, cour_ref),
+                (sw_in, sw_ref),
+                (day_in, day_ref),
+                (cnt_in, cnt_ref),
+                (x_ref.at[:, :, 0:two], sides_ref.at[:, :, 0:two]),
+                (x_ref.at[:, :, width - two : width], sides_ref.at[:, :, two : 2 * two]),
+            )
+        )
+    ]
+    for copy in copies:
+        copy.start()
+    for copy in copies[:4]:
+        copy.wait()
+    fields = face_fields(cour_ref, sw_ref, day_ref, cnt_ref)
+    columns = cour_ref.shape[2]
+    for ref, first in ((west_ref, 0), (east_ref, columns - 4)):
+        for i, field in enumerate(fields):
+            at = rows * species + i * rows
+            for half in (0, 1):
+                ref[at : at + rows, lanes_of(half)] = expand(field, first + 2 * half)
+    for copy in copies[4:]:
+        copy.wait()
+    for j, ref in enumerate((west_ref, east_ref)):
+        for r in range(rows):
+            ref[r * species : (r + 1) * species] = sides_ref[:, r, lanes_of(2 * j, 2)]
+
+
 def first_kernel(
-    x_ref, cour_in, sw_in, day_in, cnt_in, night_in, photo_in, level_in, loss_in, mixing_in,
-    south_ref, north_ref, west_ref, east_ref, coef_ref, row_ref, chem_ref,
-    xt_ref, sides_ref, cour_ref, sw_ref, day_ref, cnt_ref, night_ref, photo_ref, level_ref, loss_ref, mixing_ref,
+    west_ref, x_ref, cour_in, sw_in, day_in, cnt_in, night_in, photo_in, level_in, loss_in, mixing_in,
+    south_ref, north_ref, coef_ref, row_ref, chem_ref,
+    xt_ref, cour_ref, sw_ref, day_ref, cnt_ref, night_ref, photo_ref, level_ref, loss_ref, mixing_ref,
     row_sems, sems,
 ):
     rows, species, width = xt_ref.shape
@@ -240,26 +288,13 @@
         )
     ]
     big = {r: pltpu.make_async_copy(x_ref.at[:, r, :], xt_ref.at[r], row_sems.at[r]) for r in edge}
-    for j in (0, pieces - 2):
-        big[rows + j] = pltpu.make_async_copy(
-            x_ref.at[:, :, lanes_of(j, 2)], sides_ref.at[:, :, lanes_of(2 if j else 0, 2)], row_sems.at[4 + (1 if j else 0)]
-        )
     for copy in small:
         copy.start()
     for copy in big.values():
         copy.start()
     for copy in small:
         copy.wait()
-    cour = [cour_ref[0], cour_ref[1]]
-    switch = [sw_ref[0].astype(F32), sw_ref[1].astype(F32)]
-    fields = [
-        cour[0],
-        gain(cour[0], switch[0]),
-        cour[1],
-        gain(cour[1], switch[1]),
-        day_ref[...].astype(F32),
-        cnt_ref[...].astype(F32),
-    ]
+    fields = face_fields(cour_ref, sw_ref, day_ref, cnt_ref)
     for i, field in enumerate(fields):
         for j in range(pieces):
             coef_ref[i, :, lanes_of(j)] = expand(field, 2 * j)
@@ -280,14 +315,6 @@
                 ref[row, block, lanes_of(j)] = value
 
     tiles(species, tile)
-    big[rows].wait()
-    big[rows + pieces - 2].wait()
-    for ref, j in ((west_ref, 0), (east_ref, pieces - 2)):
-        for r in range(rows):
-            ref[r * species : (r + 1) * species] = sides_ref[:, r, lanes_of(2 if j else 0, 2)]
-        for i in range(6):
-            at = rows * species + i * rows
-            ref[at : at + rows] = coef_ref[i, :, lanes_of(j, 2)]
 
 
 def inner_kernel(
@@ -342,7 +369,7 @@
 
 
 def side_kernel(
-    edge_ref, xw_ref, xe_ref, hw_ref, he_ref, coef_ref, mid_ref, south_ref, north_ref, side_ref, cnt_ref
+    done_ref, xw_ref, xe_ref, hw_ref, he_ref, coef_ref, mid_ref, south_ref, north_ref, side_ref, cnt_ref
 ):
     rows, species = mid_ref.shape[:2]
     width = coef_ref.shape[2]
@@ -390,7 +417,7 @@
 
 
 def edge_kernel(
-    mid_ref, own_south_ref, own_north_ref, south_ref, north_ref, coef_ref, row_ref,
+    side_ref, mid_ref, own_south_ref, own_north_ref, south_ref, north_ref, coef_ref, row_ref,
     chem_ref, table_ref, cnt_ref,
     done_ref, sent_south_ref, sent_north_ref,
 ):
@@ -506,7 +533,7 @@
     tiles(species, tile)
 
 
-def rest_kernel(done_ref, south_ref, north_ref, coef_ref, swept_ref, out_ref):
+def rest_kernel(corner_ref, done_ref, south_ref, north_ref, coef_ref, swept_ref, out_ref):
     count, species, width = done_ref.shape
     pieces = width // PIECE
 
@@ -570,77 +597,81 @@
     return out + lon_sweep(inner[2:] + corner[2:], *faces)
 
 
-def join(j, pieces):
-    if 2 <= j < pieces - 2:
-        return False, lanes_of(j - 2)
-    return True, lanes_of(j if j < 2 else j - pieces + 4)
+def edge_lat(swept, own_south, own_north, south, north, coef_ref, row_ref, chem_ref, out_ref, j, own):
+    count, species = swept.shape[:2]
+    rows = count + 4
+    at, lanes = lanes_of(j), lanes_of(own)
+    valid_south = chem_ref[3 * species + 2 : 3 * species + 3]
+    valid_north = chem_ref[3 * species + 3 : 3 * species + 4]
+    lower = (
+        [south[i, :, at] * valid_south for i in (0, 1)]
+        + [own_south[i, :, at] for i in (0, 1)]
+        + [swept[i, :, at] for i in (0, 1)]
+    )
+    upper = (
+        [swept[i, :, at] for i in (2, 3)]
+        + [own_north[i, :, at] for i in (0, 1)]
+        + [north[i, :, at] * valid_north for i in (0, 1)]
+    )
+    lower_faces = [
+        [coef_ref[i, 0:1, lanes] * valid_south, coef_ref[i, 1:2, lanes], coef_ref[i, 2:3, lanes]]
+        for i in (LAT_C, LAT_G)
+    ]
+    upper_faces = [
+        [
+            coef_ref[i, rows - 2 : rows - 1, lanes],
+            coef_ref[i, rows - 1 : rows, lanes],
+            row_ref[8 * (i - LAT_C) : 8 * (i - LAT_C) + 1, lanes] * valid_north,
+        ]
+        for i in (LAT_C, LAT_G)
+    ]
+    for k, q in enumerate(lat_sweep(lower, *lower_faces) + lat_sweep(upper, *upper_faces)):
+        out_ref[k, :, at] = q
+
+
+def edge_last_kernel(
+    inner_c, swept, own_south, own_north, south, north, coef_ref, row_ref, chem_ref, out_ref
+):
+    for j in range(swept.shape[2] // PIECE):
+        edge_lat(swept, own_south, own_north, south, north, coef_ref, row_ref, chem_ref, out_ref, j, j + 2)
 
 
 def last_kernel(
-    inner_a, inner_c, swept_a, swept_c, own_south_a, own_north_a, own_south_c, own_north_c,
-    south_a, north_a, south_c, north_c, coef_ref, row_ref, chem_ref,
-    out_ref, edge_ref, sems,
+    inner_a, inner_c, edge_a, swept, own_south, own_north, south, north, coef_ref, row_ref, chem_ref,
+    out_ref, edge_c, sems,
 ):
     count, species, main = inner_a.shape
+    width = coef_ref.shape[2]
     rows = count + 4
-    width = coef_ref.shape[2]
     pieces = width // PIECE
+    two = 2 * PIECE
+
+    def copies(array, row, source, first):
+        return [
+            pltpu.make_async_copy(array.at[source, :, 0:two], out_ref.at[:, row, 0:two], sems.at[first]),
+            pltpu.make_async_copy(
+                array.at[source, :, two : 2 * two], out_ref.at[:, row, width - two : width], sems.at[first + 1]
+            ),
+        ]
+
+    started = []
     edge = (0, 1, rows - 2, rows - 1)
-    two = 2 * PIECE
-    copies = []
     for i in range(count):
-        for k, (source, at) in enumerate(
-            (
-                (inner_a.at[i], two),
-                (inner_c.at[i, :, 0:two], 0),
-                (inner_c.at[i, :, two : 2 * two], width - two),
-            )
-        ):
-            lanes = main if k == 0 else two
-            copies.append(
-                pltpu.make_async_copy(source, out_ref.at[:, i + 2, at : at + lanes], sems.at[3 * i + k])
-            )
-    for copy in copies:
+        started.append(pltpu.make_async_copy(inner_a.at[i], out_ref.at[:, i + 2, two : two + main], sems.at[i]))
+        started.append(
+            pltpu.make_async_copy(edge_a.at[i], out_ref.at[:, edge[i], two : two + main], sems.at[count + i])
+        )
+        started += copies(inner_c, i + 2, i, 2 * count + 2 * i)
+    for copy in started:
         copy.start()
-    valid_south, valid_north = chem_ref[3 * species + 2 : 3 * species + 3], chem_ref[3 * species + 3 : 3 * species + 4]
-    for j in range(pieces):
-        own = lanes_of(j)
-        side, at = join(j, pieces)
-        south, own_south, own_north, north, swept_ref = (
-            (south_c, own_south_c, own_north_c, north_c, swept_c)
-            if side
-            else (south_a, own_south_a, own_north_a, north_a, swept_a)
-        )
-        lower = (
-            [south[i, :, at] * valid_south for i in (0, 1)]
-            + [own_south[i, :, at] for i in (0, 1)]
-            + [swept_ref[i, :, at] for i in (0, 1)]
-        )
-        upper = (
-            [swept_ref[i, :, at] for i in (2, 3)]
-            + [own_north[i, :, at] for i in (0, 1)]
-            + [north[i, :, at] * valid_north for i in (0, 1)]
-        )
-        lower_faces = [
-            [coef_ref[i, 0:1, own] * valid_south, coef_ref[i, 1:2, own], coef_ref[i, 2:3, own]]
-            for i in (LAT_C, LAT_G)
-        ]
-        upper_faces = [
-            [
-                coef_ref[i, rows - 2 : rows - 1, own],
-                coef_ref[i, rows - 1 : rows, own],
-                row_ref[8 * (i - LAT_C) : 8 * (i - LAT_C) + 1, own] * valid_north,
-            ]
-            for i in (LAT_C, LAT_G)
-        ]
-        for k, q in enumerate(lat_sweep(lower, *lower_faces) + lat_sweep(upper, *upper_faces)):
-            edge_ref[k, :, own] = q
-    more = [
-        pltpu.make_async_copy(edge_ref.at[k], out_ref.at[:, r, :], sems.at[3 * count + k]) for k, r in enumerate(edge)
-    ]
+    for j, own in enumerate((0, 1, pieces - 2, pieces - 1)):
+        edge_lat(swept, own_south, own_north, south, north, coef_ref, row_ref, chem_ref, edge_c, j, own)
+    more = []
+    for k, r in enumerate(edge):
+        more += copies(edge_c, r, k, 4 * count + 2 * k)
     for copy in more:
         copy.start()
-    for copy in copies + more:
+    for copy in started + more:
         copy.wait()
 
 
@@ -662,10 +693,32 @@
     four = 4 * PIECE
     message = (rows * species + 6 * rows, two)
 
-    own_south, own_north, west, east, coef, own_row, chem = call(
+    columns = [
+        pltpu.VMEM(courant.shape, F32),
+        pltpu.VMEM(switches.shape, jnp.int32),
+        pltpu.VMEM(day_flags.shape, jnp.int32),
+        pltpu.VMEM(diffusion_counts.shape, jnp.int32),
+    ]
+    west, east = call(
+        start_kernel,
+        [message, message],
+        [FAR] * 5,
+        tracers,
+        courant,
+        switches,
+        day_flags,
+        diffusion_counts,
+        scratch=[pltpu.VMEM((species, rows, four), F32)] + columns + [pltpu.SemaphoreType.DMA((6,))],
+        cost=2,
+        limit=VMEM_ALL,
+    )
+    halo_west = ring(east, "lon", 1)
+    halo_east = ring(west, "lon", -1)
+    own_south, own_north, coef, own_row, chem = call(
         first_kernel,
-        [(2, species, inner), (2, species, inner), message, message, (6, rows, width), (16, width), (3 * species + 8, PIECE)],
-        [FAR] * 10,
+        [(2, species, inner), (2, species, inner), (6, rows, width), (16, width), (3 * species + 8, PIECE)],
+        [FAR] * 11,
+        west,
         tracers,
         courant,
         switches,
@@ -678,11 +731,7 @@
         vertical_mixing[None],
         scratch=[
             pltpu.VMEM((rows, species, width), F32),
-            pltpu.VMEM((species, rows, four), F32),
-            pltpu.VMEM(courant.shape, F32),
-            pltpu.VMEM(switches.shape, jnp.int32),
-            pltpu.VMEM(day_flags.shape, jnp.int32),
-            pltpu.VMEM(diffusion_counts.shape, jnp.int32),
+            *columns,
             pltpu.VMEM(night_rates.shape, F32),
             pltpu.VMEM(photo_rates.shape, F32),
             pltpu.VMEM((1,) + level_light.shape, F32),
@@ -696,8 +745,6 @@
     )
     south = ring(own_north, "lat", 1)
     north = ring(own_south, "lat", -1)
-    halo_west = ring(east, "lon", 1)
-    halo_east = ring(west, "lon", -1)
     row = ring(own_row, "lat", -1)
 
     mid, done, table = call(
@@ -718,10 +765,25 @@
         cost=9,
         limit=VMEM_ALL,
     )
+    mid_side, side_south, side_north, side, counts = call(
+        side_kernel,
+        [(rows, species, four), (2 * species + 8, four), (2 * species, four), (6, rows, four), jax.ShapeDtypeStruct((rows, four), jnp.int32)],
+        [FAR] + [WHOLE] * 5,
+        done,
+        west,
+        east,
+        halo_west,
+        halo_east,
+        coef,
+        cost=3,
+    )
+    side_from_south = ring(side_north, "lat", 1)
+    side_from_north = ring(side_south, "lat", -1)
     edge_done, main_south, main_north = call(
         edge_kernel,
         [(4, species, inner), (2, species, inner - two), (2, species, inner - two)],
-        [WHOLE] * 9 + [SCALARS],
+        [FAR] + [WHOLE] * 9 + [SCALARS],
+        side,
         mid,
         own_south,
         own_north,
@@ -736,30 +798,6 @@
     )
     main_from_south = ring(main_north, "lat", 1)
     main_from_north = ring(main_south, "lat", -1)
-    mid_side, side_south, side_north, side, counts = call(
-        side_kernel,
-        [(rows, species, four), (2 * species + 8, four), (2 * species, four), (6, rows, four), jax.ShapeDtypeStruct((rows, four), jnp.int32)],
-        [FAR] + [WHOLE] * 5,
-        edge_done,
-        west,
-        east,
-        halo_west,
-        halo_east,
-        coef,
-        cost=3,
-    )
-    side_from_south = ring(side_north, "lat", 1)
-    side_from_north = ring(side_south, "lat", -1)
-    swept_main, main_out = call(
-        rest_kernel,
-        [(rows - 4, species, inner - two)] * 2,
-        [WHOLE] * 4,
-        done,
-        main_south,
-        main_north,
-        coef,
-        cost=3,
-    )
     corner, corner_south, corner_north = call(
         corner_kernel,
         [(rows, species, four), (2, species, four), (2, species, four)],
@@ -777,6 +815,17 @@
     )
     corner_from_south = ring(corner_north, "lat", 1)
     corner_from_north = ring(corner_south, "lat", -1)
+    swept_main, main_out = call(
+        rest_kernel,
+        [(rows - 4, species, inner - two)] * 2,
+        [FAR] + [WHOLE] * 4,
+        corner_south,
+        done,
+        main_south,
+        main_north,
+        coef,
+        cost=0.1,
+    )
     swept_corner, corner_out = call(
         rest_corner_kernel,
         [(rows - 4, species, four)] * 2,
@@ -787,28 +836,39 @@
         corner_north,
         coef,
         side,
-        cost=2,
+        cost=0.1,
+    )
+    (edge_out,) = call(
+        edge_last_kernel,
+        [(4, species, inner - two)],
+        [FAR] + [WHOLE] * 8,
+        corner_out,
+        swept_main,
+        main_south,
+        main_north,
+        main_from_south,
+        main_from_north,
+        coef,
+        row,
+        chem,
+        cost=0.5,
     )
     (out,) = call(
         last_kernel,
         [(species, rows, width)],
-        [WHOLE] * 15,
+        [WHOLE] * 11,
         main_out,
         corner_out,
-        swept_main,
+        edge_out,
         swept_corner,
-        main_south,
-        main_north,
         corner_south,
         corner_north,
-        main_from_south,
-        main_from_north,
         corner_from_south,
         corner_from_north,
         coef,
         row,
         chem,
-        scratch=[pltpu.VMEM((4, species, width), F32), pltpu.SemaphoreType.DMA((3 * rows,))],
+        scratch=[pltpu.VMEM((4, species, four), F32), pltpu.SemaphoreType.DMA((3 * rows,))],
         out_specs=[FAR],
         cost=3,
     )

time: 60.9 us -> 58.5 us (0.961)
  the two profiles are of different devices: /device:TPU:0 before, /device:TPU:6 now
where the time goes in v3:
time: 58.5 us; the launch traced here: 58.3 us
  Pallas kernels  34.1 us (58%)
  starting transfers between devices  19.7 us (34%)
  waiting for transfers between devices  3.1 us (5%)
  local copies, waits for them, and re-layouts  1.21 us (2%)
    pallas_call x10, Pallas kernels, call(): pl.pallas_call(kernel, out_shape=[s if isinstance(s, jax.ShapeDtypeStruct...  34.1 us
    ppermute x11, starting transfers between devices, ring(): lax.ppermute(value, axis, [(i, (i + steps) % count) for i in range(count)])  19.7 us
    ppermute x11, waiting for transfers between devices, ring(): lax.ppermute(value, axis, [(i, (i + steps) % count) for i in range(count)])  3.1 us
    unnamed x22, local copies, waits for them, and re-layouts  1.21 us
  transfers between devices with their start and end apart: 11, of which 1 were waited for; matrix products, arithmetic and copies ran while one was open for 0% of the time, Pallas kernels for 52%

profile of v3, /device:TPU:6, one launch (start us, length us, event | category | flops | bytes accessed | tf_op | source)
XLA Modules:
  0.0 58.3 jit_solution(8953642925592234327)
XLA Ops:
  0.0 2.1 %shard_map.100 = (f32[304,256]{1,0:T(8,128)}, f32[304,256]{1,0:T(8,128)}) custom-call(f32[32,8,2048]{2,1,0:T(8,128)} %x_ref.5, f32[2,8,32]{2,1,0:T(8,128)} %cour_in.3, s32[2,8,32]{2,1,0:T(8,128)} %sw_in.3, s32[8,32]{1,0:T(8,128)} %day_in.3, s32[8,32]{1,0:T(8,128)} %cnt_ref.3), custom_call_target="tpu_custom_call" | custom-call | flops 2000000000 | bytes 6000000 | tf_op jit(solution)/shard_map/pallas_call | solution.py:155
  2.1 0.1 collective-permute-start
  2.2 6.2 %collective-permute-start.1 = (f32[304,256]{1,0:T(8,128)}, f32[304,256]{1,0:T(8,128)S(1)}, u32[]{:S(2)}, u32[]{:S(2)}) collective-permute-start(f32[304,256]{1,0:T(8,128)} %get-tuple-element.30.west_ref.xw_ref), channel_id=1, source_target_pairs={{0,120},{8,0},{16,8},{24,16},{32,24},{40,32},{48,40},{56,48},{64,5... | collective-permute-start | bytes 933896 | tf_op jit(solution)/shard_map/ppermute | solution.py:22
  8.4 3.7 %shard_map.101 = (f32[2,32,1792]{2,1,0:T(8,128)}, f32[2,32,1792]{2,1,0:T(8,128)}, f32[6,8,2048]{2,1,0:T(8,128)}, f32[16,2048]{1,0:T(8,128)}, f32[104,128]{1,0:T(8,128)}) custom-call(f32[304,256]{1,0:T(8,128)} %get-tuple-element.30.west_ref.xw_ref, f32[32,8,2048]{2,1,0:T(8,128)} %x_ref.5, f32[2,8,32]{2,1,0:T(8,128)} %cour_in.3, s32[2,8,32]{2,1,0:T(8,128)} %sw_in.3, ...), custom_call_target="tpu_custom_call" | custom-call | flops 3000000000 | bytes 9000000 | tf_op jit(solution)/shard_map/pallas_call | solution.py:155
  12.1 0.9 %collective-permute-start.6 = (f32[16,2048]{1,0:T(8,128)}, f32[16,2048]{1,0:T(8,128)S(1)}, u32[]{:S(2)}, u32[]{:S(2)}) collective-permute-start(f32[16,2048]{1,0:T(8,128)} %get-tuple-element.42), channel_id=1, source_target_pairs={{0,7},{1,0},{2,1},{3,2},{4,3},{5,4},{6,5},{7,6},{8,15},{9,8},{10,9... | collective-permute-start | bytes 393224 | tf_op jit(solution)/shard_map/ppermute | solution.py:22
  13.0 0.5 collective-permute-start.5
  13.5 3.6 %collective-permute-start.4 = (f32[2,32,1792]{2,1,0:T(8,128)}, f32[2,32,1792]{2,1,0:T(8,128)S(1)}, u32[]{:S(2)}, u32[]{:S(2)}) collective-permute-start(f32[2,32,1792]{2,1,0:T(8,128)} %get-tuple-element.32.north_ref.own_north_ref), channel_id=1, source_target_pairs={{0,1},{1,2},{2,3},{3,4},{4,5},{5,6},{6,7},{7,0},{8,9},{9,10},{10,1... | collective-permute-start | bytes 1376264 | tf_op jit(solution)/shard_map/ppermute | solution.py:22
  17.1 10.7 %shard_map.102 = (f32[4,32,1792]{2,1,0:T(8,128)}, f32[4,32,1792]{2,1,0:T(8,128)}, bf16[2,8,2,64,128]{4,3,2,1,0:T(8,128)(2,1)}) custom-call(f32[32,8,2048]{2,1,0:T(8,128)} %x_ref.5, f32[2,32,1792]{2,1,0:T(8,128)} %get-tuple-element.31.south_ref.own_south_ref, f32[2,32,1792]{2,1,0:T(8,128)} %get-tuple-element.32.north_ref.own_north_ref, ...), custom_call_target="tpu_custom_call" | custom-call | flops 8999999488 | bytes 27000000 | tf_op jit(solution)/shard_map/pallas_call | solution.py:155
  28.0 1.2 %copy-done = f32[4,32,1792]{2,1,0:T(8,128)S(1)} copy-done((f32[4,32,1792]{2,1,0:T(8,128)S(1)}, f32[4,32,1792]{2,1,0:T(8,128)}, u32[]{:S(2)}) %copy-start) | copy-done | bytes 917528
  29.2 0.0 copy-start.10
  29.2 1.1 %shard_map.103 = (f32[8,32,512]{2,1,0:T(8,128)S(1)}, f32[72,512]{1,0:T(8,128)S(1)}, f32[64,512]{1,0:T(8,128)S(1)}, f32[6,8,512]{2,1,0:T(8,128)S(1)}, s32[8,512]{1,0:T(8,128)S(1)}) custom-call(f32[4,32,1792]{2,1,0:T(8,128)S(1)} %copy-done, f32[304,256]{1,0:T(8,128)S(1)} %copy-done.6, f32[304,256]{1,0:T(8,128)S(1)} %copy-done.7, ...), custom_call_target="tpu_custom_call" | custom-call | flops 3000000000 | bytes 9000000 | tf_op jit(solution)/shard_map/pallas_call | solution.py:155
  30.3 1.2 %collective-permute-start.2 = (f32[64,512]{1,0:T(8,128)S(1)}, f32[64,512]{1,0:T(8,128)S(1)}, u32[]{:S(2)}, u32[]{:S(2)}) collective-permute-start(f32[64,512]{1,0:T(8,128)S(1)} %get-tuple-element.38), channel_id=1, source_target_pairs={{0,1},{1,2},{2,3},{3,4},{4,5},{5,6},{6,7},{7,0},{8,9},{9,10},{10,1... | collective-permute-start | bytes 393224 | tf_op jit(solution)/shard_map/ppermute | solution.py:22
  31.5 0.8 %collective-permute-start.3 = (f32[72,512]{1,0:T(8,128)S(1)}, f32[72,512]{1,0:T(8,128)S(1)}, u32[]{:S(2)}, u32[]{:S(2)}) collective-permute-start(f32[72,512]{1,0:T(8,128)S(1)} %get-tuple-element.39), channel_id=1, source_target_pairs={{0,7},{1,0},{2,1},{3,2},{4,3},{5,4},{6,5},{7,6},{8,15},{9,8},{10,9... | collective-permute-start | bytes 442376 | tf_op jit(solution)/shard_map/ppermute | solution.py:22
  32.4 7.4 %shard_map.104 = (f32[4,32,1792]{2,1,0:T(8,128)S(1)}, f32[2,32,1536]{2,1,0:T(8,128)S(1)}, f32[2,32,1536]{2,1,0:T(8,128)S(1)}) custom-call(f32[6,8,512]{2,1,0:T(8,128)S(1)} %get-tuple-element.40.side_ref, f32[4,32,1792]{2,1,0:T(8,128)S(1)} %copy-done.10, f32[2,32,1792]{2,1,0:T(8,128)S(1)} %copy-done.4, f32[2,32,1792]{2,1,0:T(8,128)S(1)} %copy-done.5, ...), custom_call_target="tpu_custom_call" | custom-call | flops 8999999488 | bytes 27000000 | tf_op jit(solution)/shard_map/pallas_call | solution.py:155
  39.9 0.1 collective-permute-start.8
  39.9 4.1 %collective-permute-start.7 = (f32[2,32,1536]{2,1,0:T(8,128)S(1)}, f32[2,32,1536]{2,1,0:T(8,128)S(1)}, u32[]{:S(2)}, u32[]{:S(2)}) collective-permute-start(f32[2,32,1536]{2,1,0:T(8,128)S(1)} %get-tuple-element.48.north_ref.own_north), channel_id=1, source_target_pairs={{0,1},{1,2},{2,3},{3,4},{4,5},{5,6},{6,7},{7,0},{8,9},{9,10},{10,1... | collective-permute-start | bytes 1179656 | tf_op jit(solution)/shard_map/ppermute | solution.py:22
  44.1 4.4 %shard_map.105 = (f32[8,32,512]{2,1,0:T(8,128)S(1)}, f32[2,32,512]{2,1,0:T(8,128)S(1)}, f32[2,32,512]{2,1,0:T(8,128)S(1)}) custom-call(f32[8,32,512]{2,1,0:T(8,128)S(1)} %get-tuple-element.37.mid_ref, f32[64,512]{1,0:T(8,128)S(1)} %collective-permute-done.2.south_ref, f32[72,512]{1,0:T(8,128)S(1)} %collective-permute-done.3.north_ref, ...), custom_call_target="tpu_custom_call" | custom-call | flops 5000000000 | bytes 15000000 | tf_op jit(solution)/shard_map/pallas_call | solution.py:155
  48.5 1.2 %collective-permute-start.9 = (f32[2,32,512]{2,1,0:T(8,128)S(1)}, f32[2,32,512]{2,1,0:T(8,128)S(1)}, u32[]{:S(2)}, u32[]{:S(2)}) collective-permute-start(f32[2,32,512]{2,1,0:T(8,128)S(1)} %get-tuple-element.51.north_ref.own_north), channel_id=1, source_target_pairs={{0,1},{1,2},{2,3},{3,4},{4,5},{5,6},{6,7},{7,0},{8,9},{9,10},{10,1... | collective-permute-start | bytes 393224 | tf_op jit(solution)/shard_map/ppermute | solution.py:22
  49.7 0.9 %collective-permute-start.10 = (f32[2,32,512]{2,1,0:T(8,128)S(1)}, f32[2,32,512]{2,1,0:T(8,128)S(1)}, u32[]{:S(2)}, u32[]{:S(2)}) collective-permute-start(f32[2,32,512]{2,1,0:T(8,128)S(1)} %get-tuple-element.46.corner_ref.south_ref.own_south), channel_id=1, source_target_pairs={{0,7},{1,0},{2,1},{3,2},{4,3},{5,4},{6,5},{7,6},{8,15},{9,8},{10,9... | collective-permute-start | bytes 393224 | tf_op jit(solution)/shard_map/ppermute | solution.py:22
  50.6 1.5 %shard_map.106 = (f32[4,32,1536]{2,1,0:T(8,128)S(1)}, f32[4,32,1536]{2,1,0:T(8,128)S(1)}) custom-call(f32[2,32,512]{2,1,0:T(8,128)S(1)} %get-tuple-element.46.corner_ref.south_ref.own_south, f32[4,32,1792]{2,1,0:T(8,128)S(1)} %copy-done.1, f32[2,32,1536]{2,1,0:T(8,128)S(1)} %get-tuple-element.47.south_ref.own_south, ...), custom_call_target="tpu_custom_call" | custom-call | flops 100000000 | bytes 300000 | tf_op jit(solution)/shard_map/pallas_call | solution.py:155
  52.1 1.0 %shard_map.107 = (f32[4,32,512]{2,1,0:T(8,128)S(1)}, f32[4,32,512]{2,1,0:T(8,128)S(1)}) custom-call(f32[4,32,1792]{2,1,0:T(8,128)S(1)} %copy-done.1, f32[8,32,512]{2,1,0:T(8,128)S(1)} %get-tuple-element.50.corner_ref, f32[2,32,512]{2,1,0:T(8,128)S(1)} %get-tuple-element.46.corner_ref.south_ref.own_south, ...), custom_call_target="tpu_custom_call" | custom-call | flops 100000000 | bytes 300000 | tf_op jit(solution)/shard_map/pallas_call | solution.py:155
  53.1 0.6 %shard_map.108.edge_a = f32[4,32,1536]{2,1,0:T(8,128)S(1)} custom-call(f32[4,32,512]{2,1,0:T(8,128)S(1)} %get-tuple-element.52.inner_c, f32[4,32,1536]{2,1,0:T(8,128)S(1)} %get-tuple-element.53.swept, f32[2,32,1536]{2,1,0:T(8,128)S(1)} %get-tuple-element.47.south_ref.own_south, f32[2,32,1536]{2,1,0:T(8,128)S(1)} %get-tuple-element.48.north_ref.own_north, ...), custom_call_target="tpu_custom_call" | custom-call | flops 500000000 | bytes 1500000 | tf_op jit(solution)/shard_map/pallas_call | solution.py:155
  53.7 3.1 %collective-permute-done.10.north = f32[2,32,512]{2,1,0:T(8,128)S(1)} collective-permute-done((f32[2,32,512]{2,1,0:T(8,128)S(1)}, f32[2,32,512]{2,1,0:T(8,128)S(1)}, u32[]{:S(2)}, u32[]{:S(2)}) %collective-permute-start.10) | collective-permute-done | bytes 131104 | tf_op jit(solution)/shard_map/ppermute | solution.py:22
  56.8 1.5 %shard_map.109 = f32[32,8,2048]{2,1,0:T(8,128)} custom-call(f32[4,32,1536]{2,1,0:T(8,128)S(1)} %get-tuple-element.49.inner_a, f32[4,32,512]{2,1,0:T(8,128)S(1)} %get-tuple-element.52.inner_c, f32[4,32,1536]{2,1,0:T(8,128)S(1)} %shard_map.108.edge_a, f32[4,32,512]{2,1,0:T(8,128)S(1)} %get-tuple-element.54.swept, ...), custom_call_target="tpu_custom_call" | custom-call | flops 3000000000 | bytes 9000000 | tf_op jit(solution)/shard_map/pallas_call | solution.py:155
  (30 shorter events, 0.1 us)
Async XLA Ops:
  2.1 25.8 %collective-permute-start = (f32[304,256]{1,0:T(8,128)}, f32[304,256]{1,0:T(8,128)S(1)}, u32[]{:S(2)}, u32[]{:S(2)}) collective-permute-start(f32[304,256]{1,0:T(8,128)} %get-tuple-element.36.xe_ref), channel_id=1, source_target_pairs={{0,8},{8,16},{16,24},{24,32},{32,40},{40,48},{48,56},{56,64},{64,7... | collective-permute-start | bytes 933896 | tf_op jit(solution)/shard_map/ppermute | solution.py:22
  2.2 25.7 %collective-permute-start.1 = (f32[304,256]{1,0:T(8,128)}, f32[304,256]{1,0:T(8,128)S(1)}, u32[]{:S(2)}, u32[]{:S(2)}) collective-permute-start(f32[304,256]{1,0:T(8,128)} %get-tuple-element.30.west_ref.xw_ref), channel_id=1, source_target_pairs={{0,120},{8,0},{16,8},{24,16},{32,24},{40,32},{48,40},{56,48},{64,5... | collective-permute-start | bytes 933896 | tf_op jit(solution)/shard_map/ppermute | solution.py:22
  12.1 20.2 %collective-permute-start.6 = (f32[16,2048]{1,0:T(8,128)}, f32[16,2048]{1,0:T(8,128)S(1)}, u32[]{:S(2)}, u32[]{:S(2)}) collective-permute-start(f32[16,2048]{1,0:T(8,128)} %get-tuple-element.42), channel_id=1, source_target_pairs={{0,7},{1,0},{2,1},{3,2},{4,3},{5,4},{6,5},{7,6},{8,15},{9,8},{10,9... | collective-permute-start | bytes 393224 | tf_op jit(solution)/shard_map/ppermute | solution.py:22
  13.0 19.4 %collective-permute-start.5 = (f32[2,32,1792]{2,1,0:T(8,128)}, f32[2,32,1792]{2,1,0:T(8,128)S(1)}, u32[]{:S(2)}, u32[]{:S(2)}) collective-permute-start(f32[2,32,1792]{2,1,0:T(8,128)} %get-tuple-element.31.south_ref.own_south_ref), channel_id=1, source_target_pairs={{0,7},{1,0},{2,1},{3,2},{4,3},{5,4},{6,5},{7,6},{8,15},{9,8},{10,9... | collective-permute-start | bytes 1376264 | tf_op jit(solution)/shard_map/ppermute | solution.py:22
  13.5 18.8 %collective-permute-start.4 = (f32[2,32,1792]{2,1,0:T(8,128)}, f32[2,32,1792]{2,1,0:T(8,128)S(1)}, u32[]{:S(2)}, u32[]{:S(2)}) collective-permute-start(f32[2,32,1792]{2,1,0:T(8,128)} %get-tuple-element.32.north_ref.own_north_ref), channel_id=1, source_target_pairs={{0,1},{1,2},{2,3},{3,4},{4,5},{5,6},{6,7},{7,0},{8,9},{9,10},{10,1... | collective-permute-start | bytes 1376264 | tf_op jit(solution)/shard_map/ppermute | solution.py:22
  17.1 10.8 %copy-start.2 = (f32[6,8,2048]{2,1,0:T(8,128)S(1)}, f32[6,8,2048]{2,1,0:T(8,128)}, u32[]{:S(2)}) copy-start(f32[6,8,2048]{2,1,0:T(8,128)} %get-tuple-element.33.coef_ref) | copy-start | bytes 1179652
  17.1 10.8 %copy-start.6 = (f32[304,256]{1,0:T(8,128)S(1)}, f32[304,256]{1,0:T(8,128)}, u32[]{:S(2)}) copy-start(f32[304,256]{1,0:T(8,128)} %get-tuple-element.30.west_ref.xw_ref) | copy-start | bytes 933892
  17.1 10.8 %copy-start.7 = (f32[304,256]{1,0:T(8,128)S(1)}, f32[304,256]{1,0:T(8,128)}, u32[]{:S(2)}) copy-start(f32[304,256]{1,0:T(8,128)} %get-tuple-element.36.xe_ref) | copy-start | bytes 933892
  28.0 1.2 %copy-start = (f32[4,32,1792]{2,1,0:T(8,128)S(1)}, f32[4,32,1792]{2,1,0:T(8,128)}, u32[]{:S(2)}) copy-start(f32[4,32,1792]{2,1,0:T(8,128)} %get-tuple-element.35.done_ref) | copy-start | bytes 2752516
  29.1 3.2 %copy-start.3 = (f32[104,128]{1,0:T(8,128)S(1)}, f32[104,128]{1,0:T(8,128)}, u32[]{:S(2)}) copy-start(f32[104,128]{1,0:T(8,128)} %get-tuple-element.34.chem_ref) | copy-start | bytes 159748
  29.1 3.2 %copy-start.4 = (f32[2,32,1792]{2,1,0:T(8,128)S(1)}, f32[2,32,1792]{2,1,0:T(8,128)}, u32[]{:S(2)}) copy-start(f32[2,32,1792]{2,1,0:T(8,128)} %get-tuple-element.31.south_ref.own_south_ref) | copy-start | bytes 1376260
  29.1 3.2 %copy-start.5 = (f32[2,32,1792]{2,1,0:T(8,128)S(1)}, f32[2,32,1792]{2,1,0:T(8,128)}, u32[]{:S(2)}) copy-start(f32[2,32,1792]{2,1,0:T(8,128)} %get-tuple-element.32.north_ref.own_north_ref) | copy-start | bytes 1376260
  29.1 3.3 %copy-start.8 = (s32[8,32]{1,0:T(8,128)S(1)}, s32[8,32]{1,0:T(8,128)}, u32[]{:S(2)}) copy-start(s32[8,32]{1,0:T(8,128)} %cnt_ref.3) | copy-start | bytes 3076
  29.1 3.3 %copy-start.9 = (bf16[2,8,2,64,128]{4,3,2,1,0:T(8,128)(2,1)S(1)}, bf16[2,8,2,64,128]{4,3,2,1,0:T(8,128)(2,1)}, u32[]{:S(2)}) copy-start(bf16[2,8,2,64,128]{4,3,2,1,0:T(8,128)(2,1)} %get-tuple-element.43.table_ref) | copy-start | bytes 1572868
  29.2 3.3 %copy-start.10 = (f32[4,32,1792]{2,1,0:T(8,128)S(1)}, f32[4,32,1792]{2,1,0:T(8,128)}, u32[]{:S(2)}) copy-start(f32[4,32,1792]{2,1,0:T(8,128)} %get-tuple-element.41.mid_ref) | copy-start | bytes 2752516
  30.3 13.8 %collective-permute-start.2 = (f32[64,512]{1,0:T(8,128)S(1)}, f32[64,512]{1,0:T(8,128)S(1)}, u32[]{:S(2)}, u32[]{:S(2)}) collective-permute-start(f32[64,512]{1,0:T(8,128)S(1)} %get-tuple-element.38), channel_id=1, source_target_pairs={{0,1},{1,2},{2,3},{3,4},{4,5},{5,6},{6,7},{7,0},{8,9},{9,10},{10,1... | collective-permute-start | bytes 393224 | tf_op jit(solution)/shard_map/ppermute | solution.py:22
  31.5 12.6 %collective-permute-start.3 = (f32[72,512]{1,0:T(8,128)S(1)}, f32[72,512]{1,0:T(8,128)S(1)}, u32[]{:S(2)}, u32[]{:S(2)}) collective-permute-start(f32[72,512]{1,0:T(8,128)S(1)} %get-tuple-element.39), channel_id=1, source_target_pairs={{0,7},{1,0},{2,1},{3,2},{4,3},{5,4},{6,5},{7,6},{8,15},{9,8},{10,9... | collective-permute-start | bytes 442376 | tf_op jit(solution)/shard_map/ppermute | solution.py:22
  39.9 13.2 %collective-permute-start.8 = (f32[2,32,1536]{2,1,0:T(8,128)S(1)}, f32[2,32,1536]{2,1,0:T(8,128)S(1)}, u32[]{:S(2)}, u32[]{:S(2)}) collective-permute-start(f32[2,32,1536]{2,1,0:T(8,128)S(1)} %get-tuple-element.47.south_ref.own_south), channel_id=1, source_target_pairs={{0,7},{1,0},{2,1},{3,2},{4,3},{5,4},{6,5},{7,6},{8,15},{9,8},{10,9... | collective-permute-start | bytes 1179656 | tf_op jit(solution)/shard_map/ppermute | solution.py:22
  39.9 13.1 %collective-permute-start.7 = (f32[2,32,1536]{2,1,0:T(8,128)S(1)}, f32[2,32,1536]{2,1,0:T(8,128)S(1)}, u32[]{:S(2)}, u32[]{:S(2)}) collective-permute-start(f32[2,32,1536]{2,1,0:T(8,128)S(1)} %get-tuple-element.48.north_ref.own_north), channel_id=1, source_target_pairs={{0,1},{1,2},{2,3},{3,4},{4,5},{5,6},{6,7},{7,0},{8,9},{9,10},{10,1... | collective-permute-start | bytes 1179656 | tf_op jit(solution)/shard_map/ppermute | solution.py:22
  44.1 6.5 %copy-start.1 = (f32[4,32,1792]{2,1,0:T(8,128)S(1)}, f32[4,32,1792]{2,1,0:T(8,128)}, u32[]{:S(2)}) copy-start(f32[4,32,1792]{2,1,0:T(8,128)} %get-tuple-element.35.done_ref) | copy-start | bytes 2752516
  48.5 5.2 %collective-permute-start.9 = (f32[2,32,512]{2,1,0:T(8,128)S(1)}, f32[2,32,512]{2,1,0:T(8,128)S(1)}, u32[]{:S(2)}, u32[]{:S(2)}) collective-permute-start(f32[2,32,512]{2,1,0:T(8,128)S(1)} %get-tuple-element.51.north_ref.own_north), channel_id=1, source_target_pairs={{0,1},{1,2},{2,3},{3,4},{4,5},{5,6},{6,7},{7,0},{8,9},{9,10},{10,1... | collective-permute-start | bytes 393224 | tf_op jit(solution)/shard_map/ppermute | solution.py:22
  49.7 7.1 %collective-permute-start.10 = (f32[2,32,512]{2,1,0:T(8,128)S(1)}, f32[2,32,512]{2,1,0:T(8,128)S(1)}, u32[]{:S(2)}, u32[]{:S(2)}) collective-permute-start(f32[2,32,512]{2,1,0:T(8,128)S(1)} %get-tuple-element.46.corner_ref.south_ref.own_south), channel_id=1, source_target_pairs={{0,7},{1,0},{2,1},{3,2},{4,3},{5,4},{6,5},{7,6},{8,15},{9,8},{10,9... | collective-permute-start | bytes 393224 | tf_op jit(solution)/shard_map/ppermute | solution.py:22

commit v4 on v3

--- a/solution.py
+++ b/solution.py
@@ -369,7 +369,7 @@
 
 
 def side_kernel(
-    done_ref, xw_ref, xe_ref, hw_ref, he_ref, coef_ref, mid_ref, south_ref, north_ref, side_ref, cnt_ref
+    xw_ref, xe_ref, hw_ref, he_ref, coef_ref, mid_ref, south_ref, north_ref, side_ref, cnt_ref
 ):
     rows, species = mid_ref.shape[:2]
     width = coef_ref.shape[2]
@@ -768,8 +768,7 @@
     mid_side, side_south, side_north, side, counts = call(
         side_kernel,
         [(rows, species, four), (2 * species + 8, four), (2 * species, four), (6, rows, four), jax.ShapeDtypeStruct((rows, four), jnp.int32)],
-        [FAR] + [WHOLE] * 5,
-        done,
+        [WHOLE] * 5,
         west,
         east,
         halo_west,

time: 58.5 us -> 57.4 us (0.981)
  local copies, waits for them, and re-layouts: 1.21 us -> 0.04 us
    unnamed x22 -> x20, local copies, waits for them, and re-layouts: 1.21 us -> 0.04 us
  transfers between devices with their start and end apart: 11 -> 11, of which waited for: 1 -> 1; matrix products, arithmetic and copies ran while one was open for 0% -> 0% of each run, Pallas kernels for 52% -> 53%
where the time goes in v4:
time: 57.4 us; the launch traced here: 57.2 us
  Pallas kernels  34 us (59%)
  starting transfers between devices  19.7 us (34%)
  waiting for transfers between devices  3.17 us (6%)
    pallas_call x10, Pallas kernels, call(): pl.pallas_call(kernel, out_shape=[s if isinstance(s, jax.ShapeDtypeStruct...  34 us
    ppermute x11, starting transfers between devices, ring(): lax.ppermute(value, axis, [(i, (i + steps) % count) for i in range(count)])  19.7 us
    ppermute x11, waiting for transfers between devices, ring(): lax.ppermute(value, axis, [(i, (i + steps) % count) for i in range(count)])  3.17 us
  transfers between devices with their start and end apart: 11, of which 1 were waited for; matrix products, arithmetic and copies ran while one was open for 0% of the time, Pallas kernels for 53%

profile of v4, /device:TPU:6, one launch (start us, length us, event | category | flops | bytes accessed | tf_op | source)
XLA Modules:
  0.0 57.2 jit_solution(10778134103346501207)
XLA Ops:
  0.0 2.1 %shard_map.100 = (f32[304,256]{1,0:T(8,128)}, f32[304,256]{1,0:T(8,128)}) custom-call(f32[32,8,2048]{2,1,0:T(8,128)} %x_ref.5, f32[2,8,32]{2,1,0:T(8,128)} %cour_in.3, s32[2,8,32]{2,1,0:T(8,128)} %sw_in.3, s32[8,32]{1,0:T(8,128)} %day_in.3, s32[8,32]{1,0:T(8,128)} %cnt_ref.3), custom_call_target="tpu_custom_call" | custom-call | flops 2000000000 | bytes 6000000 | tf_op jit(solution)/shard_map/pallas_call | solution.py:155
  2.1 0.1 collective-permute-start
  2.2 6.2 %collective-permute-start.1 = (f32[304,256]{1,0:T(8,128)}, f32[304,256]{1,0:T(8,128)S(1)}, u32[]{:S(2)}, u32[]{:S(2)}) collective-permute-start(f32[304,256]{1,0:T(8,128)} %get-tuple-element.30.west_ref.xw_ref), channel_id=1, source_target_pairs={{0,120},{8,0},{16,8},{24,16},{32,24},{40,32},{48,40},{56,48},{64,5... | collective-permute-start | bytes 933896 | tf_op jit(solution)/shard_map/ppermute | solution.py:22
  8.3 3.8 %shard_map.101 = (f32[2,32,1792]{2,1,0:T(8,128)}, f32[2,32,1792]{2,1,0:T(8,128)}, f32[6,8,2048]{2,1,0:T(8,128)}, f32[16,2048]{1,0:T(8,128)}, f32[104,128]{1,0:T(8,128)}) custom-call(f32[304,256]{1,0:T(8,128)} %get-tuple-element.30.west_ref.xw_ref, f32[32,8,2048]{2,1,0:T(8,128)} %x_ref.5, f32[2,8,32]{2,1,0:T(8,128)} %cour_in.3, s32[2,8,32]{2,1,0:T(8,128)} %sw_in.3, ...), custom_call_target="tpu_custom_call" | custom-call | flops 3000000000 | bytes 9000000 | tf_op jit(solution)/shard_map/pallas_call | solution.py:155
  12.1 0.9 %collective-permute-start.6 = (f32[16,2048]{1,0:T(8,128)}, f32[16,2048]{1,0:T(8,128)S(1)}, u32[]{:S(2)}, u32[]{:S(2)}) collective-permute-start(f32[16,2048]{1,0:T(8,128)} %get-tuple-element.41), channel_id=1, source_target_pairs={{0,7},{1,0},{2,1},{3,2},{4,3},{5,4},{6,5},{7,6},{8,15},{9,8},{10,9... | collective-permute-start | bytes 393224 | tf_op jit(solution)/shard_map/ppermute | solution.py:22
  13.0 0.5 collective-permute-start.5
  13.5 3.6 %collective-permute-start.4 = (f32[2,32,1792]{2,1,0:T(8,128)}, f32[2,32,1792]{2,1,0:T(8,128)S(1)}, u32[]{:S(2)}, u32[]{:S(2)}) collective-permute-start(f32[2,32,1792]{2,1,0:T(8,128)} %get-tuple-element.38.north_ref.own_north_ref), channel_id=1, source_target_pairs={{0,1},{1,2},{2,3},{3,4},{4,5},{5,6},{6,7},{7,0},{8,9},{9,10},{10,1... | collective-permute-start | bytes 1376264 | tf_op jit(solution)/shard_map/ppermute | solution.py:22
  17.2 10.8 %shard_map.103 = (f32[4,32,1792]{2,1,0:T(8,128)}, f32[4,32,1792]{2,1,0:T(8,128)}, bf16[2,8,2,64,128]{4,3,2,1,0:T(8,128)(2,1)}) custom-call(f32[32,8,2048]{2,1,0:T(8,128)} %x_ref.5, f32[2,32,1792]{2,1,0:T(8,128)} %get-tuple-element.37.south_ref.own_south_ref, f32[2,32,1792]{2,1,0:T(8,128)} %get-tuple-element.38.north_ref.own_north_ref, ...), custom_call_target="tpu_custom_call" | custom-call | flops 8999999488 | bytes 27000000 | tf_op jit(solution)/shard_map/pallas_call | solution.py:155
  28.0 0.0 copy-start.7
  28.0 0.0 copy-start.9
  28.0 1.1 %shard_map.102 = (f32[8,32,512]{2,1,0:T(8,128)S(1)}, f32[72,512]{1,0:T(8,128)S(1)}, f32[64,512]{1,0:T(8,128)S(1)}, f32[6,8,512]{2,1,0:T(8,128)S(1)}, s32[8,512]{1,0:T(8,128)S(1)}) custom-call(f32[304,256]{1,0:T(8,128)S(1)} %copy-done.5, f32[304,256]{1,0:T(8,128)S(1)} %copy-done.6, f32[304,256]{1,0:T(8,128)S(1)} %collective-permute-done.hw_ref, ...), custom_call_target="tpu_custom_call" | custom-call | flops 3000000000 | bytes 9000000 | tf_op jit(solution)/shard_map/pallas_call | solution.py:155
  29.1 1.3 %collective-permute-start.2 = (f32[64,512]{1,0:T(8,128)S(1)}, f32[64,512]{1,0:T(8,128)S(1)}, u32[]{:S(2)}, u32[]{:S(2)}) collective-permute-start(f32[64,512]{1,0:T(8,128)S(1)} %get-tuple-element.34), channel_id=1, source_target_pairs={{0,1},{1,2},{2,3},{3,4},{4,5},{5,6},{6,7},{7,0},{8,9},{9,10},{10,1... | collective-permute-start | bytes 393224 | tf_op jit(solution)/shard_map/ppermute | solution.py:22
  30.4 0.8 %collective-permute-start.3 = (f32[72,512]{1,0:T(8,128)S(1)}, f32[72,512]{1,0:T(8,128)S(1)}, u32[]{:S(2)}, u32[]{:S(2)}) collective-permute-start(f32[72,512]{1,0:T(8,128)S(1)} %get-tuple-element.35), channel_id=1, source_target_pairs={{0,7},{1,0},{2,1},{3,2},{4,3},{5,4},{6,5},{7,6},{8,15},{9,8},{10,9... | collective-permute-start | bytes 442376 | tf_op jit(solution)/shard_map/ppermute | solution.py:22
  31.3 7.4 %shard_map.104 = (f32[4,32,1792]{2,1,0:T(8,128)S(1)}, f32[2,32,1536]{2,1,0:T(8,128)S(1)}, f32[2,32,1536]{2,1,0:T(8,128)S(1)}) custom-call(f32[6,8,512]{2,1,0:T(8,128)S(1)} %get-tuple-element.36.side_ref, f32[4,32,1792]{2,1,0:T(8,128)S(1)} %copy-done.9, f32[2,32,1792]{2,1,0:T(8,128)S(1)} %copy-done.3, f32[2,32,1792]{2,1,0:T(8,128)S(1)} %copy-done.4, ...), custom_call_target="tpu_custom_call" | custom-call | flops 8999999488 | bytes 27000000 | tf_op jit(solution)/shard_map/pallas_call | solution.py:155
  38.7 0.1 collective-permute-start.8
  38.8 4.1 %collective-permute-start.7 = (f32[2,32,1536]{2,1,0:T(8,128)S(1)}, f32[2,32,1536]{2,1,0:T(8,128)S(1)}, u32[]{:S(2)}, u32[]{:S(2)}) collective-permute-start(f32[2,32,1536]{2,1,0:T(8,128)S(1)} %get-tuple-element.48.north_ref.own_north), channel_id=1, source_target_pairs={{0,1},{1,2},{2,3},{3,4},{4,5},{5,6},{6,7},{7,0},{8,9},{9,10},{10,1... | collective-permute-start | bytes 1179656 | tf_op jit(solution)/shard_map/ppermute | solution.py:22
  42.9 4.4 %shard_map.105 = (f32[8,32,512]{2,1,0:T(8,128)S(1)}, f32[2,32,512]{2,1,0:T(8,128)S(1)}, f32[2,32,512]{2,1,0:T(8,128)S(1)}) custom-call(f32[8,32,512]{2,1,0:T(8,128)S(1)} %get-tuple-element.33.mid_ref, f32[64,512]{1,0:T(8,128)S(1)} %collective-permute-done.2.south_ref, f32[72,512]{1,0:T(8,128)S(1)} %collective-permute-done.3.north_ref, ...), custom_call_target="tpu_custom_call" | custom-call | flops 5000000000 | bytes 15000000 | tf_op jit(solution)/shard_map/pallas_call | solution.py:155
  47.3 1.3 %collective-permute-start.9 = (f32[2,32,512]{2,1,0:T(8,128)S(1)}, f32[2,32,512]{2,1,0:T(8,128)S(1)}, u32[]{:S(2)}, u32[]{:S(2)}) collective-permute-start(f32[2,32,512]{2,1,0:T(8,128)S(1)} %get-tuple-element.51.north_ref.own_north), channel_id=1, source_target_pairs={{0,1},{1,2},{2,3},{3,4},{4,5},{5,6},{6,7},{7,0},{8,9},{9,10},{10,1... | collective-permute-start | bytes 393224 | tf_op jit(solution)/shard_map/ppermute | solution.py:22
  48.6 0.8 %collective-permute-start.10 = (f32[2,32,512]{2,1,0:T(8,128)S(1)}, f32[2,32,512]{2,1,0:T(8,128)S(1)}, u32[]{:S(2)}, u32[]{:S(2)}) collective-permute-start(f32[2,32,512]{2,1,0:T(8,128)S(1)} %get-tuple-element.45.corner_ref.south_ref.own_south), channel_id=1, source_target_pairs={{0,7},{1,0},{2,1},{3,2},{4,3},{5,4},{6,5},{7,6},{8,15},{9,8},{10,9... | collective-permute-start | bytes 393224 | tf_op jit(solution)/shard_map/ppermute | solution.py:22
  49.4 1.5 %shard_map.106 = (f32[4,32,1536]{2,1,0:T(8,128)S(1)}, f32[4,32,1536]{2,1,0:T(8,128)S(1)}) custom-call(f32[2,32,512]{2,1,0:T(8,128)S(1)} %get-tuple-element.45.corner_ref.south_ref.own_south, f32[4,32,1792]{2,1,0:T(8,128)S(1)} %copy-done, f32[2,32,1536]{2,1,0:T(8,128)S(1)} %get-tuple-element.47.south_ref.own_south, ...), custom_call_target="tpu_custom_call" | custom-call | flops 100000000 | bytes 300000 | tf_op jit(solution)/shard_map/pallas_call | solution.py:155
  50.9 1.0 %shard_map.107 = (f32[4,32,512]{2,1,0:T(8,128)S(1)}, f32[4,32,512]{2,1,0:T(8,128)S(1)}) custom-call(f32[4,32,1792]{2,1,0:T(8,128)S(1)} %copy-done, f32[8,32,512]{2,1,0:T(8,128)S(1)} %get-tuple-element.50.corner_ref, f32[2,32,512]{2,1,0:T(8,128)S(1)} %get-tuple-element.45.corner_ref.south_ref.own_south, ...), custom_call_target="tpu_custom_call" | custom-call | flops 100000000 | bytes 300000 | tf_op jit(solution)/shard_map/pallas_call | solution.py:155
  51.9 0.6 %shard_map.108.edge_a = f32[4,32,1536]{2,1,0:T(8,128)S(1)} custom-call(f32[4,32,512]{2,1,0:T(8,128)S(1)} %get-tuple-element.52.inner_c, f32[4,32,1536]{2,1,0:T(8,128)S(1)} %get-tuple-element.53.swept, f32[2,32,1536]{2,1,0:T(8,128)S(1)} %get-tuple-element.47.south_ref.own_south, f32[2,32,1536]{2,1,0:T(8,128)S(1)} %get-tuple-element.48.north_ref.own_north, ...), custom_call_target="tpu_custom_call" | custom-call | flops 500000000 | bytes 1500000 | tf_op jit(solution)/shard_map/pallas_call | solution.py:155
  52.5 3.1 %collective-permute-done.10.north = f32[2,32,512]{2,1,0:T(8,128)S(1)} collective-permute-done((f32[2,32,512]{2,1,0:T(8,128)S(1)}, f32[2,32,512]{2,1,0:T(8,128)S(1)}, u32[]{:S(2)}, u32[]{:S(2)}) %collective-permute-start.10) | collective-permute-done | bytes 131104 | tf_op jit(solution)/shard_map/ppermute | solution.py:22
  55.7 1.5 %shard_map.109 = f32[32,8,2048]{2,1,0:T(8,128)} custom-call(f32[4,32,1536]{2,1,0:T(8,128)S(1)} %get-tuple-element.49.inner_a, f32[4,32,512]{2,1,0:T(8,128)S(1)} %get-tuple-element.52.inner_c, f32[4,32,1536]{2,1,0:T(8,128)S(1)} %shard_map.108.edge_a, f32[4,32,512]{2,1,0:T(8,128)S(1)} %get-tuple-element.54.swept, ...), custom_call_target="tpu_custom_call" | custom-call | flops 3000000000 | bytes 9000000 | tf_op jit(solution)/shard_map/pallas_call | solution.py:155
  (28 shorter events, 0.1 us)
Async XLA Ops:
  2.1 25.9 %collective-permute-start = (f32[304,256]{1,0:T(8,128)}, f32[304,256]{1,0:T(8,128)S(1)}, u32[]{:S(2)}, u32[]{:S(2)}) collective-permute-start(f32[304,256]{1,0:T(8,128)} %get-tuple-element.31.xe_ref), channel_id=1, source_target_pairs={{0,8},{8,16},{16,24},{24,32},{32,40},{40,48},{48,56},{56,64},{64,7... | collective-permute-start | bytes 933896 | tf_op jit(solution)/shard_map/ppermute | solution.py:22
  2.2 25.8 %collective-permute-start.1 = (f32[304,256]{1,0:T(8,128)}, f32[304,256]{1,0:T(8,128)S(1)}, u32[]{:S(2)}, u32[]{:S(2)}) collective-permute-start(f32[304,256]{1,0:T(8,128)} %get-tuple-element.30.west_ref.xw_ref), channel_id=1, source_target_pairs={{0,120},{8,0},{16,8},{24,16},{32,24},{40,32},{48,40},{56,48},{64,5... | collective-permute-start | bytes 933896 | tf_op jit(solution)/shard_map/ppermute | solution.py:22
  12.1 19.1 %collective-permute-start.6 = (f32[16,2048]{1,0:T(8,128)}, f32[16,2048]{1,0:T(8,128)S(1)}, u32[]{:S(2)}, u32[]{:S(2)}) collective-permute-start(f32[16,2048]{1,0:T(8,128)} %get-tuple-element.41), channel_id=1, source_target_pairs={{0,7},{1,0},{2,1},{3,2},{4,3},{5,4},{6,5},{7,6},{8,15},{9,8},{10,9... | collective-permute-start | bytes 393224 | tf_op jit(solution)/shard_map/ppermute | solution.py:22
  13.0 18.2 %collective-permute-start.5 = (f32[2,32,1792]{2,1,0:T(8,128)}, f32[2,32,1792]{2,1,0:T(8,128)S(1)}, u32[]{:S(2)}, u32[]{:S(2)}) collective-permute-start(f32[2,32,1792]{2,1,0:T(8,128)} %get-tuple-element.37.south_ref.own_south_ref), channel_id=1, source_target_pairs={{0,7},{1,0},{2,1},{3,2},{4,3},{5,4},{6,5},{7,6},{8,15},{9,8},{10,9... | collective-permute-start | bytes 1376264 | tf_op jit(solution)/shard_map/ppermute | solution.py:22
  13.5 17.7 %collective-permute-start.4 = (f32[2,32,1792]{2,1,0:T(8,128)}, f32[2,32,1792]{2,1,0:T(8,128)S(1)}, u32[]{:S(2)}, u32[]{:S(2)}) collective-permute-start(f32[2,32,1792]{2,1,0:T(8,128)} %get-tuple-element.38.north_ref.own_north_ref), channel_id=1, source_target_pairs={{0,1},{1,2},{2,3},{3,4},{4,5},{5,6},{6,7},{7,0},{8,9},{9,10},{10,1... | collective-permute-start | bytes 1376264 | tf_op jit(solution)/shard_map/ppermute | solution.py:22
  17.2 10.9 %copy-start.1 = (f32[6,8,2048]{2,1,0:T(8,128)S(1)}, f32[6,8,2048]{2,1,0:T(8,128)}, u32[]{:S(2)}) copy-start(f32[6,8,2048]{2,1,0:T(8,128)} %get-tuple-element.32.coef_ref) | copy-start | bytes 1179652
  17.2 10.9 %copy-start.5 = (f32[304,256]{1,0:T(8,128)S(1)}, f32[304,256]{1,0:T(8,128)}, u32[]{:S(2)}) copy-start(f32[304,256]{1,0:T(8,128)} %get-tuple-element.30.west_ref.xw_ref) | copy-start | bytes 933892
  17.2 10.9 %copy-start.6 = (f32[304,256]{1,0:T(8,128)S(1)}, f32[304,256]{1,0:T(8,128)}, u32[]{:S(2)}) copy-start(f32[304,256]{1,0:T(8,128)} %get-tuple-element.31.xe_ref) | copy-start | bytes 933892
  27.9 3.3 %copy-start.2 = (f32[104,128]{1,0:T(8,128)S(1)}, f32[104,128]{1,0:T(8,128)}, u32[]{:S(2)}) copy-start(f32[104,128]{1,0:T(8,128)} %get-tuple-element.39.chem_ref) | copy-start | bytes 159748
  27.9 3.3 %copy-start.3 = (f32[2,32,1792]{2,1,0:T(8,128)S(1)}, f32[2,32,1792]{2,1,0:T(8,128)}, u32[]{:S(2)}) copy-start(f32[2,32,1792]{2,1,0:T(8,128)} %get-tuple-element.37.south_ref.own_south_ref) | copy-start | bytes 1376260
  27.9 3.3 %copy-start.4 = (f32[2,32,1792]{2,1,0:T(8,128)S(1)}, f32[2,32,1792]{2,1,0:T(8,128)}, u32[]{:S(2)}) copy-start(f32[2,32,1792]{2,1,0:T(8,128)} %get-tuple-element.38.north_ref.own_north_ref) | copy-start | bytes 1376260
  28.0 3.3 %copy-start.7 = (s32[8,32]{1,0:T(8,128)S(1)}, s32[8,32]{1,0:T(8,128)}, u32[]{:S(2)}) copy-start(s32[8,32]{1,0:T(8,128)} %cnt_ref.3) | copy-start | bytes 3076
  28.0 3.3 %copy-start.8 = (bf16[2,8,2,64,128]{4,3,2,1,0:T(8,128)(2,1)S(1)}, bf16[2,8,2,64,128]{4,3,2,1,0:T(8,128)(2,1)}, u32[]{:S(2)}) copy-start(bf16[2,8,2,64,128]{4,3,2,1,0:T(8,128)(2,1)} %get-tuple-element.42.table_ref) | copy-start | bytes 1572868
  28.0 3.3 %copy-start.9 = (f32[4,32,1792]{2,1,0:T(8,128)S(1)}, f32[4,32,1792]{2,1,0:T(8,128)}, u32[]{:S(2)}) copy-start(f32[4,32,1792]{2,1,0:T(8,128)} %get-tuple-element.40.mid_ref) | copy-start | bytes 2752516
  29.1 13.8 %collective-permute-start.2 = (f32[64,512]{1,0:T(8,128)S(1)}, f32[64,512]{1,0:T(8,128)S(1)}, u32[]{:S(2)}, u32[]{:S(2)}) collective-permute-start(f32[64,512]{1,0:T(8,128)S(1)} %get-tuple-element.34), channel_id=1, source_target_pairs={{0,1},{1,2},{2,3},{3,4},{4,5},{5,6},{6,7},{7,0},{8,9},{9,10},{10,1... | collective-permute-start | bytes 393224 | tf_op jit(solution)/shard_map/ppermute | solution.py:22
  30.4 12.5 %collective-permute-start.3 = (f32[72,512]{1,0:T(8,128)S(1)}, f32[72,512]{1,0:T(8,128)S(1)}, u32[]{:S(2)}, u32[]{:S(2)}) collective-permute-start(f32[72,512]{1,0:T(8,128)S(1)} %get-tuple-element.35), channel_id=1, source_target_pairs={{0,7},{1,0},{2,1},{3,2},{4,3},{5,4},{6,5},{7,6},{8,15},{9,8},{10,9... | collective-permute-start | bytes 442376 | tf_op jit(solution)/shard_map/ppermute | solution.py:22
  38.7 13.2 %collective-permute-start.8 = (f32[2,32,1536]{2,1,0:T(8,128)S(1)}, f32[2,32,1536]{2,1,0:T(8,128)S(1)}, u32[]{:S(2)}, u32[]{:S(2)}) collective-permute-start(f32[2,32,1536]{2,1,0:T(8,128)S(1)} %get-tuple-element.47.south_ref.own_south), channel_id=1, source_target_pairs={{0,7},{1,0},{2,1},{3,2},{4,3},{5,4},{6,5},{7,6},{8,15},{9,8},{10,9... | collective-permute-start | bytes 1179656 | tf_op jit(solution)/shard_map/ppermute | solution.py:22
  38.8 13.1 %collective-permute-start.7 = (f32[2,32,1536]{2,1,0:T(8,128)S(1)}, f32[2,32,1536]{2,1,0:T(8,128)S(1)}, u32[]{:S(2)}, u32[]{:S(2)}) collective-permute-start(f32[2,32,1536]{2,1,0:T(8,128)S(1)} %get-tuple-element.48.north_ref.own_north), channel_id=1, source_target_pairs={{0,1},{1,2},{2,3},{3,4},{4,5},{5,6},{6,7},{7,0},{8,9},{9,10},{10,1... | collective-permute-start | bytes 1179656 | tf_op jit(solution)/shard_map/ppermute | solution.py:22
  42.9 6.5 %copy-start = (f32[4,32,1792]{2,1,0:T(8,128)S(1)}, f32[4,32,1792]{2,1,0:T(8,128)}, u32[]{:S(2)}) copy-start(f32[4,32,1792]{2,1,0:T(8,128)} %get-tuple-element.46.done_ref) | copy-start | bytes 2752516
  47.3 5.2 %collective-permute-start.9 = (f32[2,32,512]{2,1,0:T(8,128)S(1)}, f32[2,32,512]{2,1,0:T(8,128)S(1)}, u32[]{:S(2)}, u32[]{:S(2)}) collective-permute-start(f32[2,32,512]{2,1,0:T(8,128)S(1)} %get-tuple-element.51.north_ref.own_north), channel_id=1, source_target_pairs={{0,1},{1,2},{2,3},{3,4},{4,5},{5,6},{6,7},{7,0},{8,9},{9,10},{10,1... | collective-permute-start | bytes 393224 | tf_op jit(solution)/shard_map/ppermute | solution.py:22
  48.6 7.1 %collective-permute-start.10 = (f32[2,32,512]{2,1,0:T(8,128)S(1)}, f32[2,32,512]{2,1,0:T(8,128)S(1)}, u32[]{:S(2)}, u32[]{:S(2)}) collective-permute-start(f32[2,32,512]{2,1,0:T(8,128)S(1)} %get-tuple-element.45.corner_ref.south_ref.own_south), channel_id=1, source_target_pairs={{0,7},{1,0},{2,1},{3,2},{4,3},{5,4},{6,5},{7,6},{8,15},{9,8},{10,9... | collective-permute-start | bytes 393224 | tf_op jit(solution)/shard_map/ppermute | solution.py:22

commit v5 on v4

--- a/solution.py
+++ b/solution.py
@@ -148,7 +148,7 @@
 WHOLE = pl.BlockSpec(memory_space=pltpu.VMEM)
 SCALARS = pl.BlockSpec(memory_space=pltpu.SMEM)
 FAR = pl.BlockSpec(memory_space=pl.ANY)
-BLOCK = 4 * PIECE
+BLOCK = 7 * PIECE
 
 
 def call(kernel, outs, ins, *args, scratch=(), out_specs=None, cost=10.0, limit=VMEM_LIMIT):

time: 57.4 us -> 53.1 us (0.925)
  Pallas kernels: 34 us -> 29.7 us
    pallas_call x10, Pallas kernels: 34 us -> 29.7 us  [call(): pl.pallas_call(kernel, out_shape=[s if isinstance(s, jax.ShapeDtypeStruct...]
  transfers between devices with their start and end apart: 11 -> 11, of which waited for: 1 -> 1; matrix products, arithmetic and copies ran while one was open for 0% -> 0% of each run, Pallas kernels for 53% -> 49%
where the time goes in v5:
time: 53.1 us; the launch traced here: 52.9 us
  Pallas kernels  29.7 us (56%)
  starting transfers between devices  19.7 us (37%)
  waiting for transfers between devices  3.17 us (6%)
    pallas_call x10, Pallas kernels, call(): pl.pallas_call(kernel, out_shape=[s if isinstance(s, jax.ShapeDtypeStruct...  29.7 us
    ppermute x11, starting transfers between devices, ring(): lax.ppermute(value, axis, [(i, (i + steps) % count) for i in range(count)])  19.7 us
    ppermute x11, waiting for transfers between devices, ring(): lax.ppermute(value, axis, [(i, (i + steps) % count) for i in range(count)])  3.17 us
  transfers between devices with their start and end apart: 11, of which 1 were waited for; matrix products, arithmetic and copies ran while one was open for 0% of the time, Pallas kernels for 49%

profile of v5, /device:TPU:6, one launch (start us, length us, event | category | flops | bytes accessed | tf_op | source)
XLA Modules:
  0.0 52.9 jit_solution(3051929634903485551)
XLA Ops:
  0.0 2.1 %shard_map.100 = (f32[304,256]{1,0:T(8,128)}, f32[304,256]{1,0:T(8,128)}) custom-call(f32[32,8,2048]{2,1,0:T(8,128)} %x_ref.5, f32[2,8,32]{2,1,0:T(8,128)} %cour_in.3, s32[2,8,32]{2,1,0:T(8,128)} %sw_in.3, s32[8,32]{1,0:T(8,128)} %day_in.3, s32[8,32]{1,0:T(8,128)} %cnt_ref.3), custom_call_target="tpu_custom_call" | custom-call | flops 2000000000 | bytes 6000000 | tf_op jit(solution)/shard_map/pallas_call | solution.py:155
  2.1 0.1 collective-permute-start
  2.2 6.2 %collective-permute-start.1 = (f32[304,256]{1,0:T(8,128)}, f32[304,256]{1,0:T(8,128)S(1)}, u32[]{:S(2)}, u32[]{:S(2)}) collective-permute-start(f32[304,256]{1,0:T(8,128)} %get-tuple-element.30.west_ref.xw_ref), channel_id=1, source_target_pairs={{0,120},{8,0},{16,8},{24,16},{32,24},{40,32},{48,40},{56,48},{64,5... | collective-permute-start | bytes 933896 | tf_op jit(solution)/shard_map/ppermute | solution.py:22
  8.3 3.8 %shard_map.101 = (f32[2,32,1792]{2,1,0:T(8,128)}, f32[2,32,1792]{2,1,0:T(8,128)}, f32[6,8,2048]{2,1,0:T(8,128)}, f32[16,2048]{1,0:T(8,128)}, f32[104,128]{1,0:T(8,128)}) custom-call(f32[304,256]{1,0:T(8,128)} %get-tuple-element.30.west_ref.xw_ref, f32[32,8,2048]{2,1,0:T(8,128)} %x_ref.5, f32[2,8,32]{2,1,0:T(8,128)} %cour_in.3, s32[2,8,32]{2,1,0:T(8,128)} %sw_in.3, ...), custom_call_target="tpu_custom_call" | custom-call | flops 3000000000 | bytes 9000000 | tf_op jit(solution)/shard_map/pallas_call | solution.py:155
  12.1 0.9 %collective-permute-start.6 = (f32[16,2048]{1,0:T(8,128)}, f32[16,2048]{1,0:T(8,128)S(1)}, u32[]{:S(2)}, u32[]{:S(2)}) collective-permute-start(f32[16,2048]{1,0:T(8,128)} %get-tuple-element.41), channel_id=1, source_target_pairs={{0,7},{1,0},{2,1},{3,2},{4,3},{5,4},{6,5},{7,6},{8,15},{9,8},{10,9... | collective-permute-start | bytes 393224 | tf_op jit(solution)/shard_map/ppermute | solution.py:22
  13.0 0.5 %collective-permute-start.5 = (f32[2,32,1792]{2,1,0:T(8,128)}, f32[2,32,1792]{2,1,0:T(8,128)S(1)}, u32[]{:S(2)}, u32[]{:S(2)}) collective-permute-start(f32[2,32,1792]{2,1,0:T(8,128)} %get-tuple-element.37.south_ref.own_south_ref), channel_id=1, source_target_pairs={{0,7},{1,0},{2,1},{3,2},{4,3},{5,4},{6,5},{7,6},{8,15},{9,8},{10,9... | collective-permute-start | bytes 1376264 | tf_op jit(solution)/shard_map/ppermute | solution.py:22
  13.5 3.6 %collective-permute-start.4 = (f32[2,32,1792]{2,1,0:T(8,128)}, f32[2,32,1792]{2,1,0:T(8,128)S(1)}, u32[]{:S(2)}, u32[]{:S(2)}) collective-permute-start(f32[2,32,1792]{2,1,0:T(8,128)} %get-tuple-element.38.north_ref.own_north_ref), channel_id=1, source_target_pairs={{0,1},{1,2},{2,3},{3,4},{4,5},{5,6},{6,7},{7,0},{8,9},{9,10},{10,1... | collective-permute-start | bytes 1376264 | tf_op jit(solution)/shard_map/ppermute | solution.py:22
  17.2 8.6 %shard_map.103 = (f32[4,32,1792]{2,1,0:T(8,128)}, f32[4,32,1792]{2,1,0:T(8,128)}, bf16[2,8,2,64,128]{4,3,2,1,0:T(8,128)(2,1)}) custom-call(f32[32,8,2048]{2,1,0:T(8,128)} %x_ref.5, f32[2,32,1792]{2,1,0:T(8,128)} %get-tuple-element.37.south_ref.own_south_ref, f32[2,32,1792]{2,1,0:T(8,128)} %get-tuple-element.38.north_ref.own_north_ref, ...), custom_call_target="tpu_custom_call" | custom-call | flops 8999999488 | bytes 27000000 | tf_op jit(solution)/shard_map/pallas_call | solution.py:155
  25.8 0.0 copy-start.7
  25.8 0.0 copy-start.9
  25.8 1.1 %shard_map.102 = (f32[8,32,512]{2,1,0:T(8,128)S(1)}, f32[72,512]{1,0:T(8,128)S(1)}, f32[64,512]{1,0:T(8,128)S(1)}, f32[6,8,512]{2,1,0:T(8,128)S(1)}, s32[8,512]{1,0:T(8,128)S(1)}) custom-call(f32[304,256]{1,0:T(8,128)S(1)} %copy-done.5, f32[304,256]{1,0:T(8,128)S(1)} %copy-done.6, f32[304,256]{1,0:T(8,128)S(1)} %collective-permute-done.hw_ref, ...), custom_call_target="tpu_custom_call" | custom-call | flops 3000000000 | bytes 9000000 | tf_op jit(solution)/shard_map/pallas_call | solution.py:155
  26.9 1.3 %collective-permute-start.2 = (f32[64,512]{1,0:T(8,128)S(1)}, f32[64,512]{1,0:T(8,128)S(1)}, u32[]{:S(2)}, u32[]{:S(2)}) collective-permute-start(f32[64,512]{1,0:T(8,128)S(1)} %get-tuple-element.34), channel_id=1, source_target_pairs={{0,1},{1,2},{2,3},{3,4},{4,5},{5,6},{6,7},{7,0},{8,9},{9,10},{10,1... | collective-permute-start | bytes 393224 | tf_op jit(solution)/shard_map/ppermute | solution.py:22
  28.2 0.8 %collective-permute-start.3 = (f32[72,512]{1,0:T(8,128)S(1)}, f32[72,512]{1,0:T(8,128)S(1)}, u32[]{:S(2)}, u32[]{:S(2)}) collective-permute-start(f32[72,512]{1,0:T(8,128)S(1)} %get-tuple-element.35), channel_id=1, source_target_pairs={{0,7},{1,0},{2,1},{3,2},{4,3},{5,4},{6,5},{7,6},{8,15},{9,8},{10,9... | collective-permute-start | bytes 442376 | tf_op jit(solution)/shard_map/ppermute | solution.py:22
  29.1 5.3 %shard_map.104 = (f32[4,32,1792]{2,1,0:T(8,128)S(1)}, f32[2,32,1536]{2,1,0:T(8,128)S(1)}, f32[2,32,1536]{2,1,0:T(8,128)S(1)}) custom-call(f32[6,8,512]{2,1,0:T(8,128)S(1)} %get-tuple-element.36.side_ref, f32[4,32,1792]{2,1,0:T(8,128)S(1)} %copy-done.9, f32[2,32,1792]{2,1,0:T(8,128)S(1)} %copy-done.3, f32[2,32,1792]{2,1,0:T(8,128)S(1)} %copy-done.4, ...), custom_call_target="tpu_custom_call" | custom-call | flops 8999999488 | bytes 27000000 | tf_op jit(solution)/shard_map/pallas_call | solution.py:155
  34.4 0.1 collective-permute-start.8
  34.5 4.1 %collective-permute-start.7 = (f32[2,32,1536]{2,1,0:T(8,128)S(1)}, f32[2,32,1536]{2,1,0:T(8,128)S(1)}, u32[]{:S(2)}, u32[]{:S(2)}) collective-permute-start(f32[2,32,1536]{2,1,0:T(8,128)S(1)} %get-tuple-element.48.north_ref.own_north), channel_id=1, source_target_pairs={{0,1},{1,2},{2,3},{3,4},{4,5},{5,6},{6,7},{7,0},{8,9},{9,10},{10,1... | collective-permute-start | bytes 1179656 | tf_op jit(solution)/shard_map/ppermute | solution.py:22
  38.6 4.4 %shard_map.105 = (f32[8,32,512]{2,1,0:T(8,128)S(1)}, f32[2,32,512]{2,1,0:T(8,128)S(1)}, f32[2,32,512]{2,1,0:T(8,128)S(1)}) custom-call(f32[8,32,512]{2,1,0:T(8,128)S(1)} %get-tuple-element.33.mid_ref, f32[64,512]{1,0:T(8,128)S(1)} %collective-permute-done.2.south_ref, f32[72,512]{1,0:T(8,128)S(1)} %collective-permute-done.3.north_ref, ...), custom_call_target="tpu_custom_call" | custom-call | flops 5000000000 | bytes 15000000 | tf_op jit(solution)/shard_map/pallas_call | solution.py:155
  43.0 1.3 %collective-permute-start.9 = (f32[2,32,512]{2,1,0:T(8,128)S(1)}, f32[2,32,512]{2,1,0:T(8,128)S(1)}, u32[]{:S(2)}, u32[]{:S(2)}) collective-permute-start(f32[2,32,512]{2,1,0:T(8,128)S(1)} %get-tuple-element.51.north_ref.own_north), channel_id=1, source_target_pairs={{0,1},{1,2},{2,3},{3,4},{4,5},{5,6},{6,7},{7,0},{8,9},{9,10},{10,1... | collective-permute-start | bytes 393224 | tf_op jit(solution)/shard_map/ppermute | solution.py:22
  44.3 0.8 %collective-permute-start.10 = (f32[2,32,512]{2,1,0:T(8,128)S(1)}, f32[2,32,512]{2,1,0:T(8,128)S(1)}, u32[]{:S(2)}, u32[]{:S(2)}) collective-permute-start(f32[2,32,512]{2,1,0:T(8,128)S(1)} %get-tuple-element.45.corner_ref.south_ref.own_south), channel_id=1, source_target_pairs={{0,7},{1,0},{2,1},{3,2},{4,3},{5,4},{6,5},{7,6},{8,15},{9,8},{10,9... | collective-permute-start | bytes 393224 | tf_op jit(solution)/shard_map/ppermute | solution.py:22
  45.1 1.5 %shard_map.106 = (f32[4,32,1536]{2,1,0:T(8,128)S(1)}, f32[4,32,1536]{2,1,0:T(8,128)S(1)}) custom-call(f32[2,32,512]{2,1,0:T(8,128)S(1)} %get-tuple-element.45.corner_ref.south_ref.own_south, f32[4,32,1792]{2,1,0:T(8,128)S(1)} %copy-done, f32[2,32,1536]{2,1,0:T(8,128)S(1)} %get-tuple-element.47.south_ref.own_south, ...), custom_call_target="tpu_custom_call" | custom-call | flops 100000000 | bytes 300000 | tf_op jit(solution)/shard_map/pallas_call | solution.py:155
  46.6 1.0 %shard_map.107 = (f32[4,32,512]{2,1,0:T(8,128)S(1)}, f32[4,32,512]{2,1,0:T(8,128)S(1)}) custom-call(f32[4,32,1792]{2,1,0:T(8,128)S(1)} %copy-done, f32[8,32,512]{2,1,0:T(8,128)S(1)} %get-tuple-element.50.corner_ref, f32[2,32,512]{2,1,0:T(8,128)S(1)} %get-tuple-element.45.corner_ref.south_ref.own_south, ...), custom_call_target="tpu_custom_call" | custom-call | flops 100000000 | bytes 300000 | tf_op jit(solution)/shard_map/pallas_call | solution.py:155
  47.6 0.6 %shard_map.108.edge_a = f32[4,32,1536]{2,1,0:T(8,128)S(1)} custom-call(f32[4,32,512]{2,1,0:T(8,128)S(1)} %get-tuple-element.52.inner_c, f32[4,32,1536]{2,1,0:T(8,128)S(1)} %get-tuple-element.53.swept, f32[2,32,1536]{2,1,0:T(8,128)S(1)} %get-tuple-element.47.south_ref.own_south, f32[2,32,1536]{2,1,0:T(8,128)S(1)} %get-tuple-element.48.north_ref.own_north, ...), custom_call_target="tpu_custom_call" | custom-call | flops 500000000 | bytes 1500000 | tf_op jit(solution)/shard_map/pallas_call | solution.py:155
  48.2 3.1 %collective-permute-done.10.north = f32[2,32,512]{2,1,0:T(8,128)S(1)} collective-permute-done((f32[2,32,512]{2,1,0:T(8,128)S(1)}, f32[2,32,512]{2,1,0:T(8,128)S(1)}, u32[]{:S(2)}, u32[]{:S(2)}) %collective-permute-start.10) | collective-permute-done | bytes 131104 | tf_op jit(solution)/shard_map/ppermute | solution.py:22
  51.4 1.5 %shard_map.109 = f32[32,8,2048]{2,1,0:T(8,128)} custom-call(f32[4,32,1536]{2,1,0:T(8,128)S(1)} %get-tuple-element.49.inner_a, f32[4,32,512]{2,1,0:T(8,128)S(1)} %get-tuple-element.52.inner_c, f32[4,32,1536]{2,1,0:T(8,128)S(1)} %shard_map.108.edge_a, f32[4,32,512]{2,1,0:T(8,128)S(1)} %get-tuple-element.54.swept, ...), custom_call_target="tpu_custom_call" | custom-call | flops 3000000000 | bytes 9000000 | tf_op jit(solution)/shard_map/pallas_call | solution.py:155
  (28 shorter events, 0.1 us)
Async XLA Ops:
  2.1 23.7 %collective-permute-start = (f32[304,256]{1,0:T(8,128)}, f32[304,256]{1,0:T(8,128)S(1)}, u32[]{:S(2)}, u32[]{:S(2)}) collective-permute-start(f32[304,256]{1,0:T(8,128)} %get-tuple-element.31.xe_ref), channel_id=1, source_target_pairs={{0,8},{8,16},{16,24},{24,32},{32,40},{40,48},{48,56},{56,64},{64,7... | collective-permute-start | bytes 933896 | tf_op jit(solution)/shard_map/ppermute | solution.py:22
  2.2 23.6 %collective-permute-start.1 = (f32[304,256]{1,0:T(8,128)}, f32[304,256]{1,0:T(8,128)S(1)}, u32[]{:S(2)}, u32[]{:S(2)}) collective-permute-start(f32[304,256]{1,0:T(8,128)} %get-tuple-element.30.west_ref.xw_ref), channel_id=1, source_target_pairs={{0,120},{8,0},{16,8},{24,16},{32,24},{40,32},{48,40},{56,48},{64,5... | collective-permute-start | bytes 933896 | tf_op jit(solution)/shard_map/ppermute | solution.py:22
  12.1 16.9 %collective-permute-start.6 = (f32[16,2048]{1,0:T(8,128)}, f32[16,2048]{1,0:T(8,128)S(1)}, u32[]{:S(2)}, u32[]{:S(2)}) collective-permute-start(f32[16,2048]{1,0:T(8,128)} %get-tuple-element.41), channel_id=1, source_target_pairs={{0,7},{1,0},{2,1},{3,2},{4,3},{5,4},{6,5},{7,6},{8,15},{9,8},{10,9... | collective-permute-start | bytes 393224 | tf_op jit(solution)/shard_map/ppermute | solution.py:22
  13.0 16.0 %collective-permute-start.5 = (f32[2,32,1792]{2,1,0:T(8,128)}, f32[2,32,1792]{2,1,0:T(8,128)S(1)}, u32[]{:S(2)}, u32[]{:S(2)}) collective-permute-start(f32[2,32,1792]{2,1,0:T(8,128)} %get-tuple-element.37.south_ref.own_south_ref), channel_id=1, source_target_pairs={{0,7},{1,0},{2,1},{3,2},{4,3},{5,4},{6,5},{7,6},{8,15},{9,8},{10,9... | collective-permute-start | bytes 1376264 | tf_op jit(solution)/shard_map/ppermute | solution.py:22
  13.5 15.5 %collective-permute-start.4 = (f32[2,32,1792]{2,1,0:T(8,128)}, f32[2,32,1792]{2,1,0:T(8,128)S(1)}, u32[]{:S(2)}, u32[]{:S(2)}) collective-permute-start(f32[2,32,1792]{2,1,0:T(8,128)} %get-tuple-element.38.north_ref.own_north_ref), channel_id=1, source_target_pairs={{0,1},{1,2},{2,3},{3,4},{4,5},{5,6},{6,7},{7,0},{8,9},{9,10},{10,1... | collective-permute-start | bytes 1376264 | tf_op jit(solution)/shard_map/ppermute | solution.py:22
  17.2 8.7 %copy-start.1 = (f32[6,8,2048]{2,1,0:T(8,128)S(1)}, f32[6,8,2048]{2,1,0:T(8,128)}, u32[]{:S(2)}) copy-start(f32[6,8,2048]{2,1,0:T(8,128)} %get-tuple-element.32.coef_ref) | copy-start | bytes 1179652
  17.2 8.7 %copy-start.5 = (f32[304,256]{1,0:T(8,128)S(1)}, f32[304,256]{1,0:T(8,128)}, u32[]{:S(2)}) copy-start(f32[304,256]{1,0:T(8,128)} %get-tuple-element.30.west_ref.xw_ref) | copy-start | bytes 933892
  17.2 8.7 %copy-start.6 = (f32[304,256]{1,0:T(8,128)S(1)}, f32[304,256]{1,0:T(8,128)}, u32[]{:S(2)}) copy-start(f32[304,256]{1,0:T(8,128)} %get-tuple-element.31.xe_ref) | copy-start | bytes 933892
  25.7 3.3 %copy-start.2 = (f32[104,128]{1,0:T(8,128)S(1)}, f32[104,128]{1,0:T(8,128)}, u32[]{:S(2)}) copy-start(f32[104,128]{1,0:T(8,128)} %get-tuple-element.39.chem_ref) | copy-start | bytes 159748
  25.7 3.3 %copy-start.3 = (f32[2,32,1792]{2,1,0:T(8,128)S(1)}, f32[2,32,1792]{2,1,0:T(8,128)}, u32[]{:S(2)}) copy-start(f32[2,32,1792]{2,1,0:T(8,128)} %get-tuple-element.37.south_ref.own_south_ref) | copy-start | bytes 1376260
  25.7 3.3 %copy-start.4 = (f32[2,32,1792]{2,1,0:T(8,128)S(1)}, f32[2,32,1792]{2,1,0:T(8,128)}, u32[]{:S(2)}) copy-start(f32[2,32,1792]{2,1,0:T(8,128)} %get-tuple-element.38.north_ref.own_north_ref) | copy-start | bytes 1376260
  25.8 3.3 %copy-start.7 = (s32[8,32]{1,0:T(8,128)S(1)}, s32[8,32]{1,0:T(8,128)}, u32[]{:S(2)}) copy-start(s32[8,32]{1,0:T(8,128)} %cnt_ref.3) | copy-start | bytes 3076
  25.8 3.3 %copy-start.8 = (bf16[2,8,2,64,128]{4,3,2,1,0:T(8,128)(2,1)S(1)}, bf16[2,8,2,64,128]{4,3,2,1,0:T(8,128)(2,1)}, u32[]{:S(2)}) copy-start(bf16[2,8,2,64,128]{4,3,2,1,0:T(8,128)(2,1)} %get-tuple-element.42.table_ref) | copy-start | bytes 1572868
  25.8 3.3 %copy-start.9 = (f32[4,32,1792]{2,1,0:T(8,128)S(1)}, f32[4,32,1792]{2,1,0:T(8,128)}, u32[]{:S(2)}) copy-start(f32[4,32,1792]{2,1,0:T(8,128)} %get-tuple-element.40.mid_ref) | copy-start | bytes 2752516
  26.9 11.7 %collective-permute-start.2 = (f32[64,512]{1,0:T(8,128)S(1)}, f32[64,512]{1,0:T(8,128)S(1)}, u32[]{:S(2)}, u32[]{:S(2)}) collective-permute-start(f32[64,512]{1,0:T(8,128)S(1)} %get-tuple-element.34), channel_id=1, source_target_pairs={{0,1},{1,2},{2,3},{3,4},{4,5},{5,6},{6,7},{7,0},{8,9},{9,10},{10,1... | collective-permute-start | bytes 393224 | tf_op jit(solution)/shard_map/ppermute | solution.py:22
  28.2 10.4 %collective-permute-start.3 = (f32[72,512]{1,0:T(8,128)S(1)}, f32[72,512]{1,0:T(8,128)S(1)}, u32[]{:S(2)}, u32[]{:S(2)}) collective-permute-start(f32[72,512]{1,0:T(8,128)S(1)} %get-tuple-element.35), channel_id=1, source_target_pairs={{0,7},{1,0},{2,1},{3,2},{4,3},{5,4},{6,5},{7,6},{8,15},{9,8},{10,9... | collective-permute-start | bytes 442376 | tf_op jit(solution)/shard_map/ppermute | solution.py:22
  34.4 13.2 %collective-permute-start.8 = (f32[2,32,1536]{2,1,0:T(8,128)S(1)}, f32[2,32,1536]{2,1,0:T(8,128)S(1)}, u32[]{:S(2)}, u32[]{:S(2)}) collective-permute-start(f32[2,32,1536]{2,1,0:T(8,128)S(1)} %get-tuple-element.47.south_ref.own_south), channel_id=1, source_target_pairs={{0,7},{1,0},{2,1},{3,2},{4,3},{5,4},{6,5},{7,6},{8,15},{9,8},{10,9... | collective-permute-start | bytes 1179656 | tf_op jit(solution)/shard_map/ppermute | solution.py:22
  34.5 13.1 %collective-permute-start.7 = (f32[2,32,1536]{2,1,0:T(8,128)S(1)}, f32[2,32,1536]{2,1,0:T(8,128)S(1)}, u32[]{:S(2)}, u32[]{:S(2)}) collective-permute-start(f32[2,32,1536]{2,1,0:T(8,128)S(1)} %get-tuple-element.48.north_ref.own_north), channel_id=1, source_target_pairs={{0,1},{1,2},{2,3},{3,4},{4,5},{5,6},{6,7},{7,0},{8,9},{9,10},{10,1... | collective-permute-start | bytes 1179656 | tf_op jit(solution)/shard_map/ppermute | solution.py:22
  38.6 6.5 %copy-start = (f32[4,32,1792]{2,1,0:T(8,128)S(1)}, f32[4,32,1792]{2,1,0:T(8,128)}, u32[]{:S(2)}) copy-start(f32[4,32,1792]{2,1,0:T(8,128)} %get-tuple-element.46.done_ref) | copy-start | bytes 2752516
  43.0 5.2 %collective-permute-start.9 = (f32[2,32,512]{2,1,0:T(8,128)S(1)}, f32[2,32,512]{2,1,0:T(8,128)S(1)}, u32[]{:S(2)}, u32[]{:S(2)}) collective-permute-start(f32[2,32,512]{2,1,0:T(8,128)S(1)} %get-tuple-element.51.north_ref.own_north), channel_id=1, source_target_pairs={{0,1},{1,2},{2,3},{3,4},{4,5},{5,6},{6,7},{7,0},{8,9},{9,10},{10,1... | collective-permute-start | bytes 393224 | tf_op jit(solution)/shard_map/ppermute | solution.py:22
  44.3 7.1 %collective-permute-start.10 = (f32[2,32,512]{2,1,0:T(8,128)S(1)}, f32[2,32,512]{2,1,0:T(8,128)S(1)}, u32[]{:S(2)}, u32[]{:S(2)}) collective-permute-start(f32[2,32,512]{2,1,0:T(8,128)S(1)} %get-tuple-element.45.corner_ref.south_ref.own_south), channel_id=1, source_target_pairs={{0,7},{1,0},{2,1},{3,2},{4,3},{5,4},{6,5},{7,6},{8,15},{9,8},{10,9... | collective-permute-start | bytes 393224 | tf_op jit(solution)/shard_map/ppermute | solution.py:22

commit v6 on v5

--- a/solution.py
+++ b/solution.py
@@ -500,20 +500,17 @@
         + [north_ref[2 * species + 4 * (i - LAT_C) : 2 * species + 4 * (i - LAT_C) + 1] * valid_north]
         for i in (LAT_C, LAT_G)
     ]
-    for r, q in enumerate(lat_sweep(cells, *faces)):
-        done_ref[r] = q
-    for part in (0, rows // 2):
-        done = column_block(
-            [done_ref[part + i] for i in range(rows // 2)],
-            [side_ref[DAY, part + i : part + i + 1] for i in range(rows // 2)],
-            lambda i, j: cnt_ref[part + i, LEVELS * j],
-            rates,
-            chem_ref[2 * species : 3 * species],
-            chem_ref[3 * species + 0 : 3 * species + 1],
-            table_ref,
-        )
-        for i, row in enumerate(done):
-            done_ref[part + i] = jnp.concatenate(row, 1)
+    done = column_block(
+        lat_sweep(cells, *faces),
+        [side_ref[DAY, r : r + 1] for r in range(rows)],
+        lambda i, j: cnt_ref[i, LEVELS * j],
+        rates,
+        chem_ref[2 * species : 3 * species],
+        chem_ref[3 * species + 0 : 3 * species + 1],
+        table_ref,
+    )
+    for r, row in enumerate(done):
+        done_ref[r] = jnp.concatenate(row, 1)
     last = edge_ref.shape[2] // PIECE
 
     def tile(block):

time: 53.1 us -> 52.4 us (0.987)
  Pallas kernels: 29.7 us -> 29 us
    pallas_call x10, Pallas kernels: 29.7 us -> 29 us  [call(): pl.pallas_call(kernel, out_shape=[s if isinstance(s, jax.ShapeDtypeStruct...]
where the time goes in v6:
time: 52.4 us; the launch traced here: 52.1 us
  Pallas kernels  29 us (55%)
  starting transfers between devices  19.7 us (38%)
  waiting for transfers between devices  3.16 us (6%)
    pallas_call x10, Pallas kernels, call(): pl.pallas_call(kernel, out_shape=[s if isinstance(s, jax.ShapeDtypeStruct...  29 us
    ppermute x11, starting transfers between devices, ring(): lax.ppermute(value, axis, [(i, (i + steps) % count) for i in range(count)])  19.7 us
    ppermute x11, waiting for transfers between devices, ring(): lax.ppermute(value, axis, [(i, (i + steps) % count) for i in range(count)])  3.16 us
  transfers between devices with their start and end apart: 11, of which 1 were waited for; matrix products, arithmetic and copies ran while one was open for 0% of the time, Pallas kernels for 49%

profile of v6, /device:TPU:6, one launch (start us, length us, event | category | flops | bytes accessed | tf_op | source)
XLA Modules:
  0.0 52.1 jit_solution(9830119920649734329)
XLA Ops:
  0.0 2.1 %shard_map.100 = (f32[304,256]{1,0:T(8,128)}, f32[304,256]{1,0:T(8,128)}) custom-call(f32[32,8,2048]{2,1,0:T(8,128)} %x_ref.5, f32[2,8,32]{2,1,0:T(8,128)} %cour_in.3, s32[2,8,32]{2,1,0:T(8,128)} %sw_in.3, s32[8,32]{1,0:T(8,128)} %day_in.3, s32[8,32]{1,0:T(8,128)} %cnt_ref.3), custom_call_target="tpu_custom_call" | custom-call | flops 2000000000 | bytes 6000000 | tf_op jit(solution)/shard_map/pallas_call | solution.py:155
  2.1 0.1 collective-permute-start
  2.2 6.2 %collective-permute-start.1 = (f32[304,256]{1,0:T(8,128)}, f32[304,256]{1,0:T(8,128)S(1)}, u32[]{:S(2)}, u32[]{:S(2)}) collective-permute-start(f32[304,256]{1,0:T(8,128)} %get-tuple-element.30.west_ref.xw_ref), channel_id=1, source_target_pairs={{0,120},{8,0},{16,8},{24,16},{32,24},{40,32},{48,40},{56,48},{64,5... | collective-permute-start | bytes 933896 | tf_op jit(solution)/shard_map/ppermute | solution.py:22
  8.3 3.8 %shard_map.101 = (f32[2,32,1792]{2,1,0:T(8,128)}, f32[2,32,1792]{2,1,0:T(8,128)}, f32[6,8,2048]{2,1,0:T(8,128)}, f32[16,2048]{1,0:T(8,128)}, f32[104,128]{1,0:T(8,128)}) custom-call(f32[304,256]{1,0:T(8,128)} %get-tuple-element.30.west_ref.xw_ref, f32[32,8,2048]{2,1,0:T(8,128)} %x_ref.5, f32[2,8,32]{2,1,0:T(8,128)} %cour_in.3, s32[2,8,32]{2,1,0:T(8,128)} %sw_in.3, ...), custom_call_target="tpu_custom_call" | custom-call | flops 3000000000 | bytes 9000000 | tf_op jit(solution)/shard_map/pallas_call | solution.py:155
  12.1 0.9 %collective-permute-start.6 = (f32[16,2048]{1,0:T(8,128)}, f32[16,2048]{1,0:T(8,128)S(1)}, u32[]{:S(2)}, u32[]{:S(2)}) collective-permute-start(f32[16,2048]{1,0:T(8,128)} %get-tuple-element.41), channel_id=1, source_target_pairs={{0,7},{1,0},{2,1},{3,2},{4,3},{5,4},{6,5},{7,6},{8,15},{9,8},{10,9... | collective-permute-start | bytes 393224 | tf_op jit(solution)/shard_map/ppermute | solution.py:22
  13.0 0.5 %collective-permute-start.5 = (f32[2,32,1792]{2,1,0:T(8,128)}, f32[2,32,1792]{2,1,0:T(8,128)S(1)}, u32[]{:S(2)}, u32[]{:S(2)}) collective-permute-start(f32[2,32,1792]{2,1,0:T(8,128)} %get-tuple-element.37.south_ref.own_south_ref), channel_id=1, source_target_pairs={{0,7},{1,0},{2,1},{3,2},{4,3},{5,4},{6,5},{7,6},{8,15},{9,8},{10,9... | collective-permute-start | bytes 1376264 | tf_op jit(solution)/shard_map/ppermute | solution.py:22
  13.5 3.6 %collective-permute-start.4 = (f32[2,32,1792]{2,1,0:T(8,128)}, f32[2,32,1792]{2,1,0:T(8,128)S(1)}, u32[]{:S(2)}, u32[]{:S(2)}) collective-permute-start(f32[2,32,1792]{2,1,0:T(8,128)} %get-tuple-element.38.north_ref.own_north_ref), channel_id=1, source_target_pairs={{0,1},{1,2},{2,3},{3,4},{4,5},{5,6},{6,7},{7,0},{8,9},{9,10},{10,1... | collective-permute-start | bytes 1376264 | tf_op jit(solution)/shard_map/ppermute | solution.py:22
  17.2 8.6 %shard_map.103 = (f32[4,32,1792]{2,1,0:T(8,128)}, f32[4,32,1792]{2,1,0:T(8,128)}, bf16[2,8,2,64,128]{4,3,2,1,0:T(8,128)(2,1)}) custom-call(f32[32,8,2048]{2,1,0:T(8,128)} %x_ref.5, f32[2,32,1792]{2,1,0:T(8,128)} %get-tuple-element.37.south_ref.own_south_ref, f32[2,32,1792]{2,1,0:T(8,128)} %get-tuple-element.38.north_ref.own_north_ref, ...), custom_call_target="tpu_custom_call" | custom-call | flops 8999999488 | bytes 27000000 | tf_op jit(solution)/shard_map/pallas_call | solution.py:155
  25.8 0.0 copy-start.7
  25.8 0.0 copy-start.9
  25.8 1.1 %shard_map.102 = (f32[8,32,512]{2,1,0:T(8,128)S(1)}, f32[72,512]{1,0:T(8,128)S(1)}, f32[64,512]{1,0:T(8,128)S(1)}, f32[6,8,512]{2,1,0:T(8,128)S(1)}, s32[8,512]{1,0:T(8,128)S(1)}) custom-call(f32[304,256]{1,0:T(8,128)S(1)} %copy-done.5, f32[304,256]{1,0:T(8,128)S(1)} %copy-done.6, f32[304,256]{1,0:T(8,128)S(1)} %collective-permute-done.hw_ref, ...), custom_call_target="tpu_custom_call" | custom-call | flops 3000000000 | bytes 9000000 | tf_op jit(solution)/shard_map/pallas_call | solution.py:155
  26.9 1.3 %collective-permute-start.2 = (f32[64,512]{1,0:T(8,128)S(1)}, f32[64,512]{1,0:T(8,128)S(1)}, u32[]{:S(2)}, u32[]{:S(2)}) collective-permute-start(f32[64,512]{1,0:T(8,128)S(1)} %get-tuple-element.34), channel_id=1, source_target_pairs={{0,1},{1,2},{2,3},{3,4},{4,5},{5,6},{6,7},{7,0},{8,9},{9,10},{10,1... | collective-permute-start | bytes 393224 | tf_op jit(solution)/shard_map/ppermute | solution.py:22
  28.2 0.8 %collective-permute-start.3 = (f32[72,512]{1,0:T(8,128)S(1)}, f32[72,512]{1,0:T(8,128)S(1)}, u32[]{:S(2)}, u32[]{:S(2)}) collective-permute-start(f32[72,512]{1,0:T(8,128)S(1)} %get-tuple-element.35), channel_id=1, source_target_pairs={{0,7},{1,0},{2,1},{3,2},{4,3},{5,4},{6,5},{7,6},{8,15},{9,8},{10,9... | collective-permute-start | bytes 442376 | tf_op jit(solution)/shard_map/ppermute | solution.py:22
  29.1 5.3 %shard_map.104 = (f32[4,32,1792]{2,1,0:T(8,128)S(1)}, f32[2,32,1536]{2,1,0:T(8,128)S(1)}, f32[2,32,1536]{2,1,0:T(8,128)S(1)}) custom-call(f32[6,8,512]{2,1,0:T(8,128)S(1)} %get-tuple-element.36.side_ref, f32[4,32,1792]{2,1,0:T(8,128)S(1)} %copy-done.9, f32[2,32,1792]{2,1,0:T(8,128)S(1)} %copy-done.3, f32[2,32,1792]{2,1,0:T(8,128)S(1)} %copy-done.4, ...), custom_call_target="tpu_custom_call" | custom-call | flops 8999999488 | bytes 27000000 | tf_op jit(solution)/shard_map/pallas_call | solution.py:155
  34.4 0.1 collective-permute-start.8
  34.5 4.1 %collective-permute-start.7 = (f32[2,32,1536]{2,1,0:T(8,128)S(1)}, f32[2,32,1536]{2,1,0:T(8,128)S(1)}, u32[]{:S(2)}, u32[]{:S(2)}) collective-permute-start(f32[2,32,1536]{2,1,0:T(8,128)S(1)} %get-tuple-element.48.north_ref.own_north), channel_id=1, source_target_pairs={{0,1},{1,2},{2,3},{3,4},{4,5},{5,6},{6,7},{7,0},{8,9},{9,10},{10,1... | collective-permute-start | bytes 1179656 | tf_op jit(solution)/shard_map/ppermute | solution.py:22
  38.6 3.6 %shard_map.105 = (f32[8,32,512]{2,1,0:T(8,128)S(1)}, f32[2,32,512]{2,1,0:T(8,128)S(1)}, f32[2,32,512]{2,1,0:T(8,128)S(1)}) custom-call(f32[8,32,512]{2,1,0:T(8,128)S(1)} %get-tuple-element.33.mid_ref, f32[64,512]{1,0:T(8,128)S(1)} %collective-permute-done.2.south_ref, f32[72,512]{1,0:T(8,128)S(1)} %collective-permute-done.3.north_ref, ...), custom_call_target="tpu_custom_call" | custom-call | flops 5000000000 | bytes 15000000 | tf_op jit(solution)/shard_map/pallas_call | solution.py:155
  42.2 1.3 %collective-permute-start.9 = (f32[2,32,512]{2,1,0:T(8,128)S(1)}, f32[2,32,512]{2,1,0:T(8,128)S(1)}, u32[]{:S(2)}, u32[]{:S(2)}) collective-permute-start(f32[2,32,512]{2,1,0:T(8,128)S(1)} %get-tuple-element.51.north_ref.own_north), channel_id=1, source_target_pairs={{0,1},{1,2},{2,3},{3,4},{4,5},{5,6},{6,7},{7,0},{8,9},{9,10},{10,1... | collective-permute-start | bytes 393224 | tf_op jit(solution)/shard_map/ppermute | solution.py:22
  43.5 0.8 %collective-permute-start.10 = (f32[2,32,512]{2,1,0:T(8,128)S(1)}, f32[2,32,512]{2,1,0:T(8,128)S(1)}, u32[]{:S(2)}, u32[]{:S(2)}) collective-permute-start(f32[2,32,512]{2,1,0:T(8,128)S(1)} %get-tuple-element.45.corner_ref.south_ref.own_south), channel_id=1, source_target_pairs={{0,7},{1,0},{2,1},{3,2},{4,3},{5,4},{6,5},{7,6},{8,15},{9,8},{10,9... | collective-permute-start | bytes 393224 | tf_op jit(solution)/shard_map/ppermute | solution.py:22
  44.3 1.5 %shard_map.106 = (f32[4,32,1536]{2,1,0:T(8,128)S(1)}, f32[4,32,1536]{2,1,0:T(8,128)S(1)}) custom-call(f32[2,32,512]{2,1,0:T(8,128)S(1)} %get-tuple-element.45.corner_ref.south_ref.own_south, f32[4,32,1792]{2,1,0:T(8,128)S(1)} %copy-done, f32[2,32,1536]{2,1,0:T(8,128)S(1)} %get-tuple-element.47.south_ref.own_south, ...), custom_call_target="tpu_custom_call" | custom-call | flops 100000000 | bytes 300000 | tf_op jit(solution)/shard_map/pallas_call | solution.py:155
  45.9 1.0 %shard_map.107 = (f32[4,32,512]{2,1,0:T(8,128)S(1)}, f32[4,32,512]{2,1,0:T(8,128)S(1)}) custom-call(f32[4,32,1792]{2,1,0:T(8,128)S(1)} %copy-done, f32[8,32,512]{2,1,0:T(8,128)S(1)} %get-tuple-element.50.corner_ref, f32[2,32,512]{2,1,0:T(8,128)S(1)} %get-tuple-element.45.corner_ref.south_ref.own_south, ...), custom_call_target="tpu_custom_call" | custom-call | flops 100000000 | bytes 300000 | tf_op jit(solution)/shard_map/pallas_call | solution.py:155
  46.8 0.6 %shard_map.108.edge_a = f32[4,32,1536]{2,1,0:T(8,128)S(1)} custom-call(f32[4,32,512]{2,1,0:T(8,128)S(1)} %get-tuple-element.52.inner_c, f32[4,32,1536]{2,1,0:T(8,128)S(1)} %get-tuple-element.53.swept, f32[2,32,1536]{2,1,0:T(8,128)S(1)} %get-tuple-element.47.south_ref.own_south, f32[2,32,1536]{2,1,0:T(8,128)S(1)} %get-tuple-element.48.north_ref.own_north, ...), custom_call_target="tpu_custom_call" | custom-call | flops 500000000 | bytes 1500000 | tf_op jit(solution)/shard_map/pallas_call | solution.py:155
  47.4 3.1 %collective-permute-done.10.north = f32[2,32,512]{2,1,0:T(8,128)S(1)} collective-permute-done((f32[2,32,512]{2,1,0:T(8,128)S(1)}, f32[2,32,512]{2,1,0:T(8,128)S(1)}, u32[]{:S(2)}, u32[]{:S(2)}) %collective-permute-start.10) | collective-permute-done | bytes 131104 | tf_op jit(solution)/shard_map/ppermute | solution.py:22
  50.6 1.5 %shard_map.109 = f32[32,8,2048]{2,1,0:T(8,128)} custom-call(f32[4,32,1536]{2,1,0:T(8,128)S(1)} %get-tuple-element.49.inner_a, f32[4,32,512]{2,1,0:T(8,128)S(1)} %get-tuple-element.52.inner_c, f32[4,32,1536]{2,1,0:T(8,128)S(1)} %shard_map.108.edge_a, f32[4,32,512]{2,1,0:T(8,128)S(1)} %get-tuple-element.54.swept, ...), custom_call_target="tpu_custom_call" | custom-call | flops 3000000000 | bytes 9000000 | tf_op jit(solution)/shard_map/pallas_call | solution.py:155
  (28 shorter events, 0.1 us)
Async XLA Ops:
  2.1 23.7 %collective-permute-start = (f32[304,256]{1,0:T(8,128)}, f32[304,256]{1,0:T(8,128)S(1)}, u32[]{:S(2)}, u32[]{:S(2)}) collective-permute-start(f32[304,256]{1,0:T(8,128)} %get-tuple-element.31.xe_ref), channel_id=1, source_target_pairs={{0,8},{8,16},{16,24},{24,32},{32,40},{40,48},{48,56},{56,64},{64,7... | collective-permute-start | bytes 933896 | tf_op jit(solution)/shard_map/ppermute | solution.py:22
  2.2 23.6 %collective-permute-start.1 = (f32[304,256]{1,0:T(8,128)}, f32[304,256]{1,0:T(8,128)S(1)}, u32[]{:S(2)}, u32[]{:S(2)}) collective-permute-start(f32[304,256]{1,0:T(8,128)} %get-tuple-element.30.west_ref.xw_ref), channel_id=1, source_target_pairs={{0,120},{8,0},{16,8},{24,16},{32,24},{40,32},{48,40},{56,48},{64,5... | collective-permute-start | bytes 933896 | tf_op jit(solution)/shard_map/ppermute | solution.py:22
  12.1 16.9 %collective-permute-start.6 = (f32[16,2048]{1,0:T(8,128)}, f32[16,2048]{1,0:T(8,128)S(1)}, u32[]{:S(2)}, u32[]{:S(2)}) collective-permute-start(f32[16,2048]{1,0:T(8,128)} %get-tuple-element.41), channel_id=1, source_target_pairs={{0,7},{1,0},{2,1},{3,2},{4,3},{5,4},{6,5},{7,6},{8,15},{9,8},{10,9... | collective-permute-start | bytes 393224 | tf_op jit(solution)/shard_map/ppermute | solution.py:22
  13.0 16.0 %collective-permute-start.5 = (f32[2,32,1792]{2,1,0:T(8,128)}, f32[2,32,1792]{2,1,0:T(8,128)S(1)}, u32[]{:S(2)}, u32[]{:S(2)}) collective-permute-start(f32[2,32,1792]{2,1,0:T(8,128)} %get-tuple-element.37.south_ref.own_south_ref), channel_id=1, source_target_pairs={{0,7},{1,0},{2,1},{3,2},{4,3},{5,4},{6,5},{7,6},{8,15},{9,8},{10,9... | collective-permute-start | bytes 1376264 | tf_op jit(solution)/shard_map/ppermute | solution.py:22
  13.5 15.5 %collective-permute-start.4 = (f32[2,32,1792]{2,1,0:T(8,128)}, f32[2,32,1792]{2,1,0:T(8,128)S(1)}, u32[]{:S(2)}, u32[]{:S(2)}) collective-permute-start(f32[2,32,1792]{2,1,0:T(8,128)} %get-tuple-element.38.north_ref.own_north_ref), channel_id=1, source_target_pairs={{0,1},{1,2},{2,3},{3,4},{4,5},{5,6},{6,7},{7,0},{8,9},{9,10},{10,1... | collective-permute-start | bytes 1376264 | tf_op jit(solution)/shard_map/ppermute | solution.py:22
  17.2 8.7 %copy-start.1 = (f32[6,8,2048]{2,1,0:T(8,128)S(1)}, f32[6,8,2048]{2,1,0:T(8,128)}, u32[]{:S(2)}) copy-start(f32[6,8,2048]{2,1,0:T(8,128)} %get-tuple-element.32.coef_ref) | copy-start | bytes 1179652
  17.2 8.7 %copy-start.5 = (f32[304,256]{1,0:T(8,128)S(1)}, f32[304,256]{1,0:T(8,128)}, u32[]{:S(2)}) copy-start(f32[304,256]{1,0:T(8,128)} %get-tuple-element.30.west_ref.xw_ref) | copy-start | bytes 933892
  17.2 8.7 %copy-start.6 = (f32[304,256]{1,0:T(8,128)S(1)}, f32[304,256]{1,0:T(8,128)}, u32[]{:S(2)}) copy-start(f32[304,256]{1,0:T(8,128)} %get-tuple-element.31.xe_ref) | copy-start | bytes 933892
  25.7 3.3 %copy-start.2 = (f32[104,128]{1,0:T(8,128)S(1)}, f32[104,128]{1,0:T(8,128)}, u32[]{:S(2)}) copy-start(f32[104,128]{1,0:T(8,128)} %get-tuple-element.39.chem_ref) | copy-start | bytes 159748
  25.7 3.3 %copy-start.3 = (f32[2,32,1792]{2,1,0:T(8,128)S(1)}, f32[2,32,1792]{2,1,0:T(8,128)}, u32[]{:S(2)}) copy-start(f32[2,32,1792]{2,1,0:T(8,128)} %get-tuple-element.37.south_ref.own_south_ref) | copy-start | bytes 1376260
  25.7 3.3 %copy-start.4 = (f32[2,32,1792]{2,1,0:T(8,128)S(1)}, f32[2,32,1792]{2,1,0:T(8,128)}, u32[]{:S(2)}) copy-start(f32[2,32,1792]{2,1,0:T(8,128)} %get-tuple-element.38.north_ref.own_north_ref) | copy-start | bytes 1376260
  25.8 3.3 %copy-start.7 = (s32[8,32]{1,0:T(8,128)S(1)}, s32[8,32]{1,0:T(8,128)}, u32[]{:S(2)}) copy-start(s32[8,32]{1,0:T(8,128)} %cnt_ref.3) | copy-start | bytes 3076
  25.8 3.3 %copy-start.8 = (bf16[2,8,2,64,128]{4,3,2,1,0:T(8,128)(2,1)S(1)}, bf16[2,8,2,64,128]{4,3,2,1,0:T(8,128)(2,1)}, u32[]{:S(2)}) copy-start(bf16[2,8,2,64,128]{4,3,2,1,0:T(8,128)(2,1)} %get-tuple-element.42.table_ref) | copy-start | bytes 1572868
  25.8 3.3 %copy-start.9 = (f32[4,32,1792]{2,1,0:T(8,128)S(1)}, f32[4,32,1792]{2,1,0:T(8,128)}, u32[]{:S(2)}) copy-start(f32[4,32,1792]{2,1,0:T(8,128)} %get-tuple-element.40.mid_ref) | copy-start | bytes 2752516
  26.9 11.7 %collective-permute-start.2 = (f32[64,512]{1,0:T(8,128)S(1)}, f32[64,512]{1,0:T(8,128)S(1)}, u32[]{:S(2)}, u32[]{:S(2)}) collective-permute-start(f32[64,512]{1,0:T(8,128)S(1)} %get-tuple-element.34), channel_id=1, source_target_pairs={{0,1},{1,2},{2,3},{3,4},{4,5},{5,6},{6,7},{7,0},{8,9},{9,10},{10,1... | collective-permute-start | bytes 393224 | tf_op jit(solution)/shard_map/ppermute | solution.py:22
  28.2 10.4 %collective-permute-start.3 = (f32[72,512]{1,0:T(8,128)S(1)}, f32[72,512]{1,0:T(8,128)S(1)}, u32[]{:S(2)}, u32[]{:S(2)}) collective-permute-start(f32[72,512]{1,0:T(8,128)S(1)} %get-tuple-element.35), channel_id=1, source_target_pairs={{0,7},{1,0},{2,1},{3,2},{4,3},{5,4},{6,5},{7,6},{8,15},{9,8},{10,9... | collective-permute-start | bytes 442376 | tf_op jit(solution)/shard_map/ppermute | solution.py:22
  34.4 12.4 %collective-permute-start.8 = (f32[2,32,1536]{2,1,0:T(8,128)S(1)}, f32[2,32,1536]{2,1,0:T(8,128)S(1)}, u32[]{:S(2)}, u32[]{:S(2)}) collective-permute-start(f32[2,32,1536]{2,1,0:T(8,128)S(1)} %get-tuple-element.47.south_ref.own_south), channel_id=1, source_target_pairs={{0,7},{1,0},{2,1},{3,2},{4,3},{5,4},{6,5},{7,6},{8,15},{9,8},{10,9... | collective-permute-start | bytes 1179656 | tf_op jit(solution)/shard_map/ppermute | solution.py:22
  34.5 12.3 %collective-permute-start.7 = (f32[2,32,1536]{2,1,0:T(8,128)S(1)}, f32[2,32,1536]{2,1,0:T(8,128)S(1)}, u32[]{:S(2)}, u32[]{:S(2)}) collective-permute-start(f32[2,32,1536]{2,1,0:T(8,128)S(1)} %get-tuple-element.48.north_ref.own_north), channel_id=1, source_target_pairs={{0,1},{1,2},{2,3},{3,4},{4,5},{5,6},{6,7},{7,0},{8,9},{9,10},{10,1... | collective-permute-start | bytes 1179656 | tf_op jit(solution)/shard_map/ppermute | solution.py:22
  38.6 5.7 %copy-start = (f32[4,32,1792]{2,1,0:T(8,128)S(1)}, f32[4,32,1792]{2,1,0:T(8,128)}, u32[]{:S(2)}) copy-start(f32[4,32,1792]{2,1,0:T(8,128)} %get-tuple-element.46.done_ref) | copy-start | bytes 2752516
  42.2 5.2 %collective-permute-start.9 = (f32[2,32,512]{2,1,0:T(8,128)S(1)}, f32[2,32,512]{2,1,0:T(8,128)S(1)}, u32[]{:S(2)}, u32[]{:S(2)}) collective-permute-start(f32[2,32,512]{2,1,0:T(8,128)S(1)} %get-tuple-element.51.north_ref.own_north), channel_id=1, source_target_pairs={{0,1},{1,2},{2,3},{3,4},{4,5},{5,6},{6,7},{7,0},{8,9},{9,10},{10,1... | collective-permute-start | bytes 393224 | tf_op jit(solution)/shard_map/ppermute | solution.py:22
  43.5 7.1 %collective-permute-start.10 = (f32[2,32,512]{2,1,0:T(8,128)S(1)}, f32[2,32,512]{2,1,0:T(8,128)S(1)}, u32[]{:S(2)}, u32[]{:S(2)}) collective-permute-start(f32[2,32,512]{2,1,0:T(8,128)S(1)} %get-tuple-element.45.corner_ref.south_ref.own_south), channel_id=1, source_target_pairs={{0,7},{1,0},{2,1},{3,2},{4,3},{5,4},{6,5},{7,6},{8,15},{9,8},{10,9... | collective-permute-start | bytes 393224 | tf_op jit(solution)/shard_map/ppermute | solution.py:22
